TPU v7x, 32 devices: a whole 2x2x4 slice. The times are simulated.
32 devices in a mesh: wide: 8 (over y, x, core), narrow: 4 (over z).
Axes of the slice: x: 2, y: 2, z: 4, core: 2. Of those that a mesh axis runs over, the one named last changes fastest.
Arguments:
- user_input: bfloat16 [64, 64, 2048], P('wide'), may hold values from -6 to 6
- out_grad: bfloat16 [64, 64, 2048], P('wide'), may hold values from -6 to 6
- hist_len: int32 [64], P('wide'), may hold values from 1 to 64, 3072 in all
- hist_items: int32 [64, 64], P('wide'), may hold values from 0 to 1023, as said below
- item_row: int32 [1024], replicated, may hold values from 0 to 1023, as said below
- item_feat: bfloat16 [1024, 2048], P('wide'), may hold values from -6 to 6
- user_gain: bfloat16 [2048], replicated, may hold values from 0.5 to 1.5
- user_gate: bfloat16 [2048, 3072], P(None, 'narrow'), may hold values from -0.125 to 0.125
- user_up: bfloat16 [2048, 3072], P(None, 'narrow'), may hold values from -0.125 to 0.125
- user_down: bfloat16 [3072, 2048], P('narrow'), may hold values from -0.109375 to 0.109375
- item_gain: bfloat16 [2048], replicated, may hold values from 0.5 to 1.5
- item_gate: bfloat16 [2048, 3072], P(None, 'narrow'), may hold values from -0.125 to 0.125
- item_up: bfloat16 [2048, 3072], P(None, 'narrow'), may hold values from -0.125 to 0.125
- item_down: bfloat16 [3072, 2048], P('narrow'), may hold values from -0.109375 to 0.109375
Outputs:
- item_feat_grad: bfloat16 [1024, 2048], P('wide')
- user_gate_grad: float32 [2048, 3072], P('wide', 'narrow')
- user_up_grad: float32 [2048, 3072], P('wide', 'narrow')
- user_down_grad: float32 [3072, 2048], P('narrow', 'wide')
- item_gate_grad: float32 [2048, 3072], P('wide', 'narrow')
- item_up_grad: float32 [2048, 3072], P('wide', 'narrow')
- item_down_grad: float32 [3072, 2048], P('narrow', 'wide')
Inputs may be any that keep to these rules, and one draw needn't show every extreme that they name: `hist_items`: among the 512 positions of one index of wide, at most 128 name items whose table rows lie on any one index of wide; the rows of one index of wide, the same for all, are named by exactly 128 positions of every index of wide. A permutation: item id i lies in table row item_row[i], held by index item_row[i] // 128 of wide.
All inputs are finite; a program needn't handle non-finite values. No bound on the sum of `hist_len` on one device may be relied on, other than what follows from the above.
Results may differ from a plain program's by a relative error of at most 0.027.
Values may be sent and summed in bfloat16 or wider, within the bound.
No kernel may reach another device: no remote copies, remote signals or barrier semaphores. Data moves between devices by JAX's collectives and lax.ppermute only.
A program may use at most 128 MiB of HBM per device.

v0:
```python
import jax
import jax.numpy as jnp
from jax import lax
from jax.sharding import PartitionSpec as P


def layer_local(row_vals, gain_vec, w_gate, w_up, w_down, cot_bf):
    floats = row_vals.astype(jnp.float32)
    inv_rms = lax.rsqrt(jnp.mean(floats * floats, axis=1, keepdims=True) + 1e-05)
    unit_rows = floats * inv_rms
    gain_f = gain_vec.astype(jnp.float32)
    normed = (unit_rows * gain_f).astype(jnp.bfloat16)
    gate_act = jnp.dot(normed, w_gate, preferred_element_type=jnp.float32)
    up_act = jnp.dot(normed, w_up, preferred_element_type=jnp.float32)
    sig_gate = jax.nn.sigmoid(gate_act)
    hidden = (gate_act * sig_gate * up_act).astype(jnp.bfloat16)
    last_dims = (((1,), (1,)), ((), ()))
    first_dims = (((0,), (0,)), ((), ()))
    d_hidden = lax.dot_general(cot_bf, w_down, last_dims, preferred_element_type=jnp.float32)
    d_up = (d_hidden * gate_act * sig_gate).astype(jnp.bfloat16)
    d_gate = (d_hidden * up_act * sig_gate * (1.0 + gate_act * (1.0 - sig_gate))).astype(
        jnp.bfloat16
    )
    d_partial = lax.dot_general(
        d_gate, w_gate, last_dims, preferred_element_type=jnp.float32
    ) + lax.dot_general(d_up, w_up, last_dims, preferred_element_type=jnp.float32)
    terms = (
        lax.dot_general(normed, d_gate, first_dims, preferred_element_type=jnp.float32),
        lax.dot_general(normed, d_up, first_dims, preferred_element_type=jnp.float32),
        lax.dot_general(hidden, cot_bf, first_dims, preferred_element_type=jnp.float32),
    )
    return (unit_rows, inv_rms, gain_f, d_partial, terms)


def send_buffers(values, owner_dev, local_row, wide_count, slot_depth):
    row_count = owner_dev.shape[0]
    row_ids = jnp.arange(row_count, dtype=jnp.int32)
    same_owner = (owner_dev[:, None] == owner_dev[None, :]) & (row_ids[None, :] < row_ids[:, None])
    before = jnp.sum(same_owner.astype(jnp.int32), axis=1)
    slot_code = owner_dev * slot_depth + before
    slot_ids = jnp.arange(wide_count * slot_depth, dtype=jnp.int32)
    hits = (slot_ids[:, None] == slot_code[None, :]).astype(jnp.int32)
    filled = jnp.sum(hits, axis=1)
    source = jnp.sum(hits * row_ids[None, :], axis=1)
    taken = jnp.take(values, source, axis=0) * filled[:, None].astype(jnp.float32)
    buffer = taken.reshape(wide_count, slot_depth, values.shape[1])
    labels = (jnp.take(local_row, source, axis=0) * filled).reshape(wide_count, slot_depth)
    return (buffer, labels)


def merge_rows(got_rows, got_labels, item_dev):
    flat_rows = got_rows.reshape(-1, got_rows.shape[2])
    flat_labels = got_labels.reshape(-1)
    one_hot = (jnp.arange(item_dev, dtype=jnp.int32)[:, None] == flat_labels[None, :]).astype(
        jnp.float32
    )
    return jnp.dot(
        one_hot, flat_rows, precision=lax.Precision.HIGHEST, preferred_element_type=jnp.float32
    )


def body(
    user_input,
    out_grad,
    hist_len,
    hist_items,
    item_row,
    item_feat,
    user_gain,
    user_gate,
    user_up,
    user_down,
    item_gain,
    item_gate,
    item_up,
    item_down,
):
    wide_count = lax.axis_size("wide")
    user_count, hist_length, model_width = user_input.shape
    row_count = user_count * hist_length
    user_rows = user_input.reshape(row_count, model_width)
    valid_mask = (jnp.arange(hist_length, dtype=jnp.int32)[None, :] < hist_len[:, None]).astype(
        jnp.float32
    )
    masked = (
        (out_grad.astype(jnp.float32) * valid_mask[:, :, None])
        .astype(jnp.bfloat16)
        .reshape(row_count, model_width)
    )
    unit_rows, inv_rms, gain_f, d_partial, user_terms = layer_local(
        user_rows, user_gain, user_gate, user_up, user_down, masked
    )
    item_dev = item_feat.shape[0]
    targets = item_row[hist_items.reshape(row_count)]
    owner_dev = targets // item_dev
    local_row = targets % item_dev
    slot_depth = 2 * row_count // wide_count
    d_normed = lax.psum(d_partial.astype(jnp.bfloat16), "narrow").astype(jnp.float32)
    scaled = gain_f * d_normed
    row_mean = jnp.mean(scaled * unit_rows, axis=1, keepdims=True)
    occ_grad = masked.astype(jnp.float32) + inv_rms * (scaled - unit_rows * row_mean)
    buffer, labels = send_buffers(occ_grad, owner_dev, local_row, wide_count, slot_depth)
    got_rows, got_labels = (
        lax.all_to_all(
            buffer.astype(jnp.bfloat16), "wide", split_axis=0, concat_axis=0, tiled=True
        ).astype(buffer.dtype),
        lax.all_to_all(labels, "wide", split_axis=0, concat_axis=0, tiled=True),
    )
    item_in = merge_rows(got_rows, got_labels, item_dev)
    item_unit, item_inv, item_gain_f, item_partial, item_terms = layer_local(
        item_feat, item_gain, item_gate, item_up, item_down, item_in.astype(jnp.bfloat16)
    )
    item_normed = lax.psum(item_partial.astype(jnp.bfloat16), "narrow").astype(jnp.float32)
    item_scaled = item_gain_f * item_normed
    item_mean = jnp.mean(item_scaled * item_unit, axis=1, keepdims=True)
    feat_grad = (item_in + item_inv * (item_scaled - item_unit * item_mean)).astype(jnp.bfloat16)
    summed = (
        lax.psum_scatter(
            user_terms[0].astype(jnp.bfloat16), "wide", scatter_dimension=0, tiled=True
        ).astype(jnp.float32),
        lax.psum_scatter(
            user_terms[1].astype(jnp.bfloat16), "wide", scatter_dimension=0, tiled=True
        ).astype(jnp.float32),
        lax.psum_scatter(
            user_terms[2].astype(jnp.bfloat16), "wide", scatter_dimension=1, tiled=True
        ).astype(jnp.float32),
        lax.psum_scatter(
            item_terms[0].astype(jnp.bfloat16), "wide", scatter_dimension=0, tiled=True
        ).astype(jnp.float32),
        lax.psum_scatter(
            item_terms[1].astype(jnp.bfloat16), "wide", scatter_dimension=0, tiled=True
        ).astype(jnp.float32),
        lax.psum_scatter(
            item_terms[2].astype(jnp.bfloat16), "wide", scatter_dimension=1, tiled=True
        ).astype(jnp.float32),
    )
    return (
        feat_grad,
        summed[0] / wide_count,
        summed[1] / wide_count,
        summed[2] / wide_count,
        summed[3] / wide_count,
        summed[4] / wide_count,
        summed[5] / wide_count,
    )


def solution(mesh):
    placed = (
        P("wide", None, None),
        P("wide", None, None),
        P("wide"),
        P("wide", None),
        P(),
        P("wide", None),
        P(),
        P(None, "narrow"),
        P(None, "narrow"),
        P("narrow", None),
        P(),
        P(None, "narrow"),
        P(None, "narrow"),
        P("narrow", None),
    )
    return jax.shard_map(
        body,
        mesh=mesh,
        in_specs=placed,
        out_specs=(
            P("wide", None),
            P("wide", "narrow"),
            P("wide", "narrow"),
            P("narrow", "wide"),
            P("wide", "narrow"),
            P("wide", "narrow"),
            P("narrow", "wide"),
        ),
        check_vma=False,
    )
```

profile of v0, /device:TPU:0, one launch (start us, length us, event | category | flops | bytes accessed | tf_op | source)
XLA Modules:
  0.0 370.6 jit_solution(9729802765544622086)
XLA Ops:
  8.1 0.9 fusion.20
  8.9 2.1 multiply_reduce_fusion.1
  11.0 0.1 rsqrt.20
  11.1 0.7 convert_element_type.141
  11.8 2.1 multiply_convert_fusion.1
  14.0 1.8 fusion.31
  15.8 0.8 copy-done.24
  16.6 1.8 fusion.30
  18.4 0.4 copy-done.13
  18.8 0.4 multiply_convert_fusion.2
  19.2 2.8 copy-done.23
  22.0 2.2 multiply_convert_fusion.4
  24.3 1.8 fusion.32
  26.1 3.2 add_convert_fusion
  29.4 5.4 %convolution_convert_fusion = bf16[768,2048]{1,0:T(8,128)(2,1)} fusion(bf16[512,2048]{1,0:T(8,128)(2,1)S(1)} %bitcast.52, f32[512,768]{1,0:T(8,128)} %copy-done.31, f32[512,768]{1,0:T(8,128)} %copy-done.30), kind=kOutput, calls=%fused_computation.12 | convolution fusion | flops 1614544896 | bytes 8388608 | tf_op jit(solution)/shard_map/dot_general | solution.py:30
  34.8 0.2 reduce-scatter.9.cloned.1.call-start
  35.1 1.3 copy-done.15
  36.4 0.2 copy-done.27
  36.6 3.5 convolution_convert_fusion.1
  40.1 0.7 copy-done.22
  40.8 0.1 reshape.252
  40.9 2.3 gather_fusion
  43.2 0.2 convert_reduce_fusion.1
  43.5 0.6 convert_reduce_fusion
  44.1 6.9 %gather_fusion.1 = s32[1024]{0:T(1024)S(1)} fusion(s32[512]{0:T(512)S(1)} %get-tuple-element.13, s32[1024]{0:T(1024)S(1)} %broadcast_clamp_fusion), kind=kCustom, calls=%fused_computation.1 | custom fusion | bytes 12288 | tf_op jit(solution)/shard_map/jit(_take)/gather | solution.py:47
  51.0 0.6 fusion.19
  51.6 5.3 %all-to-all-start = ((s32[8,1,128]{2,1,0:T(1,128)}), s32[8,1,128]{2,1,0:T(1,128)S(1)}, u32[]{:S(2)}, u32[]{:S(2)}) async-start(s32[8,1,128]{2,1,0:T(1,128)} %fusion.19), calls=%async_computation | async-start | bytes 8192 | tf_op jit(solution)/shard_map/all_to_all | solution.py:107
  57.0 61.8 %all-reduce.3.cloned.1.call-done = bf16[512,2048]{1,0:T(8,128)(2,1)} async-done(((bf16[512,2048]{1,0:T(8,128)(2,1)}), bf16[512,2048]{1,0:T(8,128)(2,1)}) %all-reduce.3.cloned.1.call-update) | async-done | bytes 2097168 | tf_op jit(solution)/shard_map/psum | solution.py:98
  118.7 2.7 multiply_reduce_fusion
  121.4 0.2 copy-done.12
  121.7 3.5 multiply_add_fusion
  125.2 11.4 %gather_fusion.2 = f32[1024,2048]{1,0:T(8,128)} fusion(f32[512,2048]{1,0:T(8,128)} %multiply_add_fusion, s32[1024]{0:T(1024)S(1)} %broadcast_clamp_fusion), kind=kCustom, calls=%fused_computation.2 | custom fusion | bytes 16781312 | tf_op jit(solution)/shard_map/jit(_take)/gather | solution.py:45
  136.5 5.3 %multiply_convert_fusion = bf16[8,128,2048]{2,1,0:T(8,128)(2,1)} fusion(f32[8,128,2048]{2,1,0:T(8,128)} %bitcast.50, f32[8,128]{1,0:T(8,128)S(1)} %convert_bitcast_fusion, pred[8,128]{1,0:T(8,128)(4,1)S(1)} %compare_and_fusion), kind=kLoop, calls=%fused_computation.3 | loop fusion | flops 6291456 | bytes 12588032 | tf_op jit(solution)/shard_map/convert_element_type | solution.py:105
  141.8 4.8 %all-to-all-start.1 = ((bf16[8,128,2048]{2,1,0:T(8,128)(2,1)}), bf16[8,128,2048]{2,1,0:T(8,128)(2,1)}, u32[]{:S(2)}, u32[]{:S(2)}) async-start(bf16[8,128,2048]{2,1,0:T(8,128)(2,1)} %multiply_convert_fusion), calls=%async_computation.1 | async-start | bytes 8388608 | tf_op jit(solution)/shard_map/all_to_all | solution.py:104
  146.7 3.5 convolution_convert_fusion.2
  150.3 0.3 all-reduce.5.cloned.1.call-start
  150.6 0.4 copy-done.21
  151.0 0.4 copy-done.4
  151.3 0.2 fusion.10
  151.5 2.8 fusion.26
  154.3 0.6 fusion.28
  155.0 49.3 %all-to-all-done.1 = bf16[8,128,2048]{2,1,0:T(8,128)(2,1)} async-done(((bf16[8,128,2048]{2,1,0:T(8,128)(2,1)}), bf16[8,128,2048]{2,1,0:T(8,128)(2,1)}, u32[]{:S(2)}, u32[]{:S(2)}) %all-to-all-start.1) | async-done | bytes 4194336 | tf_op jit(solution)/shard_map/all_to_all | solution.py:104
  204.2 3.2 fusion.13
  207.4 0.1 copy-done.25
  207.6 1.2 multiply_convert_fusion.8
  208.9 1.1 copy-done.7
  210.0 1.1 fusion.33
  211.2 1.9 fusion
  213.2 0.0 reduce-scatter.17.cloned.1.call-start
  213.2 2.7 convolution_convert_fusion.3
  216.0 2.8 convolution_convert_fusion.4
  219.0 2.7 convolution_convert_fusion.5
  221.7 1.9 convert_multiply_fusion.7
  223.7 2.0 convert_multiply_fusion.8
  225.6 2.0 convert_multiply_fusion.9
  227.6 20.9 %all-reduce.5.cloned.1.call-done = bf16[128,2048]{1,0:T(8,128)(2,1)} async-done(((bf16[128,2048]{1,0:T(8,128)(2,1)}), bf16[128,2048]{1,0:T(8,128)(2,1)}) %all-reduce.5.cloned.1.call-update) | async-done | bytes 524304 | tf_op jit(solution)/shard_map/psum | solution.py:113
  248.5 1.7 fusion.5
  250.2 2.7 fusion.9
  252.9 8.9 %reduce-scatter.17.cloned.1.call-done = bf16[768,256]{1,0:T(8,128)(2,1)} async-done(((bf16[768,2048]{1,0:T(8,128)(2,1)}), bf16[768,256]{1,0:T(8,128)(2,1)}) %reduce-scatter.17.cloned.1.call-update) | async-done | bytes 393232 | tf_op jit(solution)/shard_map/reduce_scatter | solution.py:133
  261.8 1.9 convert_multiply_fusion.4
  263.7 48.0 %reduce-scatter.15.cloned.1.call-done = bf16[256,768]{1,0:T(8,128)(2,1)} async-done(((bf16[2048,768]{1,0:T(8,128)(2,1)}), bf16[256,768]{1,0:T(8,128)(2,1)}) %reduce-scatter.15.cloned.1.call-update) | async-done | bytes 393232 | tf_op jit(solution)/shard_map/reduce_scatter | solution.py:130
  311.7 1.9 convert_multiply_fusion.5
  313.6 47.6 %reduce-scatter.13.cloned.1.call-done = bf16[256,768]{1,0:T(8,128)(2,1)} async-done(((bf16[2048,768]{1,0:T(8,128)(2,1)}), bf16[256,768]{1,0:T(8,128)(2,1)}) %reduce-scatter.13.cloned.1.call-update) | async-done | bytes 393232 | tf_op jit(solution)/shard_map/reduce_scatter | solution.py:127
  361.2 1.9 convert_multiply_fusion.6
  (83 shorter events, 0.6 us)
Async XLA Ops:
  8.0 6.0 %copy-start = (bf16[2048,768]{1,0:T(8,128)(2,1)S(1)}, bf16[2048,768]{1,0:T(8,128)(2,1)}, u32[]{:S(2)}) copy-start(bf16[2048,768]{1,0:T(8,128)(2,1)} %param.21) | copy-start | bytes 9437188
  8.0 110.7 %all-reduce.3.cloned.1.call-start = ((), (), s32[]{:S(2)}) async-start(), calls=%async_computation.8 | async-start | bytes 4194304 | tf_op jit(solution)/shard_map/psum | solution.py:98
  14.0 1.8 copy-start.14
  14.0 2.6 copy-start.24
  16.6 2.6 copy-start.30
  16.6 2.2 copy-start.13
  18.8 5.4 %copy-start.31 = (f32[512,768]{1,0:T(8,128)}, f32[512,768]{1,0:T(8,128)S(1)}, u32[]{:S(2)}) copy-start(f32[512,768]{1,0:T(8,128)S(1)} %fusion.30) | copy-start | bytes 4718596
  18.8 3.2 copy-start.23
  19.2 5.0 %copy-start.9 = (bf16[8,64,2048]{2,1,0:T(8,128)(2,1)}, bf16[8,64,2048]{2,1,0:T(8,128)(2,1)S(1)}, u32[]{:S(2)}) copy-start(bf16[8,64,2048]{2,1,0:T(8,128)(2,1)S(1)} %multiply_convert_fusion.2) | copy-start | bytes 6291460
  24.2 1.9 copy-start.28
  24.3 1.9 copy-start.26
  26.1 3.3 copy-start.10
  29.3 192.4 %reduce-scatter.11.cloned.1.call-start = ((), (), s32[]{:S(2)}) async-start(), calls=%async_computation.12 | async-start | bytes 3538944 | tf_op jit(solution)/shard_map/reduce_scatter | solution.py:124
  34.8 1.6 copy-start.15
  34.8 1.8 copy-start.27
  34.8 188.9 %reduce-scatter.9.cloned.1.call-start = ((), (), s32[]{:S(2)}) async-start(), calls=%async_computation.11 | async-start | bytes 3538944 | tf_op jit(solution)/shard_map/reduce_scatter | solution.py:121
  40.1 0.7 copy-start.22
  40.1 0.8 copy-start.2
  40.9 77.9 %copy-start.3 = (bf16[8,64,2048]{2,1,0:T(8,128)(2,1)S(1)}, bf16[8,64,2048]{2,1,0:T(8,128)(2,1)}, u32[]{:S(2)}) copy-start(bf16[8,64,2048]{2,1,0:T(8,128)(2,1)} %param.14) | copy-start | bytes 6291460
  51.6 90.2 %all-to-all-start = ((s32[8,1,128]{2,1,0:T(1,128)}), s32[8,1,128]{2,1,0:T(1,128)S(1)}, u32[]{:S(2)}, u32[]{:S(2)}) async-start(s32[8,1,128]{2,1,0:T(1,128)} %fusion.19), calls=%async_computation | async-start | bytes 8192 | tf_op jit(solution)/shard_map/all_to_all | solution.py:107
  118.7 2.7 copy-start.11
  118.7 2.9 copy-start.12
  141.8 4.9 %copy-start.16 = (bf16[512,2048]{1,0:T(8,128)(2,1)S(1)}, bf16[512,2048]{1,0:T(8,128)(2,1)}, u32[]{:S(2)}) copy-start(bf16[512,2048]{1,0:T(8,128)(2,1)} %copy-done.14) | copy-start | bytes 6291460
  141.8 4.9 %copy-start.29 = (bf16[512,768]{1,0:T(8,128)(2,1)S(1)}, bf16[512,768]{1,0:T(8,128)(2,1)}, u32[]{:S(2)}) copy-start(bf16[512,768]{1,0:T(8,128)(2,1)} %copy-done.28) | copy-start | bytes 2359300
  141.8 62.4 %all-to-all-start.1 = ((bf16[8,128,2048]{2,1,0:T(8,128)(2,1)}), bf16[8,128,2048]{2,1,0:T(8,128)(2,1)}, u32[]{:S(2)}, u32[]{:S(2)}) async-start(bf16[8,128,2048]{2,1,0:T(8,128)(2,1)} %multiply_convert_fusion), calls=%async_computation.1 | async-start | bytes 8388608 | tf_op jit(solution)/shard_map/all_to_all | solution.py:104
  146.7 79.0 %reduce-scatter.7.cloned.1.call-start = ((), (), s32[]{:S(2)}) async-start(), calls=%async_computation.10 | async-start | bytes 3538944 | tf_op jit(solution)/shard_map/reduce_scatter | solution.py:118
  150.3 0.7 copy-start.21
  150.3 1.1 copy-start.4
  150.3 98.2 %all-reduce.5.cloned.1.call-start = ((), (), s32[]{:S(2)}) async-start(), calls=%async_computation.9 | async-start | bytes 1048576 | tf_op jit(solution)/shard_map/psum | solution.py:113
  150.9 3.4 copy-start.5
  204.2 3.4 copy-start.25
  207.6 5.6 %copy-start.8 = (f32[128,2048]{1,0:T(8,128)}, f32[128,2048]{1,0:T(8,128)S(1)}, u32[]{:S(2)}) copy-start(f32[128,2048]{1,0:T(8,128)S(1)} %fusion.13) | copy-start | bytes 3145732
  207.6 2.4 copy-start.7
  208.8 2.3 copy-start.17
  208.9 2.3 copy-start.19
  208.9 2.3 copy-start.6
  213.2 2.9 copy-start.20
  213.2 48.7 %reduce-scatter.17.cloned.1.call-start = ((), (), s32[]{:S(2)}) async-start(), calls=%async_computation.15 | async-start | bytes 3538944 | tf_op jit(solution)/shard_map/reduce_scatter | solution.py:133
  216.0 3.0 copy-start.18
  216.0 95.7 %reduce-scatter.15.cloned.1.call-start = ((), (), s32[]{:S(2)}) async-start(), calls=%async_computation.14 | async-start | bytes 3538944 | tf_op jit(solution)/shard_map/reduce_scatter | solution.py:130
  218.9 142.4 %reduce-scatter.13.cloned.1.call-start = ((), (), s32[]{:S(2)}) async-start(), calls=%async_computation.13 | async-start | bytes 3538944 | tf_op jit(solution)/shard_map/reduce_scatter | solution.py:127
  248.5 114.7 %copy-start.1 = (bf16[2048,768]{1,0:T(8,128)(2,1)S(1)}, bf16[2048,768]{1,0:T(8,128)(2,1)}, u32[]{:S(2)}) copy-start(bf16[2048,768]{1,0:T(8,128)(2,1)} %param.21) | copy-start | bytes 9437188
Sparse Core Ops, SparseCore 0:
  29.5 89.2 all-reduce.2
  213.3 35.1 all-reduce.4
Sparse Core Ops, SparseCore 1:
  34.9 48.8 reduce-scatter.10
  87.0 46.0 reduce-scatter.8
  150.9 61.4 reduce-scatter.6
  217.3 44.4 reduce-scatter.16
  265.6 46.0 reduce-scatter.14
  315.1 46.1 reduce-scatter.12
where the time goes:
time: 372 us; the launch traced here: 371 us
  waiting for transfers between devices  237 us (64%)
  matrix products  42.5 us (11%)
  other arithmetic  35.5 us (10%)
  local copies, waits for them, and re-layouts  29.2 us (8%)
  between operations  16 us (4%)
  starting transfers between devices  10.9 us (3%)
    psum x1, waiting for transfers between devices, body(): lax.psum(d_partial.astype(jnp.bfloat16), 'narrow').astype(jnp.float32)  61.8 us
    all_to_all x1, waiting for transfers between devices, body(): lax.all_to_all(buffer.astype(jnp.bfloat16), 'wide', split_axis=0, concat_...  49.3 us
    reduce_scatter x1, waiting for transfers between devices, body(): lax.psum_scatter(item_terms[1].astype(jnp.bfloat16), 'wide', scatter_dime...  48 us
    reduce_scatter x1, waiting for transfers between devices, body(): lax.psum_scatter(item_terms[0].astype(jnp.bfloat16), 'wide', scatter_dime...  47.6 us
    psum x1, waiting for transfers between devices, body(): lax.psum(item_partial.astype(jnp.bfloat16), 'narrow').astype(jnp.float32)  20.9 us
    gather x1, local copies, waits for them, and re-layouts, send_buffers(): jnp.take(values, source, axis=0) * filled[:, None].astype(jnp.float32)  11.4 us
    reduce_scatter x1, waiting for transfers between devices, body(): lax.psum_scatter(item_terms[2].astype(jnp.bfloat16), 'wide', scatter_dime...  8.93 us
    unnamed x64, local copies, waits for them, and re-layouts  8.54 us
  transfers between devices with their start and end apart: 10, of which 6 were waited for; matrix products, arithmetic and copies ran while one was open for 21% of the time, Pallas kernels for 0%

commit v1 on v0

v1 whole, which is shorter than its diff:
```python
import functools

import jax
import jax.numpy as jnp
from jax import lax
from jax.experimental import pallas as pl
from jax.experimental.pallas import tpu as pltpu
from jax.sharding import PartitionSpec as P

F32 = jnp.float32
BF16 = jnp.bfloat16
LAST = (((1,), (1,)), ((), ()))
FIRST = (((0,), (0,)), ((), ()))
PLAIN = (((1,), (0,)), ((), ()))
TILE = 256
VMEM_BYTES = 58 * 1024 * 1024


def mm(a, b, dims=PLAIN):
    return lax.dot_general(a, b, dims, preferred_element_type=F32)


def params():
    return pltpu.CompilerParams(vmem_limit_bytes=VMEM_BYTES)


def cost(flops, touched):
    return pl.CostEstimate(flops=int(flops), bytes_accessed=int(touched), transcendentals=0)


def whole_spec(shape):
    return pl.BlockSpec(shape, lambda *_: (0,) * len(shape))


def swap(value, bit):
    count = lax.axis_size("wide")
    return lax.ppermute(value, "wide", [(i, i ^ bit) for i in range(count)])


def user_kernel(
    steps, share, x_ref, og_ref, valid_ref, gain_ref, gate_ref, up_ref, down_ref, target_ref,
    sent_ids_ref, kept_ids_ref,
    normed_out, masked_out, hidden_ref, d_gate_ref, d_up_ref, sent_ref, kept_ref,
    normed, masked, inv_ref, total, sems,
):
    step = pl.program_id(0)

    @pl.when(step == 0)
    def _():
        rows = x_ref[...].astype(F32)
        inv = lax.rsqrt(jnp.mean(rows * rows, axis=1, keepdims=True) + 1e-05)
        inv_ref[...] = inv
        normed[...] = (rows * inv * gain_ref[...].astype(F32)).astype(BF16)
        masked[...] = (og_ref[...].astype(F32) * valid_ref[...]).astype(BF16)
        pltpu.make_async_copy(normed, normed_out, sems.at[0]).start()
        pltpu.make_async_copy(masked, masked_out, sems.at[1]).start()

    gate_act = mm(normed[...], gate_ref[...])
    up_act = mm(normed[...], up_ref[...])
    d_hidden = mm(masked[...], down_ref[...], LAST)
    sig = 1.0 / (1.0 + jnp.exp(-gate_act))
    silu = gate_act * sig
    hidden_ref[...] = (silu * up_act).astype(BF16)
    d_up = (d_hidden * silu).astype(BF16)
    d_gate = (d_hidden * up_act * sig * (1.0 + gate_act * (1.0 - sig))).astype(BF16)
    d_up_ref[...] = d_up
    d_gate_ref[...] = d_gate
    part = mm(d_gate, gate_ref[...], LAST) + mm(d_up, up_ref[...], LAST)

    @pl.when(step == 0)
    def _():
        total[...] = part

    @pl.when(step > 0)
    def _():
        total[...] += part

    @pl.when(step == steps - 1)
    def _():
        inv = inv_ref[...]
        scaled = total[...] * gain_ref[...].astype(F32)
        unit = x_ref[...].astype(F32) * inv
        mean = jnp.mean(scaled * unit, axis=1, keepdims=True)
        occ = (masked[...].astype(F32) * share + inv * (scaled - unit * mean)).astype(BF16)
        targets = target_ref[...]
        sent_ref[...] = mm((sent_ids_ref[...] == targets).astype(BF16), occ).astype(BF16)
        kept_ref[...] = mm((kept_ids_ref[...] == targets).astype(BF16), occ).astype(BF16)
        pltpu.make_async_copy(normed, normed_out, sems.at[0]).wait()
        pltpu.make_async_copy(masked, masked_out, sems.at[1]).wait()


def user_layer(x, og, valid, gain, w_gate, w_up, w_down, targets, sent_ids, kept_ids, share):
    rows, width = x.shape
    hid = w_gate.shape[1]
    tile = min(TILE, hid)
    steps = hid // tile
    half = sent_ids.shape[0]
    columns = pl.BlockSpec((rows, tile), lambda s: (0, s))
    weights = pl.BlockSpec((width, tile), lambda s: (0, s))
    wide = jax.ShapeDtypeStruct((rows, width), BF16)
    narrow = jax.ShapeDtypeStruct((rows, hid), BF16)
    summed = jax.ShapeDtypeStruct((half, width), BF16)
    return pl.pallas_call(
        functools.partial(user_kernel, steps, share),
        grid=(steps,),
        in_specs=[
            whole_spec((rows, width)),
            whole_spec((rows, width)),
            whole_spec((rows, 1)),
            whole_spec((1, width)),
            weights,
            weights,
            pl.BlockSpec((tile, width), lambda s: (s, 0)),
            whole_spec((1, rows)),
            whole_spec((half, 1)),
            whole_spec((half, 1)),
        ],
        out_specs=[pl.BlockSpec(memory_space=pl.ANY)] * 2
        + [columns] * 3
        + [whole_spec((half, width))] * 2,
        out_shape=[wide, wide, narrow, narrow, narrow, summed, summed],
        scratch_shapes=[
            pltpu.VMEM((rows, width), BF16),
            pltpu.VMEM((rows, width), BF16),
            pltpu.VMEM((rows, 1), F32),
            pltpu.VMEM((rows, width), F32),
            pltpu.SemaphoreType.DMA((2,)),
        ],
        compiler_params=params(),
        cost_estimate=cost(10 * rows * width * hid, 20e6),
        name="user_layer",
    )(x, og, valid, gain, w_gate, w_up, w_down, targets, sent_ids, kept_ids)


def grad_rows(normed_ref, masked_ref, d_gate_ref, d_up_ref, hidden_ref):
    left, right = normed_ref[...], masked_ref[...]
    return (
        mm(left, d_gate_ref[...], FIRST),
        mm(left, d_up_ref[...], FIRST),
        mm(right, hidden_ref[...], FIRST),
    )


def sent_kernel(table_ref, normed_ref, masked_ref, d_gate_ref, d_up_ref, hidden_ref, out_ref):
    hid = hidden_ref.shape[1]
    found = grad_rows(normed_ref, masked_ref, d_gate_ref, d_up_ref, hidden_ref)
    for k, piece in enumerate(found):
        out_ref[0, :, k * hid : (k + 1) * hid] = piece.astype(BF16)


def kept_kernel(
    table_ref, normed_ref, masked_ref, d_gate_ref, d_up_ref, hidden_ref, got_ref,
    sent_a, kept_a, sent_b, kept_b,
):
    step = pl.program_id(0)
    hid = hidden_ref.shape[1]
    cut = got_ref.shape[1] // 2
    found = grad_rows(normed_ref, masked_ref, d_gate_ref, d_up_ref, hidden_ref)
    for first, sent, kept, flag in ((0, sent_a, kept_a, 3), (cut, sent_b, kept_b, 6)):
        for k, piece in enumerate(found):
            at = slice(k * hid, (k + 1) * hid)
            value = piece[first : first + cut] + got_ref[0, first : first + cut, at].astype(F32)
            value = value.astype(BF16)

            @pl.when(table_ref[flag, step] == 1)
            def _(sent=sent, value=value, at=at):
                sent[0, :, at] = value

            @pl.when(table_ref[flag, step] == 0)
            def _(kept=kept, value=value, at=at):
                kept[0, :, at] = value


def lhs_specs(rows, block, hid):
    if block % 128:
        column = pl.BlockSpec((None, rows, block), lambda s, t: (s, 0, 0))
    else:
        column = pl.BlockSpec((rows, block), lambda s, t: (0, t[0, s]))
    return [column, column] + [whole_spec((rows, hid))] * 3


def lhs_arrays(table, normed, masked, block):
    if block % 128 == 0:
        return normed, masked
    return tuple(
        jnp.take(jnp.swapaxes(a.reshape(a.shape[0], -1, block), 0, 1), table[0], axis=0)
        for a in (normed, masked)
    )


def sent_grads(table, normed, masked, d_gate, d_up, hidden, block):
    rows, hid = hidden.shape
    count = table.shape[1]
    return pl.pallas_call(
        sent_kernel,
        grid_spec=pltpu.PrefetchScalarGridSpec(
            num_scalar_prefetch=1,
            grid=(count,),
            in_specs=lhs_specs(rows, block, hid),
            out_specs=pl.BlockSpec((1, block, 3 * hid), lambda s, t: (s, 0, 0)),
        ),
        out_shape=jax.ShapeDtypeStruct((count, block, 3 * hid), BF16),
        compiler_params=params(),
        cost_estimate=cost(6 * rows * block * count * hid, 10e6),
        name="sent_grads",
    )(table, *lhs_arrays(table, normed, masked, block), d_gate, d_up, hidden)


def kept_grads(table, normed, masked, d_gate, d_up, hidden, got, block):
    rows, hid = hidden.shape
    count = table.shape[1]
    piece = jax.ShapeDtypeStruct((count // 2, block // 2, 3 * hid), BF16)

    def out(row):
        return pl.BlockSpec((1, block // 2, 3 * hid), lambda s, t: (t[row, s], 0, 0))

    return pl.pallas_call(
        kept_kernel,
        grid_spec=pltpu.PrefetchScalarGridSpec(
            num_scalar_prefetch=1,
            grid=(count,),
            in_specs=lhs_specs(rows, block, hid)
            + [pl.BlockSpec((1, block, 3 * hid), lambda s, t: (t[7, s], 0, 0))],
            out_specs=[out(1), out(2), out(4), out(5)],
        ),
        out_shape=[piece] * 4,
        compiler_params=params(),
        cost_estimate=cost(6 * rows * block * count * hid, 15e6),
        name="kept_grads",
    )(table, *lhs_arrays(table, normed, masked, block), d_gate, d_up, hidden, got)


def forward_kernel(x_ref, gain_ref, gate_ref, up_ref, slope_up, slope_gate, hidden_ref, normed_out, normed):
    @pl.when(pl.program_id(0) == 0)
    def _():
        rows = x_ref[...].astype(F32)
        inv = lax.rsqrt(jnp.mean(rows * rows, axis=1, keepdims=True) + 1e-05)
        normed[...] = (rows * inv * gain_ref[...].astype(F32)).astype(BF16)
        normed_out[...] = normed[...]

    gate_act = mm(normed[...], gate_ref[...])
    up_act = mm(normed[...], up_ref[...])
    sig = 1.0 / (1.0 + jnp.exp(-gate_act))
    silu = gate_act * sig
    hidden_ref[...] = (silu * up_act).astype(BF16)
    slope_up[...] = silu.astype(BF16)
    slope_gate[...] = (up_act * sig * (1.0 + gate_act * (1.0 - sig))).astype(BF16)


def item_forward(x, gain, w_gate, w_up):
    rows, width = x.shape
    hid = w_gate.shape[1]
    tile = min(TILE, hid)
    weights = pl.BlockSpec((width, tile), lambda s: (0, s))
    columns = pl.BlockSpec((rows, tile), lambda s: (0, s))
    narrow = jax.ShapeDtypeStruct((rows, hid), BF16)
    return pl.pallas_call(
        forward_kernel,
        grid=(hid // tile,),
        in_specs=[whole_spec((rows, width)), whole_spec((1, width)), weights, weights],
        out_specs=[columns] * 3 + [whole_spec((rows, width))],
        out_shape=[narrow] * 3 + [jax.ShapeDtypeStruct((rows, width), BF16)],
        scratch_shapes=[pltpu.VMEM((rows, width), BF16)],
        compiler_params=params(),
        cost_estimate=cost(4 * rows * width * hid, 12e6),
        name="item_forward",
    )(x, gain, w_gate, w_up)


def own_kernel(cot_ref, slope_up, slope_gate, gate_ref, up_ref, down_ref, out_ref, total):
    step = pl.program_id(0)
    d_hidden = mm(cot_ref[...], down_ref[...], LAST)
    d_up = (d_hidden * slope_up[...].astype(F32)).astype(BF16)
    d_gate = (d_hidden * slope_gate[...].astype(F32)).astype(BF16)
    part = mm(d_gate, gate_ref[...], LAST) + mm(d_up, up_ref[...], LAST)

    @pl.when(step == 0)
    def _():
        total[...] = part

    @pl.when(step > 0)
    def _():
        total[...] += part

    @pl.when(step == pl.num_programs(0) - 1)
    def _():
        out_ref[...] = total[...].astype(BF16)


def item_own(cot, slope_up, slope_gate, w_gate, w_up, w_down):
    rows, width = cot.shape
    hid = w_gate.shape[1]
    tile = min(TILE, hid)
    weights = pl.BlockSpec((width, tile), lambda s: (0, s))
    columns = pl.BlockSpec((rows, tile), lambda s: (0, s))
    return pl.pallas_call(
        own_kernel,
        grid=(hid // tile,),
        in_specs=[
            whole_spec((rows, width)),
            columns,
            columns,
            weights,
            weights,
            pl.BlockSpec((tile, width), lambda s: (s, 0)),
        ],
        out_specs=whole_spec((rows, width)),
        out_shape=jax.ShapeDtypeStruct((rows, width), BF16),
        scratch_shapes=[pltpu.VMEM((rows, width), F32)],
        compiler_params=params(),
        cost_estimate=cost(6 * rows * width * hid, 11e6),
        name="item_own",
    )(cot, slope_up, slope_gate, w_gate, w_up, w_down)


def late_kernel(
    scale, at_ref, cot0, cot1, col0, col1, n0, n1, su0, su1, sg0, sg1, h0, h1, down_ref,
    gate_out, up_out, down_out,
):
    sums = None
    for cot, col, normed, su, sg, hidden in ((cot0, col0, n0, su0, sg0, h0), (cot1, col1, n1, su1, sg1, h1)):
        d_hidden = mm(cot[...], down_ref[...], LAST)
        d_up = (d_hidden * su[...].astype(F32)).astype(BF16)
        d_gate = (d_hidden * sg[...].astype(F32)).astype(BF16)
        found = (
            mm(normed[...], d_gate, FIRST),
            mm(normed[...], d_up, FIRST),
            mm(hidden[...], col[...], FIRST),
        )
        sums = found if sums is None else tuple(a + b for a, b in zip(sums, found))
    gate_out[...] = sums[0] * scale
    up_out[...] = sums[1] * scale
    down_out[...] = sums[2] * scale


def item_late(me, cots, normeds, slope_ups, slope_gates, hiddens, w_down, block, scale):
    rows, width = cots[0].shape
    hid = w_down.shape[0]
    tile = min(TILE, hid)
    full = pl.BlockSpec((rows, width), lambda s, t: (0, 0))
    columns_of = list(cots) + list(normeds)
    if block % 128:
        mine = pl.BlockSpec((rows, block), lambda s, t: (0, 0))
        columns_of = [lax.dynamic_slice_in_dim(a, me * block, block, axis=1) for a in columns_of]
    else:
        mine = pl.BlockSpec((rows, block), lambda s, t: (0, t[0]))
    columns = pl.BlockSpec((rows, tile), lambda s, t: (0, s))
    out = pl.BlockSpec((block, tile), lambda s, t: (0, s))
    return pl.pallas_call(
        functools.partial(late_kernel, scale),
        grid_spec=pltpu.PrefetchScalarGridSpec(
            num_scalar_prefetch=1,
            grid=(hid // tile,),
            in_specs=[full, full, mine, mine, mine, mine]
            + [columns] * 6
            + [pl.BlockSpec((tile, width), lambda s, t: (s, 0))],
            out_specs=[out, out, pl.BlockSpec((tile, block), lambda s, t: (s, 0))],
        ),
        out_shape=[
            jax.ShapeDtypeStruct((block, hid), F32),
            jax.ShapeDtypeStruct((block, hid), F32),
            jax.ShapeDtypeStruct((hid, block), F32),
        ],
        compiler_params=params(),
        cost_estimate=cost(4 * rows * width * hid + 12 * rows * block * hid, 16e6),
        name="item_late",
    )(jnp.reshape(me, (1,)), *cots, *columns_of, *slope_ups, *slope_gates, *hiddens, w_down)


def grad_tables(n_chips, chip, core, order_a, order_b):
    first_a, first_b = order_a[0] >> 1, order_b[0] >> 1
    rels = sorted(range(n_chips), key=lambda r: (not (r & first_a), not (r & first_b), r))
    rows = [[], [], [], [], [], [], []]
    places = {}
    for name, first, row in (("a", first_a, 0), ("b", first_b, 3)):
        sent_order = [r for r in rels if r & first]
        kept_order = [r for r in rels if not r & first]
        last_sent = last_kept = 0
        for r in rels:
            is_sent = bool(r & first)
            if is_sent:
                last_sent = sent_order.index(r)
            else:
                last_kept = kept_order.index(r)
            rows[row].append(last_sent)
            rows[row + 1].append(last_kept)
            rows[row + 2].append(int(is_sent))
        places[name] = kept_order
    rel = jnp.array(rels, jnp.int32)
    fixed = [jnp.array(r, jnp.int32) for r in rows[:6]]
    table = jnp.stack([(chip ^ rel) * 2 + core, *fixed, rel])
    return table, places


def finish_halving(sent, kept, order, slots):
    got = swap(sent, order[0])
    total = {r: kept[i].astype(F32) + got[i].astype(F32) for i, r in enumerate(slots)}
    for bit in order[1:]:
        away = sorted(r for r in total if r & (bit >> 1))
        block = jnp.stack([total[r].astype(BF16) for r in away])
        got = swap(block, bit)
        total = {
            r ^ (bit >> 1): total[r ^ (bit >> 1)].astype(BF16).astype(F32) + got[i].astype(F32)
            for i, r in enumerate(away)
        }
    return total[0]


def body(
    user_input,
    out_grad,
    hist_len,
    hist_items,
    item_row,
    item_feat,
    user_gain,
    user_gate,
    user_up,
    user_down,
    item_gain,
    item_gate,
    item_up,
    item_down,
):
    n_wide, n_narrow = lax.axis_size("wide"), lax.axis_size("narrow")
    me, here = lax.axis_index("wide"), lax.axis_index("narrow")
    chip, core = me // 2, me % 2
    n_chips = n_wide // 2
    bits = [1 << k for k in range(1, n_wide.bit_length() - 1)]
    order_a = bits
    order_b = bits[len(bits) // 2 :] + bits[: len(bits) // 2]
    user_count, hist_length, width = user_input.shape
    rows = user_count * hist_length
    item_dev = item_feat.shape[0]
    hid = user_gate.shape[1]
    block = width // n_wide
    rels = jnp.arange(n_chips, dtype=jnp.int32)
    gain_user, gain_item = user_gain.reshape(1, width), item_gain.reshape(1, width)

    def gather_wide(value):
        near = jnp.concatenate([value] + [swap(value, r << 1) for r in range(1, n_chips)], axis=0)
        return near, swap(near, 1)

    feats = gather_wide(item_feat)

    valid = (jnp.arange(hist_length, dtype=jnp.int32)[None, :] < hist_len[:, None]).astype(F32)
    ids = jnp.arange(item_row.shape[0], dtype=jnp.int32)
    targets = jnp.sum(
        jnp.where(hist_items.reshape(rows)[:, None] == ids[None, :], item_row[None, :], 0), axis=1
    )

    def item_ids(parity):
        first = ((chip ^ rels) * 2 + parity) * item_dev
        return (first[:, None] + jnp.arange(item_dev, dtype=jnp.int32)[None, :]).reshape(-1, 1)

    normed, masked, hidden, d_gate, d_up, sent, kept = user_layer(
        user_input.reshape(rows, width),
        out_grad.reshape(rows, width),
        valid.reshape(rows, 1),
        gain_user,
        user_gate,
        user_up,
        user_down,
        targets.reshape(1, rows),
        item_ids(1 - core),
        item_ids(core),
        1.0 / n_narrow,
    )

    got = swap(sent, 1)
    pieces = []
    for r in range(n_chips):
        at = slice(r * item_dev, (r + 1) * item_dev)
        piece = kept[at].astype(F32) + got[at].astype(F32)
        pieces.append(piece if r == 0 else swap(piece.astype(BF16), r << 1))
    mine = functools.reduce(jnp.add, [p.astype(F32) for p in pieces]).astype(BF16)

    sent_table = jnp.stack([(chip ^ rels) * 2 + 1 - core])
    kept_table, places = grad_tables(n_chips, chip, core, order_a, order_b)
    grads_got = swap(sent_grads(sent_table, normed, masked, d_gate, d_up, hidden, block), 1)
    sent_a, kept_a, sent_b, kept_b = kept_grads(
        kept_table, normed, masked, d_gate, d_up, hidden, grads_got, block
    )
    user_grads = jnp.concatenate(
        [
            finish_halving(sent_a, kept_a, order_a, places["a"]),
            finish_halving(sent_b, kept_b, order_b, places["b"]),
        ],
        axis=0,
    ) * (1.0 / n_wide)

    quarter = item_dev // n_narrow

    def narrow_rows(value):
        return lax.dynamic_slice_in_dim(value, here * quarter, quarter, axis=0)

    def narrow_scatter(value):
        parts = lax.all_to_all(
            value.reshape(n_narrow, quarter, width), "narrow", split_axis=0, concat_axis=0, tiled=True
        )
        return jnp.sum(parts.astype(F32), axis=0)

    def narrow_gather(piece):
        return lax.all_gather(piece, "narrow", axis=0, tiled=True)

    forwards = [item_forward(x, gain_item, item_gate, item_up) for x in feats]
    slope_ups, slope_gates, hiddens, normeds = zip(*forwards)

    item_in = narrow_scatter(mine)
    item_cot = narrow_gather(item_in.astype(BF16))
    cots = gather_wide(item_cot)
    item_part = item_own(
        item_cot, slope_ups[0][:item_dev], slope_gates[0][:item_dev], item_gate, item_up, item_down
    )
    item_scaled = gain_item.astype(F32) * narrow_scatter(item_part)
    own = narrow_rows(item_feat).astype(F32)
    own_inv = lax.rsqrt(jnp.mean(own * own, axis=1, keepdims=True) + 1e-05)
    own_unit = own * own_inv
    item_mean = jnp.mean(item_scaled * own_unit, axis=1, keepdims=True)
    feat_grad = narrow_gather(
        (item_in + own_inv * (item_scaled - own_unit * item_mean)).astype(BF16)
    )
    item_gate_grad, item_up_grad, item_down_grad = item_late(
        me, cots, normeds, slope_ups, slope_gates, hiddens, item_down, block, 1.0 / n_wide
    )
    return (
        feat_grad,
        user_grads[:, :hid],
        user_grads[:, hid : 2 * hid],
        user_grads[:, 2 * hid :].T,
        item_gate_grad,
        item_up_grad,
        item_down_grad,
    )


def solution(mesh):
    placed = (
        P("wide", None, None),
        P("wide", None, None),
        P("wide"),
        P("wide", None),
        P(),
        P("wide", None),
        P(),
        P(None, "narrow"),
        P(None, "narrow"),
        P("narrow", None),
        P(),
        P(None, "narrow"),
        P(None, "narrow"),
        P("narrow", None),
    )
    return jax.shard_map(
        body,
        mesh=mesh,
        in_specs=placed,
        out_specs=(
            P("wide", None),
            P("wide", "narrow"),
            P("wide", "narrow"),
            P("narrow", "wide"),
            P("wide", "narrow"),
            P("wide", "narrow"),
            P("narrow", "wide"),
        ),
        check_vma=False,
    )
```

time: 372 us -> 220 us (0.59)
  waiting for transfers between devices: 237 us -> 46.6 us
  Pallas kernels: 0 us -> 80.9 us
  matrix products: 42.5 us -> 0 us
  blocking collectives: 0 us -> 30.8 us
  other arithmetic: 35.5 us -> 13.1 us
  starting transfers between devices: 10.9 us -> 26.1 us
  between operations: 16 us -> 0.93 us
  local copies, waits for them, and re-layouts: 29.2 us -> 20.3 us
    reduce_scatter x6 -> x0, waiting for transfers between devices: 105 us -> none  [the longest x1 48 us: body(): lax.psum_scatter(item_terms[1].astype(jnp.bfloat16), 'wide', scatter_dime...]
    psum x2 -> x0, waiting for transfers between devices: 82.6 us -> none  [the longest x1 61.8 us: body(): lax.psum(d_partial.astype(jnp.bfloat16), 'narrow').astype(jnp.float32)]
    pallas_call x0 -> x7, Pallas kernels: none -> 80.9 us  [the longest x1 27.1 us: user_layer(): pl.pallas_call(functools.partial(user_kernel, steps, share), grid=(steps,...]
    all_to_all x2, waiting for transfers between devices: 49.3 us -> 1.18 us  [narrow_scatter(): lax.all_to_all(value.reshape(n_narrow, quarter, width), 'narrow', split_a...]
    ppermute x0 -> x17, waiting for transfers between devices: none -> 45.4 us  [swap(): return lax.ppermute(value, 'wide', [(i, i ^ bit) for i in range(count)])]
    dot_general x17 -> x0, matrix products: 42.5 us -> none  [the longest x2 8.12 us: layer_local(): lax.dot_general(hidden, cot_bf, first_dims, preferred_element_type=jnp.fl...]
    all_gather x0 -> x2, blocking collectives: none -> 30.8 us  [narrow_gather(): return lax.all_gather(piece, 'narrow', axis=0, tiled=True)]
    gather x3 -> x0, local copies, waits for them, and re-layouts: 20.5 us -> none  [the longest x1 11.4 us: send_buffers(): jnp.take(values, source, axis=0) * filled[:, None].astype(jnp.float32)]
  transfers between devices with their start and end apart: 10 -> 19, of which waited for: 6 -> 9; matrix products, arithmetic and copies ran while one was open for 21% -> 10% of each run, Pallas kernels for 0% -> 25%
where the time goes in v1:
time: 220 us; the launch traced here: 219 us
  Pallas kernels  80.9 us (37%)
  waiting for transfers between devices  46.6 us (21%)
  blocking collectives  30.8 us (14%)
  starting transfers between devices  26.1 us (12%)
  local copies, waits for them, and re-layouts  20.3 us (9%)
  other arithmetic  13.1 us (6%)
    ppermute x17, waiting for transfers between devices, swap(): return lax.ppermute(value, 'wide', [(i, i ^ bit) for i in range(count)])  45.4 us
    all_gather x2, blocking collectives, narrow_gather(): return lax.all_gather(piece, 'narrow', axis=0, tiled=True)  30.8 us
    pallas_call x1, Pallas kernels, user_layer(): pl.pallas_call(functools.partial(user_kernel, steps, share), grid=(steps,...  27.1 us
    pallas_call x2, Pallas kernels, item_forward(): pl.pallas_call(forward_kernel, grid=(hid // tile,), in_specs=[whole_spec(...  17.4 us
    ppermute x17, starting transfers between devices, swap(): return lax.ppermute(value, 'wide', [(i, i ^ bit) for i in range(count)])  16.1 us
    pallas_call x1, Pallas kernels, item_late(): pl.pallas_call(functools.partial(late_kernel, scale), grid_spec=pltpu.Pre...  10.5 us
    all_to_all x2, starting transfers between devices, narrow_scatter(): lax.all_to_all(value.reshape(n_narrow, quarter, width), 'narrow', split_a...  9.98 us
    pallas_call x1, Pallas kernels, kept_grads(): pl.pallas_call(kept_kernel, grid_spec=pltpu.PrefetchScalarGridSpec(num_sc...  9.59 us
  transfers between devices with their start and end apart: 19, of which 9 were waited for; matrix products, arithmetic and copies ran while one was open for 10% of the time, Pallas kernels for 25%

profile of v1, /device:TPU:0, one launch (start us, length us, event | category | flops | bytes accessed | tf_op | source)
XLA Modules:
  0.0 218.6 jit_solution(4692254515455928871)
XLA Ops:
  0.8 0.8 eq.17
  1.6 0.7 fusion.8
  2.3 1.3 reshape.174.gain_ref
  3.6 0.9 reshape.187.valid_ref
  4.5 0.9 copy.34.sent_ids_ref
  5.3 0.9 copy.35.kept_ids_ref
  6.2 1.7 select_reduce_fusion
  7.9 27.1 %user_layer.1 = (bf16[512,2048]{1,0:T(8,128)(2,1)}, bf16[512,2048]{1,0:T(8,128)(2,1)}, bf16[512,768]{1,0:T(8,128)(2,1)}, bf16[512,768]{1,0:T(8,128)(2,1)}, bf16[...) custom-call(bf16[512,2048]{1,0:T(8,128)(2,1)} %bitcast.20, bf16[512,2048]{1,0:T(8,128)(2,1)} %bitcast.21, ...), custom_call_target="tpu_custom_call" | custom-call | flops 8053063680 | bytes 20000000 | tf_op jit(solution)/shard_map/user_layer/pallas_call | solution.py:103
  35.0 0.5 collective-permute-start
  35.5 2.6 %collective-permute-start.5 = (bf16[128,2048]{1,0:T(8,128)(2,1)S(1)}, bf16[128,2048]{1,0:T(8,128)(2,1)S(1)}, u32[]{:S(2)}, u32[]{:S(2)}) collective-permute-start(bf16[128,2048]{1,0:T(8,128)(2,1)S(1)} %copy-done.3), channel_id=1, source_target_pairs={{0,16},{4,20},{8,24},{12,28},{16,0},{20,4},{24,8},{28,12},{1,17},{... | collective-permute-start | bytes 1572872 | tf_op jit(solution)/shard_map/ppermute | solution.py:37
  38.1 1.5 collective-permute-start.4
  39.6 0.5 add_subtract_fusion.table_ref
  40.1 7.6 %sent_grads.1 = bf16[4,256,2304]{2,1,0:T(8,128)(2,1)} custom-call(s32[1,4]{1,0:T(1,128)} %add_subtract_fusion.table_ref, bf16[512,2048]{1,0:T(8,128)(2,1)} %get-tuple-element.33.normed_ref, bf16[512,2048]{1,0:T(8,128)(2,1)} %get-tuple-element.34.masked_ref, bf16[512,768]{1,0:T(8,128)(2,1)} %get-tuple-element.35.d_gate_ref, ...), custom_call_target="tpu_custom_call" | custom-call | flops 2415919104 | bytes 10000000 | tf_op jit(solution)/shard_map/sent_grads/pallas_call | solution.py:194
  47.8 0.8 constant_dynamic-update-slice_fusion.3
  48.7 4.2 %collective-permute-done.4 = bf16[128,2048]{1,0:T(8,128)(2,1)S(1)} collective-permute-done((bf16[128,2048]{1,0:T(8,128)(2,1)S(1)}, bf16[128,2048]{1,0:T(8,128)(2,1)S(1)}, u32[]{:S(2)}, u32[]{:S(2)}) %collective-permute-start.4) | collective-permute-done | bytes 524320 | tf_op jit(solution)/shard_map/ppermute | solution.py:37
  52.9 0.8 constant_dynamic-update-slice_fusion.2
  53.7 0.9 constant_dynamic-update-slice_fusion.1
  54.6 0.5 add_convert_fusion.7
  55.1 1.6 collective-permute-start.1
  56.7 2.0 collective-permute-start.2
  58.7 4.7 %collective-permute-done.6 = bf16[128,2048]{1,0:T(8,128)(2,1)S(1)} collective-permute-done((bf16[128,2048]{1,0:T(8,128)(2,1)S(1)}, bf16[128,2048]{1,0:T(8,128)(2,1)S(1)}, u32[]{:S(2)}, u32[]{:S(2)}) %collective-permute-start.6) | collective-permute-done | bytes 524320 | tf_op jit(solution)/shard_map/ppermute | solution.py:37
  63.4 0.9 constant_dynamic-update-slice_fusion.x_ref
  64.4 10.9 %collective-permute-done.1 = bf16[128,2048]{1,0:T(8,128)(2,1)S(1)} collective-permute-done((bf16[128,2048]{1,0:T(8,128)(2,1)S(1)}, bf16[128,2048]{1,0:T(8,128)(2,1)S(1)}, u32[]{:S(2)}, u32[]{:S(2)}) %collective-permute-start.1) | collective-permute-done | bytes 524320 | tf_op jit(solution)/shard_map/ppermute | solution.py:37
  75.4 10.2 %collective-permute-done.3 = bf16[128,2048]{1,0:T(8,128)(2,1)S(1)} collective-permute-done((bf16[128,2048]{1,0:T(8,128)(2,1)S(1)}, bf16[128,2048]{1,0:T(8,128)(2,1)S(1)}, u32[]{:S(2)}, u32[]{:S(2)}) %collective-permute-start.3) | collective-permute-done | bytes 524320 | tf_op jit(solution)/shard_map/ppermute | solution.py:37
  85.5 1.2 add_convert_fusion.4
  86.8 5.1 %all-to-all-start = ((bf16[4,32,2048]{2,1,0:T(8,128)(2,1)}), bf16[4,32,2048]{2,1,0:T(8,128)(2,1)S(1)}, u32[]{:S(2)}, u32[]{:S(2)}) async-start(bf16[4,32,2048]{2,1,0:T(8,128)(2,1)} %bitcast.5), calls=%async_computation | async-start | bytes 1048576 | tf_op jit(solution)/shard_map/all_to_all | solution.py:498
  91.9 0.6 reshape.177.gain_ref
  92.5 0.6 stack.38.table_ref
  93.3 8.6 %item_forward.2 = (bf16[512,768]{1,0:T(8,128)(2,1)}, bf16[512,768]{1,0:T(8,128)(2,1)}, bf16[512,768]{1,0:T(8,128)(2,1)}, bf16[512,2048]{1,0:T(8,128)(2,1)}) custom-call(bf16[512,2048]{1,0:T(8,128)(2,1)} %constant_dynamic-update-slice_fusion.x_ref, bf16[1,2048]{1,0:T(2,128)(2,1)} %reshape.177.gain_ref, bf16[2048,768]{1,0:T(8,128)(2,1)} %gate_ref.7, ...), custom_call_target="tpu_custom_call" | custom-call | flops 3221225472 | bytes 12000000 | tf_op jit(solution)/shard_map/item_forward/pallas_call | solution.py:257
  101.9 1.6 slice.71.slope_up
  103.6 1.6 slice.72.slope_gate
  105.2 1.2 all-to-all-done
  106.5 15.2 %all_gather.6.cot_ref = bf16[128,2048]{1,0:T(8,128)(2,1)S(1)} all-gather(bf16[32,2048]{1,0:T(8,128)(2,1)S(1)} %convert_element_type.169), channel_id=1, replica_groups=mesh['wide'=8,'narrow'=4] {'narrow'}, dimensions={0}, use_global_device_ids=true | all-gather | bytes 655360 | tf_op jit(solution)/shard_map/all_gather | solution.py:504
  121.7 1.0 collective-permute-start.12
  122.7 8.8 %item_forward.3 = (bf16[512,768]{1,0:T(8,128)(2,1)}, bf16[512,768]{1,0:T(8,128)(2,1)}, bf16[512,768]{1,0:T(8,128)(2,1)}, bf16[512,2048]{1,0:T(8,128)(2,1)}) custom-call(bf16[512,2048]{1,0:T(8,128)(2,1)} %collective-permute-done.16.x_ref, bf16[1,2048]{1,0:T(2,128)(2,1)} %reshape.177.gain_ref, bf16[2048,768]{1,0:T(8,128)(2,1)} %gate_ref.7, ...), custom_call_target="tpu_custom_call" | custom-call | flops 3221225472 | bytes 12000000 | tf_op jit(solution)/shard_map/item_forward/pallas_call | solution.py:257
  131.4 1.4 collective-permute-start.14
  132.8 1.1 collective-permute-start.13
  133.9 8.7 %item_own.1 = bf16[128,2048]{1,0:T(8,128)(2,1)} custom-call(bf16[128,2048]{1,0:T(8,128)(2,1)} %copy-done.1, bf16[128,768]{1,0:T(8,128)(2,1)} %slice.71.slope_up, bf16[128,768]{1,0:T(8,128)(2,1)} %slice.72.slope_gate, bf16[2048,768]{1,0:T(8,128)(2,1)} %gate_ref.7, bf16[2048,768]{1,0:T(8,128)(2,1)} %up_ref.7, bf16[768,2048]{1,0:T(8,128)(2,1)} %down_ref.5), custom_call_target="tpu_custom_call" | custom-call | flops 1207959552 | bytes 11000000 | tf_op jit(solution)/shard_map/item_own/pallas_call | solution.py:296
  142.7 4.9 %all-to-all-start.1 = ((bf16[4,32,2048]{2,1,0:T(8,128)(2,1)}), bf16[4,32,2048]{2,1,0:T(8,128)(2,1)S(1)}, u32[]{:S(2)}, u32[]{:S(2)}) async-start(bf16[4,32,2048]{2,1,0:T(8,128)(2,1)} %bitcast.16), calls=%async_computation.1 | async-start | bytes 1048576 | tf_op jit(solution)/shard_map/all_to_all | solution.py:498
  147.5 1.1 constant_dynamic-update-slice_fusion.7
  148.6 1.1 constant_dynamic-update-slice_fusion.6
  149.7 5.0 %collective-permute-done.13 = bf16[128,2048]{1,0:T(8,128)(2,1)} collective-permute-done((bf16[128,2048]{1,0:T(8,128)(2,1)S(1)}, bf16[128,2048]{1,0:T(8,128)(2,1)}, u32[]{:S(2)}, u32[]{:S(2)}) %collective-permute-start.13) | collective-permute-done | bytes 524320 | tf_op jit(solution)/shard_map/ppermute | solution.py:37
  154.7 1.1 constant_dynamic-update-slice_fusion.5
  155.8 9.6 %kept_grads.1 = (bf16[2,128,2304]{2,1,0:T(8,128)(2,1)}, bf16[2,128,2304]{2,1,0:T(8,128)(2,1)}, bf16[2,128,2304]{2,1,0:T(8,128)(2,1)}, bf16[2,128,2304]{2,1,0:T(8,128)(2,1)}) custom-call(s32[8,4]{1,0:T(8,128)} %stack.38.table_ref, bf16[512,2048]{1,0:T(8,128)(2,1)} %get-tuple-element.33.normed_ref, bf16[512,2048]{1,0:T(8,128)(2,1)} %get-tuple-element.34.masked_ref, ...), custom_call_target="tpu_custom_call" | custom-call | flops 2415919104 | bytes 15000000 | tf_op jit(solution)/shard_map/kept_grads/pallas_call | solution.py:217
  165.4 1.5 collective-permute-start.8
  166.9 1.1 constant_dynamic-update-slice_fusion.4.cot0.col0
  168.2 1.7 fusion.2
  169.9 0.6 collective-permute-start.10
  170.5 1.0 fusion.6
  171.5 15.6 %all_gather.7 = bf16[128,2048]{1,0:T(8,128)(2,1)S(1)} all-gather(bf16[32,2048]{1,0:T(8,128)(2,1)S(1)} %fusion.6), channel_id=1, replica_groups=mesh['wide'=8,'narrow'=4] {'narrow'}, dimensions={0}, use_global_device_ids=true | all-gather | bytes 655360 | tf_op jit(solution)/shard_map/all_gather | solution.py:504
  187.1 5.3 %collective-permute-done.8 = bf16[2,128,2304]{2,1,0:T(8,128)(2,1)} collective-permute-done((bf16[2,128,2304]{2,1,0:T(8,128)(2,1)}, bf16[2,128,2304]{2,1,0:T(8,128)(2,1)}, u32[]{:S(2)}, u32[]{:S(2)}) %collective-permute-start.8) | collective-permute-done | bytes 1179680 | tf_op jit(solution)/shard_map/ppermute | solution.py:37
  192.4 1.2 add_convert_fusion.2
  193.6 1.6 collective-permute-start.9
  195.2 3.8 %collective-permute-done.10 = bf16[2,128,2304]{2,1,0:T(8,128)(2,1)S(1)} collective-permute-done((bf16[2,128,2304]{2,1,0:T(8,128)(2,1)}, bf16[2,128,2304]{2,1,0:T(8,128)(2,1)S(1)}, u32[]{:S(2)}, u32[]{:S(2)}) %collective-permute-start.10) | collective-permute-done | bytes 1179680 | tf_op jit(solution)/shard_map/ppermute | solution.py:37
  199.0 1.1 add_convert_fusion
  200.1 0.5 collective-permute-start.11
  200.6 10.5 %item_late.1 = (f32[256,768]{1,0:T(8,128)}, f32[256,768]{1,0:T(8,128)}, f32[768,256]{1,0:T(8,128)}) custom-call(s32[1]{0:T(128)} %bitcast.11.at_ref, bf16[512,2048]{1,0:T(8,128)(2,1)} %copy-done, bf16[512,2048]{1,0:T(8,128)(2,1)} %collective-permute-done.15.cot1.col1, bf16[512,2048]{1,0:T(8,128)(2,1)} %copy-done, ...), custom_call_target="tpu_custom_call" | custom-call | flops 4429185024 | bytes 16000000 | tf_op jit(solution)/shard_map/item_late/pallas_call | solution.py:349
  211.2 1.5 add_bitcast_fusion.1
  212.7 1.2 collective-permute-done.11
  213.9 1.3 add_bitcast_fusion
  215.1 0.2 maximum_multiply_fusion
  215.3 1.4 slice_bitcast_fusion
  216.7 1.1 copy.36
  217.8 0.8 copy.44
  (58 shorter events, 0.9 us)
Async XLA Ops:
  7.9 27.6 %copy-start.3 = (bf16[128,2048]{1,0:T(8,128)(2,1)S(1)}, bf16[128,2048]{1,0:T(8,128)(2,1)}, u32[]{:S(2)}) copy-start(bf16[128,2048]{1,0:T(8,128)(2,1)} %param.26) | copy-start | bytes 1572868
  35.0 19.6 %collective-permute-start = (bf16[512,2048]{1,0:T(8,128)(2,1)}, bf16[512,2048]{1,0:T(8,128)(2,1)S(1)}, u32[]{:S(2)}, u32[]{:S(2)}) collective-permute-start(bf16[512,2048]{1,0:T(8,128)(2,1)} %get-tuple-element.30), channel_id=1, source_target_pairs={{0,4},{4,0},{8,12},{12,8},{16,20},{20,16},{24,28},{28,24},{1,5},{5... | collective-permute-start | bytes 6291464 | tf_op jit(solution)/shard_map/ppermute | solution.py:37
  35.5 18.2 %collective-permute-start.5 = (bf16[128,2048]{1,0:T(8,128)(2,1)S(1)}, bf16[128,2048]{1,0:T(8,128)(2,1)S(1)}, u32[]{:S(2)}, u32[]{:S(2)}) collective-permute-start(bf16[128,2048]{1,0:T(8,128)(2,1)S(1)} %copy-done.3), channel_id=1, source_target_pairs={{0,16},{4,20},{8,24},{12,28},{16,0},{20,4},{24,8},{28,12},{1,17},{... | collective-permute-start | bytes 1572872 | tf_op jit(solution)/shard_map/ppermute | solution.py:37
  38.1 14.8 %collective-permute-start.4 = (bf16[128,2048]{1,0:T(8,128)(2,1)S(1)}, bf16[128,2048]{1,0:T(8,128)(2,1)S(1)}, u32[]{:S(2)}, u32[]{:S(2)}) collective-permute-start(bf16[128,2048]{1,0:T(8,128)(2,1)S(1)} %copy-done.3), channel_id=1, source_target_pairs={{0,8},{4,12},{8,0},{12,4},{16,24},{20,28},{24,16},{28,20},{1,9},{5... | collective-permute-start | bytes 1572872 | tf_op jit(solution)/shard_map/ppermute | solution.py:37
  47.7 6.9 %copy-start.2 = (bf16[512,2048]{1,0:T(8,128)(2,1)S(1)}, bf16[512,2048]{1,0:T(8,128)(2,1)}, u32[]{:S(2)}) copy-start(bf16[512,2048]{1,0:T(8,128)(2,1)} %get-tuple-element.29) | copy-start | bytes 6291460
  47.7 108.1 %collective-permute-start.7 = (bf16[4,256,2304]{2,1,0:T(8,128)(2,1)}, bf16[4,256,2304]{2,1,0:T(8,128)(2,1)}, u32[]{:S(2)}, u32[]{:S(2)}) collective-permute-start(bf16[4,256,2304]{2,1,0:T(8,128)(2,1)} %sent_grads.1), channel_id=1, source_target_pairs={{0,4},{4,0},{8,12},{12,8},{16,20},{20,16},{24,28},{28,24},{1,5},{5... | collective-permute-start | bytes 14155784 | tf_op jit(solution)/shard_map/ppermute | solution.py:37
  47.7 15.7 %collective-permute-start.6 = (bf16[128,2048]{1,0:T(8,128)(2,1)S(1)}, bf16[128,2048]{1,0:T(8,128)(2,1)S(1)}, u32[]{:S(2)}, u32[]{:S(2)}) collective-permute-start(bf16[128,2048]{1,0:T(8,128)(2,1)S(1)} %copy-done.3), channel_id=1, source_target_pairs={{0,24},{4,28},{8,16},{12,20},{16,8},{20,12},{24,0},{28,4},{1,25},{... | collective-permute-start | bytes 1572872 | tf_op jit(solution)/shard_map/ppermute | solution.py:37
  55.1 20.2 %collective-permute-start.1 = (bf16[128,2048]{1,0:T(8,128)(2,1)S(1)}, bf16[128,2048]{1,0:T(8,128)(2,1)S(1)}, u32[]{:S(2)}, u32[]{:S(2)}) collective-permute-start(bf16[128,2048]{1,0:T(8,128)(2,1)S(1)} %get-tuple-element.72), channel_id=1, source_target_pairs={{0,8},{4,12},{8,0},{12,4},{16,24},{20,28},{24,16},{28,20},{1,9},{5... | collective-permute-start | bytes 1572872 | tf_op jit(solution)/shard_map/ppermute | solution.py:37
  56.7 28.8 %collective-permute-start.3 = (bf16[128,2048]{1,0:T(8,128)(2,1)S(1)}, bf16[128,2048]{1,0:T(8,128)(2,1)S(1)}, u32[]{:S(2)}, u32[]{:S(2)}) collective-permute-start(bf16[128,2048]{1,0:T(8,128)(2,1)S(1)} %get-tuple-element.73), channel_id=1, source_target_pairs={{0,24},{4,28},{8,16},{12,20},{16,8},{20,12},{24,0},{28,4},{1,25},{... | collective-permute-start | bytes 1572872 | tf_op jit(solution)/shard_map/ppermute | solution.py:37
  56.7 28.8 %collective-permute-start.2 = (bf16[128,2048]{1,0:T(8,128)(2,1)S(1)}, bf16[128,2048]{1,0:T(8,128)(2,1)S(1)}, u32[]{:S(2)}, u32[]{:S(2)}) collective-permute-start(bf16[128,2048]{1,0:T(8,128)(2,1)S(1)} %get-tuple-element.74), channel_id=1, source_target_pairs={{0,16},{4,20},{8,24},{12,28},{16,0},{20,4},{24,8},{28,12},{1,17},{... | collective-permute-start | bytes 1572872 | tf_op jit(solution)/shard_map/ppermute | solution.py:37
  64.3 27.6 %copy-start.8 = (bf16[2048]{0:T(1024)(128)(2,1)S(1)}, bf16[2048]{0:T(1024)(128)(2,1)}, u32[]{:S(2)}) copy-start(bf16[2048]{0:T(1024)(128)(2,1)} %param.31) | copy-start | bytes 12292
  64.3 28.2 %copy-start.15 = (s32[4]{0:T(128)S(1)}, s32[4]{0:T(128)}, u32[]{:S(2)}) copy-start(s32[4]{0:T(128)} %constant.64.clone) | copy-start | bytes 52
  64.3 28.2 %copy-start.9 = (s32[1,4]{1,0:T(1,128)S(1)}, s32[1,4]{1,0:T(1,128)}, u32[]{:S(2)}) copy-start(s32[1,4]{1,0:T(1,128)} %constant.71) | copy-start | bytes 52
  64.3 28.2 %copy-start.10 = (s32[1,4]{1,0:T(1,128)S(1)}, s32[1,4]{1,0:T(1,128)}, u32[]{:S(2)}) copy-start(s32[1,4]{1,0:T(1,128)} %constant.75) | copy-start | bytes 52
  64.3 28.2 %copy-start.11 = (s32[1,4]{1,0:T(1,128)S(1)}, s32[1,4]{1,0:T(1,128)}, u32[]{:S(2)}) copy-start(s32[1,4]{1,0:T(1,128)} %constant.74) | copy-start | bytes 52
  64.3 28.2 %copy-start.12 = (s32[1,4]{1,0:T(1,128)S(1)}, s32[1,4]{1,0:T(1,128)}, u32[]{:S(2)}) copy-start(s32[1,4]{1,0:T(1,128)} %constant.73) | copy-start | bytes 52
  64.3 28.2 %copy-start.13 = (s32[1,4]{1,0:T(1,128)S(1)}, s32[1,4]{1,0:T(1,128)}, u32[]{:S(2)}) copy-start(s32[1,4]{1,0:T(1,128)} %constant.72) | copy-start | bytes 52
  64.3 28.2 %copy-start.14 = (s32[1,4]{1,0:T(1,128)S(1)}, s32[1,4]{1,0:T(1,128)}, u32[]{:S(2)}) copy-start(s32[1,4]{1,0:T(1,128)} %constant.70) | copy-start | bytes 52
  64.3 58.3 %collective-permute-start.16 = (bf16[512,2048]{1,0:T(8,128)(2,1)}, bf16[512,2048]{1,0:T(8,128)(2,1)}, u32[]{:S(2)}, u32[]{:S(2)}) collective-permute-start(bf16[512,2048]{1,0:T(8,128)(2,1)} %constant_dynamic-update-slice_fusion.x_ref), channel_id=1, source_target_pairs={{0,4},{4,0},{8,12},{12,8},{16,20},{20,16},{24,28},{28,24},{1,5},{5... | collective-permute-start | bytes 6291464 | tf_op jit(solution)/shard_map/ppermute | solution.py:37
  86.8 19.6 %all-to-all-start = ((bf16[4,32,2048]{2,1,0:T(8,128)(2,1)}), bf16[4,32,2048]{2,1,0:T(8,128)(2,1)S(1)}, u32[]{:S(2)}, u32[]{:S(2)}) async-start(bf16[4,32,2048]{2,1,0:T(8,128)(2,1)} %bitcast.5), calls=%async_computation | async-start | bytes 1048576 | tf_op jit(solution)/shard_map/all_to_all | solution.py:498
  121.7 12.3 %copy-start.1 = (bf16[128,2048]{1,0:T(8,128)(2,1)}, bf16[128,2048]{1,0:T(8,128)(2,1)S(1)}, u32[]{:S(2)}) copy-start(bf16[128,2048]{1,0:T(8,128)(2,1)S(1)} %all_gather.6.cot_ref) | copy-start | bytes 1572868
  121.7 26.9 %collective-permute-start.12 = (bf16[128,2048]{1,0:T(8,128)(2,1)S(1)}, bf16[128,2048]{1,0:T(8,128)(2,1)}, u32[]{:S(2)}, u32[]{:S(2)}) collective-permute-start(bf16[128,2048]{1,0:T(8,128)(2,1)S(1)} %all_gather.6.cot_ref), channel_id=1, source_target_pairs={{0,8},{4,12},{8,0},{12,4},{16,24},{20,28},{24,16},{28,20},{1,9},{5... | collective-permute-start | bytes 1572872 | tf_op jit(solution)/shard_map/ppermute | solution.py:37
  131.4 35.5 %collective-permute-start.14 = (bf16[128,2048]{1,0:T(8,128)(2,1)S(1)}, bf16[128,2048]{1,0:T(8,128)(2,1)}, u32[]{:S(2)}, u32[]{:S(2)}) collective-permute-start(bf16[128,2048]{1,0:T(8,128)(2,1)S(1)} %all_gather.6.cot_ref), channel_id=1, source_target_pairs={{0,24},{4,28},{8,16},{12,20},{16,8},{20,12},{24,0},{28,4},{1,25},{... | collective-permute-start | bytes 1572872 | tf_op jit(solution)/shard_map/ppermute | solution.py:37
  132.8 21.9 %collective-permute-start.13 = (bf16[128,2048]{1,0:T(8,128)(2,1)S(1)}, bf16[128,2048]{1,0:T(8,128)(2,1)}, u32[]{:S(2)}, u32[]{:S(2)}) collective-permute-start(bf16[128,2048]{1,0:T(8,128)(2,1)S(1)} %all_gather.6.cot_ref), channel_id=1, source_target_pairs={{0,16},{4,20},{8,24},{12,28},{16,0},{20,4},{24,8},{28,12},{1,17},{... | collective-permute-start | bytes 1572872 | tf_op jit(solution)/shard_map/ppermute | solution.py:37
  142.7 25.4 %all-to-all-start.1 = ((bf16[4,32,2048]{2,1,0:T(8,128)(2,1)}), bf16[4,32,2048]{2,1,0:T(8,128)(2,1)S(1)}, u32[]{:S(2)}, u32[]{:S(2)}) async-start(bf16[4,32,2048]{2,1,0:T(8,128)(2,1)} %bitcast.16), calls=%async_computation.1 | async-start | bytes 1048576 | tf_op jit(solution)/shard_map/all_to_all | solution.py:498
  165.4 27.0 %collective-permute-start.8 = (bf16[2,128,2304]{2,1,0:T(8,128)(2,1)}, bf16[2,128,2304]{2,1,0:T(8,128)(2,1)}, u32[]{:S(2)}, u32[]{:S(2)}) collective-permute-start(bf16[2,128,2304]{2,1,0:T(8,128)(2,1)} %get-tuple-element.39), channel_id=1, source_target_pairs={{0,8},{4,12},{8,0},{12,4},{16,24},{20,28},{24,16},{28,20},{1,9},{5... | collective-permute-start | bytes 3538952 | tf_op jit(solution)/shard_map/ppermute | solution.py:37
  168.0 25.6 %copy-start = (bf16[512,2048]{1,0:T(8,128)(2,1)}, bf16[512,2048]{1,0:T(8,128)(2,1)S(1)}, u32[]{:S(2)}) copy-start(bf16[512,2048]{1,0:T(8,128)(2,1)S(1)} %constant_dynamic-update-slice_fusion.4.cot0.col0) | copy-start | bytes 6291460
  168.0 32.6 %collective-permute-start.15 = (bf16[512,2048]{1,0:T(8,128)(2,1)S(1)}, bf16[512,2048]{1,0:T(8,128)(2,1)}, u32[]{:S(2)}, u32[]{:S(2)}) collective-permute-start(bf16[512,2048]{1,0:T(8,128)(2,1)S(1)} %constant_dynamic-update-slice_fusion.4.cot0.col0), channel_id=1, source_target_pairs={{0,4},{4,0},{8,12},{12,8},{16,20},{20,16},{24,28},{28,24},{1,5},{5... | collective-permute-start | bytes 6291464 | tf_op jit(solution)/shard_map/ppermute | solution.py:37
  168.1 24.3 %copy-start.5 = (bf16[2,128,2304]{2,1,0:T(8,128)(2,1)S(1)}, bf16[2,128,2304]{2,1,0:T(8,128)(2,1)}, u32[]{:S(2)}) copy-start(bf16[2,128,2304]{2,1,0:T(8,128)(2,1)} %get-tuple-element.38) | copy-start | bytes 3538948
  168.1 30.9 %copy-start.4 = (bf16[2,128,2304]{2,1,0:T(8,128)(2,1)S(1)}, bf16[2,128,2304]{2,1,0:T(8,128)(2,1)}, u32[]{:S(2)}) copy-start(bf16[2,128,2304]{2,1,0:T(8,128)(2,1)} %get-tuple-element.40) | copy-start | bytes 3538948
  169.9 29.1 %collective-permute-start.10 = (bf16[2,128,2304]{2,1,0:T(8,128)(2,1)}, bf16[2,128,2304]{2,1,0:T(8,128)(2,1)S(1)}, u32[]{:S(2)}, u32[]{:S(2)}) collective-permute-start(bf16[2,128,2304]{2,1,0:T(8,128)(2,1)} %get-tuple-element.41), channel_id=1, source_target_pairs={{0,16},{4,20},{8,24},{12,28},{16,0},{20,4},{24,8},{28,12},{1,17},{... | collective-permute-start | bytes 3538952 | tf_op jit(solution)/shard_map/ppermute | solution.py:37
  193.6 17.5 %collective-permute-start.9 = (bf16[1,128,2304]{2,1,0:T(8,128)(2,1)S(1)}, bf16[1,128,2304]{2,1,0:T(8,128)(2,1)}, u32[]{:S(2)}, u32[]{:S(2)}) collective-permute-start(bf16[1,128,2304]{2,1,0:T(8,128)(2,1)S(1)} %add_convert_fusion.2), channel_id=1, source_target_pairs={{0,16},{4,20},{8,24},{12,28},{16,0},{20,4},{24,8},{28,12},{1,17},{... | collective-permute-start | bytes 1769480 | tf_op jit(solution)/shard_map/ppermute | solution.py:37
  199.0 1.6 copy-start.6
  200.1 13.8 %collective-permute-start.11 = (bf16[1,128,2304]{2,1,0:T(8,128)(2,1)}, bf16[1,128,2304]{2,1,0:T(8,128)(2,1)}, u32[]{:S(2)}, u32[]{:S(2)}) collective-permute-start(bf16[1,128,2304]{2,1,0:T(8,128)(2,1)} %add_convert_fusion), channel_id=1, source_target_pairs={{0,8},{4,12},{8,0},{12,4},{16,24},{20,28},{24,16},{28,20},{1,9},{5... | collective-permute-start | bytes 1769480 | tf_op jit(solution)/shard_map/ppermute | solution.py:37
  211.1 2.7 %copy-start.7 = (bf16[2,128,2304]{2,1,0:T(8,128)(2,1)S(1)}, bf16[2,128,2304]{2,1,0:T(8,128)(2,1)}, u32[]{:S(2)}) copy-start(bf16[2,128,2304]{2,1,0:T(8,128)(2,1)} %copy-done.6) | copy-start | bytes 3538948

commit v2 on v1

v2 whole, which is shorter than its diff:
```python
import functools

import jax
import jax.numpy as jnp
from jax import lax
from jax.experimental import pallas as pl
from jax.experimental.pallas import tpu as pltpu
from jax.sharding import PartitionSpec as P

F32 = jnp.float32
BF16 = jnp.bfloat16
LAST = (((1,), (1,)), ((), ()))
FIRST = (((0,), (0,)), ((), ()))
PLAIN = (((1,), (0,)), ((), ()))
TILE = 256


def mm(a, b, dims=PLAIN):
    return lax.dot_general(a, b, dims, preferred_element_type=F32)


def params():
    return pltpu.CompilerParams(vmem_limit_bytes=60 << 20)


def cost(flops, touched):
    return pl.CostEstimate(flops=int(flops) // 6, bytes_accessed=int(touched) // 6, transcendentals=0)


def hbm():
    return pl.BlockSpec(memory_space=pl.ANY)


def vmem():
    return pl.BlockSpec(memory_space=pltpu.VMEM)


def smem():
    return pl.BlockSpec(memory_space=pltpu.SMEM)


def whole_spec(shape):
    return pl.BlockSpec(shape, lambda *_: (0,) * len(shape))


def swap(value, bit):
    count = lax.axis_size("wide")
    return lax.ppermute(value, "wide", [(i, i ^ bit) for i in range(count)])


def after(value, *others):
    return lax.optimization_barrier((value, *others))[0]


def tiles(total, size):
    size = min(size, total)
    return [slice(k, k + size) for k in range(0, total, size)]


def segment_picks(place, parity, targets, item_dev, count):
    column = lax.broadcasted_iota(jnp.int32, (1, count), 1)
    block = (place ^ (column // item_dev)) * 2 + parity
    return (targets == block * item_dev + column % item_dev).astype(BF16)


def user_kernel(
    share, item_dev, place_ref, hist_len_ref, x_hbm, og_hbm, hist_ref, item_row_ref, gain_ref,
    gate_hbm, up_hbm, down_hbm,
    normed_out, masked_out, hidden_out, d_gate_out, d_up_out, sent_out, kept_out,
    x, og, gate, up, down, normed, hidden, d_gate, d_up, gate_act, up_act, total, sent, kept, inv_ref,
    sems,
):
    loads = [
        pltpu.make_async_copy(src, dst, sems.at[k])
        for k, (src, dst) in enumerate(
            ((x_hbm, x), (gate_hbm, gate), (up_hbm, up), (og_hbm, og), (down_hbm, down))
        )
    ]
    for load in loads[:2]:
        load.start()
    stores = [
        pltpu.make_async_copy(src, dst, sems.at[5 + k])
        for k, (src, dst) in enumerate(
            (
                (normed, normed_out),
                (og, masked_out),
                (hidden, hidden_out),
                (d_gate, d_gate_out),
                (d_up, d_up_out),
            )
        )
    ]
    rows, width = x.shape
    users, length = hist_ref.shape
    hid = hidden.shape[1]
    gain = gain_ref[...].reshape(1, width).astype(F32)

    square = (length, length)
    diagonal = lax.broadcasted_iota(jnp.int32, square, 0) == lax.broadcasted_iota(jnp.int32, square, 1)
    item_row = item_row_ref[...].reshape(1, -1)
    ids = lax.broadcasted_iota(jnp.int32, (1, item_row.shape[1]), 1)
    targets = []
    for u in range(users):
        items = jnp.sum(jnp.where(diagonal, hist_ref[u : u + 1, :], 0), axis=1, keepdims=True)
        targets.append(jnp.sum(jnp.where(items == ids, item_row, 0), axis=1, keepdims=True))
    targets = jnp.concatenate(targets, axis=0)

    loads[0].wait()
    for load in loads[2:]:
        load.start()
    for at in tiles(rows, 64):
        part = x[at, :].astype(F32)
        inv = lax.rsqrt(jnp.mean(part * part, axis=1, keepdims=True) + 1e-05)
        inv_ref[at, :] = inv
        normed[at, :] = (part * inv * gain).astype(BF16)
    stores[0].start()
    loads[1].wait()
    for at in tiles(hid, TILE):
        gate_act[:, at] = mm(normed[...], gate[:, at])
    loads[2].wait()
    for at in tiles(hid, TILE):
        up_act[:, at] = mm(normed[...], up[:, at])
    loads[3].wait()
    place = lax.broadcasted_iota(jnp.int32, (length, 1), 0)
    for u in range(users):
        at = slice(u * length, (u + 1) * length)
        og[at, :] = jnp.where(place < hist_len_ref[u], og[at, :].astype(F32), 0.0).astype(BF16)
    stores[1].start()
    loads[4].wait()
    for at in tiles(hid, TILE):
        d_hidden = mm(og[...], down[at, :], LAST)
        gate_part, up_part = gate_act[:, at], up_act[:, at]
        sig = 1.0 / (1.0 + jnp.exp(-gate_part))
        silu = gate_part * sig
        hidden[:, at] = (silu * up_part).astype(BF16)
        d_up[:, at] = (d_hidden * silu).astype(BF16)
        d_gate[:, at] = (d_hidden * up_part * sig * (1.0 + gate_part * (1.0 - sig))).astype(BF16)
    for k in (2, 3, 4):
        stores[k].start()
    mean = jnp.zeros((rows, 1), F32)
    inv = inv_ref[...]
    for at in tiles(width, 512):
        part = mm(d_gate[...], gate[at, :], LAST) + mm(d_up[...], up[at, :], LAST)
        part = part * gain[:, at]
        total[:, at] = part
        mean = mean + jnp.sum(part * (x[:, at].astype(F32) * inv), axis=1, keepdims=True)
    slope = inv * inv * mean * (1.0 / width)
    chip, core = place_ref[0], place_ref[1]
    half = sent.shape[0]
    picks_sent = segment_picks(chip, 1 - core, targets, item_dev, half)
    picks_kept = segment_picks(chip, core, targets, item_dev, half)
    for at in tiles(width, 512):
        occ = (
            og[:, at].astype(F32) * share + inv * total[:, at] - x[:, at].astype(F32) * slope
        ).astype(BF16)
        sent[:, at] = mm(picks_sent, occ, FIRST).astype(BF16)
        kept[:, at] = mm(picks_kept, occ, FIRST).astype(BF16)
        for src, dst in ((sent, sent_out), (kept, kept_out)):
            stores.append(pltpu.make_async_copy(src.at[:, at], dst.at[:, at], sems.at[5 + len(stores)]))
            stores[-1].start()
    for store in stores:
        store.wait()


def user_layer(place, hist_len, x, og, hist, item_row, gain, w_gate, w_up, w_down, share, item_dev):
    rows, width = x.shape
    hid = w_gate.shape[1]
    half = item_row.shape[0] // 2
    wide = jax.ShapeDtypeStruct((rows, width), BF16)
    narrow = jax.ShapeDtypeStruct((rows, hid), BF16)
    summed = jax.ShapeDtypeStruct((half, width), BF16)
    return pl.pallas_call(
        functools.partial(user_kernel, share, item_dev),
        in_specs=[smem()] * 2 + [hbm()] * 2 + [vmem()] * 3 + [hbm()] * 3,
        out_specs=[hbm()] * 7,
        out_shape=[wide, wide, narrow, narrow, narrow, summed, summed],
        scratch_shapes=[
            pltpu.VMEM((rows, width), BF16),
            pltpu.VMEM((rows, width), BF16),
            pltpu.VMEM((width, hid), BF16),
            pltpu.VMEM((width, hid), BF16),
            pltpu.VMEM((hid, width), BF16),
            pltpu.VMEM((rows, width), BF16),
            pltpu.VMEM((rows, hid), BF16),
            pltpu.VMEM((rows, hid), BF16),
            pltpu.VMEM((rows, hid), BF16),
            pltpu.VMEM((rows, hid), F32),
            pltpu.VMEM((rows, hid), F32),
            pltpu.VMEM((rows, width), F32),
            pltpu.VMEM((half, width), BF16),
            pltpu.VMEM((half, width), BF16),
            pltpu.VMEM((rows, 1), F32),
            pltpu.SemaphoreType.DMA((10 + 2 * len(tiles(width, 512)),)),
        ],
        compiler_params=params(),
        cost_estimate=cost(10 * rows * width * hid, 24e6),
        name="user_layer",
    )(place, hist_len, x, og, hist, item_row, gain, w_gate, w_up, w_down)


def grad_rows(normed_ref, masked_ref, d_gate_ref, d_up_ref, hidden_ref):
    left, right = normed_ref[...], masked_ref[...]
    return (
        mm(left, d_gate_ref[...], FIRST),
        mm(left, d_up_ref[...], FIRST),
        mm(right, hidden_ref[...], FIRST),
    )


def sent_kernel(table_ref, normed_ref, masked_ref, d_gate_ref, d_up_ref, hidden_ref, out_ref):
    hid = hidden_ref.shape[1]
    found = grad_rows(normed_ref, masked_ref, d_gate_ref, d_up_ref, hidden_ref)
    for k, piece in enumerate(found):
        out_ref[0, :, k * hid : (k + 1) * hid] = piece.astype(BF16)


def kept_kernel(
    table_ref, normed_ref, masked_ref, d_gate_ref, d_up_ref, hidden_ref, got_ref,
    sent_a, kept_a, sent_b, kept_b,
):
    step = pl.program_id(0)
    hid = hidden_ref.shape[1]
    cut = got_ref.shape[1] // 2
    found = grad_rows(normed_ref, masked_ref, d_gate_ref, d_up_ref, hidden_ref)
    for first, sent, kept, flag in ((0, sent_a, kept_a, 3), (cut, sent_b, kept_b, 6)):
        for k, piece in enumerate(found):
            at = slice(k * hid, (k + 1) * hid)
            value = piece[first : first + cut] + got_ref[0, first : first + cut, at].astype(F32)
            value = value.astype(BF16)

            @pl.when(table_ref[flag, step] == 1)
            def _(sent=sent, value=value, at=at):
                sent[0, :, at] = value

            @pl.when(table_ref[flag, step] == 0)
            def _(kept=kept, value=value, at=at):
                kept[0, :, at] = value


def lhs_specs(rows, block, hid):
    if block % 128:
        column = pl.BlockSpec((None, rows, block), lambda s, t: (s, 0, 0))
    else:
        column = pl.BlockSpec((rows, block), lambda s, t: (0, t[0, s]))
    return [column, column] + [whole_spec((rows, hid))] * 3


def lhs_arrays(table, normed, masked, block):
    if block % 128 == 0:
        return normed, masked
    return tuple(
        jnp.take(jnp.swapaxes(a.reshape(a.shape[0], -1, block), 0, 1), table[0], axis=0)
        for a in (normed, masked)
    )


def sent_grads(table, normed, masked, d_gate, d_up, hidden, block):
    rows, hid = hidden.shape
    count = table.shape[1]
    return pl.pallas_call(
        sent_kernel,
        grid_spec=pltpu.PrefetchScalarGridSpec(
            num_scalar_prefetch=1,
            grid=(count,),
            in_specs=lhs_specs(rows, block, hid),
            out_specs=pl.BlockSpec((1, block, 3 * hid), lambda s, t: (s, 0, 0)),
        ),
        out_shape=jax.ShapeDtypeStruct((count, block, 3 * hid), BF16),
        compiler_params=params(),
        cost_estimate=cost(6 * rows * block * count * hid, 10e6),
        name="sent_grads",
    )(table, *lhs_arrays(table, normed, masked, block), d_gate, d_up, hidden)


def kept_grads(table, normed, masked, d_gate, d_up, hidden, got, block):
    rows, hid = hidden.shape
    count = table.shape[1]
    piece = jax.ShapeDtypeStruct((count // 2, block // 2, 3 * hid), BF16)

    def out(row):
        return pl.BlockSpec((1, block // 2, 3 * hid), lambda s, t: (t[row, s], 0, 0))

    return pl.pallas_call(
        kept_kernel,
        grid_spec=pltpu.PrefetchScalarGridSpec(
            num_scalar_prefetch=1,
            grid=(count,),
            in_specs=lhs_specs(rows, block, hid)
            + [pl.BlockSpec((1, block, 3 * hid), lambda s, t: (t[7, s], 0, 0))],
            out_specs=[out(1), out(2), out(4), out(5)],
        ),
        out_shape=[piece] * 4,
        compiler_params=params(),
        cost_estimate=cost(6 * rows * block * count * hid, 15e6),
        name="kept_grads",
    )(table, *lhs_arrays(table, normed, masked, block), d_gate, d_up, hidden, got)


def forward_kernel(count, place_ref, gain_ref, *refs):
    feats, (gate_hbm, up_hbm) = refs[:count], refs[count : count + 2]
    normed_out, hidden_out, slope_up_out, slope_gate_out = refs[count + 2 : count + 6]
    x, normed, gate, up, gate_act, hidden, slope_up, slope_gate, sems = refs[count + 6 :]
    width, hid = gate.shape
    all_rows = x.shape[0]
    rows = all_rows // count
    pieces = [
        pltpu.make_async_copy(feats[k], x.at[pl.ds(k * rows, rows)], sems.at[k]) for k in range(count)
    ]
    gate_load = pltpu.make_async_copy(gate_hbm, gate, sems.at[count])
    up_load = pltpu.make_async_copy(up_hbm, up, sems.at[count + 1])
    halves = [range(count // 2), range(count // 2, count)]
    for k in halves[0]:
        pieces[k].start()
    gate_load.start()
    gain = gain_ref[...].reshape(1, width).astype(F32)

    def normalise(k):
        for at in tiles(rows, 64):
            at = slice(k * rows + at.start, k * rows + at.stop)
            part = x[at, :].astype(F32)
            inv = lax.rsqrt(jnp.mean(part * part, axis=1, keepdims=True) + 1e-05)
            normed[at, :] = (part * inv * gain).astype(BF16)

    for k in halves[0]:
        pieces[k].wait()
    for k in halves[1]:
        pieces[k].start()
    up_load.start()
    for k in halves[0]:
        normalise(k)
    gate_load.wait()
    for h in range(2):
        part = slice(h * all_rows // 2, (h + 1) * all_rows // 2)
        if h == 1:
            for k in halves[1]:
                pieces[k].wait()
            for k in halves[1]:
                normalise(k)
        for at in tiles(hid, TILE):
            gate_act[part, at] = mm(normed[part, :], gate[:, at])
    block = normed_out.shape[1]
    mine = normed
    if block < width:
        mine = normed.at[:, pl.ds(pl.multiple_of(place_ref[2] * block, 128), block)]
    stores = [pltpu.make_async_copy(mine, normed_out, sems.at[count + 2])]
    stores[0].start()
    up_load.wait()
    for at in tiles(hid, TILE):
        up_part = mm(normed[...], up[:, at])
        gate_part = gate_act[:, at]
        sig = 1.0 / (1.0 + jnp.exp(-gate_part))
        silu = gate_part * sig
        hidden[:, at] = (silu * up_part).astype(BF16)
        slope_up[:, at] = silu.astype(BF16)
        slope_gate[:, at] = (up_part * sig * (1.0 + gate_part * (1.0 - sig))).astype(BF16)
        for src, dst in ((hidden, hidden_out), (slope_up, slope_up_out), (slope_gate, slope_gate_out)):
            sem = sems.at[count + 2 + len(stores)]
            stores.append(pltpu.make_async_copy(src.at[:, at], dst.at[:, at], sem))
            stores[-1].start()
    for store in stores:
        store.wait()


def item_forward(place, gain, feats, w_gate, w_up, block):
    count = len(feats)
    rows, width = count * feats[0].shape[0], feats[0].shape[1]
    hid = w_gate.shape[1]
    kept = width if block % 128 else block
    narrow = jax.ShapeDtypeStruct((rows, hid), BF16)
    return pl.pallas_call(
        functools.partial(forward_kernel, count),
        in_specs=[smem(), vmem()] + [hbm()] * (count + 2),
        out_specs=[hbm()] * 4,
        out_shape=[jax.ShapeDtypeStruct((rows, kept), BF16)] + [narrow] * 3,
        scratch_shapes=[
            pltpu.VMEM((rows, width), BF16),
            pltpu.VMEM((rows, width), BF16),
            pltpu.VMEM((width, hid), BF16),
            pltpu.VMEM((width, hid), BF16),
            pltpu.VMEM((rows, hid), F32),
            pltpu.VMEM((rows, hid), BF16),
            pltpu.VMEM((rows, hid), BF16),
            pltpu.VMEM((rows, hid), BF16),
            pltpu.SemaphoreType.DMA((count + 3 + 3 * len(tiles(hid, TILE)),)),
        ],
        compiler_params=params(),
        cost_estimate=cost(4 * rows * width * hid, 16e6),
        name="item_forward",
    )(place, gain, *feats, w_gate, w_up)


def own_kernel(
    cot, slope_up, slope_gate, gate_hbm, up_hbm, down_hbm, out_ref, gate, up, down, sems
):
    loads = [
        pltpu.make_async_copy(src, dst, sems.at[k])
        for k, (src, dst) in enumerate(((down_hbm, down), (gate_hbm, gate), (up_hbm, up)))
    ]
    for load in loads:
        load.start()
    loads[0].wait()
    d_hidden = mm(cot[...], down[...], LAST)
    d_up = (d_hidden * slope_up[...].astype(F32)).astype(BF16)
    d_gate = (d_hidden * slope_gate[...].astype(F32)).astype(BF16)
    loads[1].wait()
    loads[2].wait()
    for at in tiles(out_ref.shape[1], 512):
        out_ref[:, at] = (mm(d_gate, gate[at, :], LAST) + mm(d_up, up[at, :], LAST)).astype(BF16)


def item_own(cot, slope_up, slope_gate, w_gate, w_up, w_down):
    rows, width = cot.shape
    hid = w_gate.shape[1]
    return pl.pallas_call(
        own_kernel,
        grid=(1,),
        in_specs=[whole_spec((rows, width)), whole_spec((rows, hid)), whole_spec((rows, hid))]
        + [hbm()] * 3,
        out_specs=whole_spec((rows, width)),
        out_shape=jax.ShapeDtypeStruct((rows, width), BF16),
        scratch_shapes=[
            pltpu.VMEM((width, hid), BF16),
            pltpu.VMEM((width, hid), BF16),
            pltpu.VMEM((hid, width), BF16),
            pltpu.SemaphoreType.DMA((3,)),
        ],
        compiler_params=params(),
        cost_estimate=cost(6 * rows * width * hid, 11e6),
        name="item_own",
    )(cot, slope_up, slope_gate, w_gate, w_up, w_down)


def late_kernel(count, scale, place_ref, *refs):
    pieces, (column_hbm, normed_hbm, hidden_hbm, slope_up_hbm, slope_gate_hbm, down_hbm) = (
        refs[:count],
        refs[count : count + 6],
    )
    gate_out, up_out, down_out = refs[count + 6 : count + 9]
    cot, column, normed, hidden, slope_up, slope_gate, down, sems = refs[count + 9 :]
    rows = cot.shape[0] // count
    half = cot.shape[0] // 2
    used = 0

    def load(src, dst):
        nonlocal used
        copy = pltpu.make_async_copy(src, dst, sems.at[used])
        used += 1
        return copy

    narrow = normed.shape[1] % 128 != 0
    parts = []
    down_load = load(down_hbm, down)
    for h in range(2):
        at = pl.ds(h * half, half)
        waits = [
            load(pieces[k], cot.at[pl.ds(k * rows, rows)])
            for k in range(h * count // 2, (h + 1) * count // 2)
        ]
        for src, dst in (
            (slope_up_hbm, slope_up),
            (slope_gate_hbm, slope_gate),
            (normed_hbm, normed),
            (hidden_hbm, hidden),
        ):
            waits.append(load(src.at[at], dst.at[at]))
        if narrow:
            waits.append(load(column_hbm.at[at], column.at[at]))
        parts.append(waits)
    down_load.start()
    for copy in parts[0]:
        copy.start()
    block = column.shape[1]
    for h in range(2):
        for copy in parts[h]:
            copy.wait()
        if h == 0:
            down_load.wait()
            for copy in parts[1]:
                copy.start()
        at = slice(h * half, (h + 1) * half)
        if not narrow:
            column[at, :] = cot[at, pl.ds(pl.multiple_of(place_ref[2] * block, 128), block)]
        for to in tiles(hidden.shape[1], TILE):
            d_hidden = mm(cot[at, :], down[to, :], LAST)
            d_up = (d_hidden * slope_up[at, to].astype(F32)).astype(BF16)
            d_gate = (d_hidden * slope_gate[at, to].astype(F32)).astype(BF16)
            gate_part = mm(normed[at, :], d_gate, FIRST) * scale
            up_part = mm(normed[at, :], d_up, FIRST) * scale
            down_part = mm(hidden[at, to], column[at, :], FIRST) * scale
            if h == 0:
                gate_out[:, to] = gate_part
                up_out[:, to] = up_part
                down_out[to, :] = down_part
            else:
                gate_out[:, to] += gate_part
                up_out[:, to] += up_part
                down_out[to, :] += down_part


def item_late(place, pieces, column, normed, hidden, slope_up, slope_gate, w_down, scale):
    count = len(pieces)
    rows, width = count * pieces[0].shape[0], pieces[0].shape[1]
    hid, block = w_down.shape[0], normed.shape[1]
    return pl.pallas_call(
        functools.partial(late_kernel, count, scale),
        in_specs=[smem()] + [hbm()] * (count + 6),
        out_specs=[vmem()] * 3,
        out_shape=[
            jax.ShapeDtypeStruct((block, hid), F32),
            jax.ShapeDtypeStruct((block, hid), F32),
            jax.ShapeDtypeStruct((hid, block), F32),
        ],
        scratch_shapes=[
            pltpu.VMEM((rows, width), BF16),
            pltpu.VMEM((rows, block), BF16),
            pltpu.VMEM((rows, block), BF16),
            pltpu.VMEM((rows, hid), BF16),
            pltpu.VMEM((rows, hid), BF16),
            pltpu.VMEM((rows, hid), BF16),
            pltpu.VMEM((hid, width), BF16),
            pltpu.SemaphoreType.DMA((count + 11,)),
        ],
        compiler_params=params(),
        cost_estimate=cost(4 * rows * width * hid + 12 * rows * block * hid, 16e6),
        name="item_late",
    )(place, *pieces, column, normed, hidden, slope_up, slope_gate, w_down)


def place_kernel(here_ref, *refs):
    slots, out = refs[:-1], refs[-1]
    rows = slots[0].shape[0]
    for k, slot in enumerate(slots):
        out[pl.ds(pl.multiple_of((here_ref[0] ^ k) * rows, rows), rows), :] = slot[...]


def place_rows(here, slots):
    rows, width = slots[0].shape
    count = len(slots)
    return pl.pallas_call(
        place_kernel,
        in_specs=[smem()] + [vmem()] * count,
        out_specs=vmem(),
        out_shape=jax.ShapeDtypeStruct((count * rows, width), slots[0].dtype),
        compiler_params=params(),
        cost_estimate=cost(0, 4 * count * rows * width),
        name="place_rows",
    )(jnp.reshape(here, (1,)), *slots)


def grad_tables(n_chips, chip, core, order_a, order_b):
    first_a, first_b = order_a[0] >> 1, order_b[0] >> 1
    rels = sorted(range(n_chips), key=lambda r: (not (r & first_a), not (r & first_b), r))
    rows = [[], [], [], [], [], [], []]
    places = {}
    for name, first, row in (("a", first_a, 0), ("b", first_b, 3)):
        sent_order = [r for r in rels if r & first]
        kept_order = [r for r in rels if not r & first]
        last_sent = last_kept = 0
        for r in rels:
            is_sent = bool(r & first)
            if is_sent:
                last_sent = sent_order.index(r)
            else:
                last_kept = kept_order.index(r)
            rows[row].append(last_sent)
            rows[row + 1].append(last_kept)
            rows[row + 2].append(int(is_sent))
        places[name] = kept_order
    rel = jnp.array(rels, jnp.int32)
    fixed = [jnp.array(r, jnp.int32) for r in rows[:6]]
    table = jnp.stack([(chip ^ rel) * 2 + core, *fixed, rel])
    return table, places


def first_sums(got, kept, slots):
    return {r: kept[i].astype(F32) + got[i].astype(F32) for i, r in enumerate(slots)}


def sent_away(total, bit):
    away = sorted(r for r in total if r & (bit >> 1))
    return jnp.stack([total[r].astype(BF16) for r in away])


def next_sums(total, got, bit):
    away = sorted(r for r in total if r & (bit >> 1))
    return {r ^ (bit >> 1): total[r ^ (bit >> 1)] + got[i].astype(F32) for i, r in enumerate(away)}


def body(
    user_input,
    out_grad,
    hist_len,
    hist_items,
    item_row,
    item_feat,
    user_gain,
    user_gate,
    user_up,
    user_down,
    item_gain,
    item_gate,
    item_up,
    item_down,
):
    n_wide, n_narrow = lax.axis_size("wide"), lax.axis_size("narrow")
    me, here = lax.axis_index("wide"), lax.axis_index("narrow")
    chip, core = me // 2, me % 2
    n_chips = n_wide // 2
    bits = [1 << k for k in range(1, n_wide.bit_length() - 1)]
    order_a = bits
    order_b = bits[len(bits) // 2 :] + bits[: len(bits) // 2]
    user_count, hist_length, width = user_input.shape
    rows = user_count * hist_length
    item_dev = item_feat.shape[0]
    hid = user_gate.shape[1]
    block = width // n_wide
    rels = jnp.arange(n_chips, dtype=jnp.int32)
    place = jnp.stack([chip, core, me])

    def near(value):
        return [value] + [swap(value, r << 1) for r in range(1, n_chips)]

    def gather_wide(value):
        pieces = near(value)
        return pieces + [swap(piece, 1) for piece in pieces]

    feats = gather_wide(item_feat)

    normed, masked, hidden, d_gate, d_up, sent, kept = user_layer(
        place,
        hist_len,
        user_input.reshape(rows, width),
        out_grad.reshape(rows, width),
        hist_items,
        item_row,
        user_gain,
        user_gate,
        user_up,
        user_down,
        1.0 / n_narrow,
        item_dev,
    )
    sent, *_ = lax.optimization_barrier((sent, feats[1], feats[2 % n_wide]))
    got = swap(sent, 1)
    sent_table = jnp.stack([(chip ^ rels) * 2 + 1 - core])
    grads_sent = sent_grads(sent_table, normed, masked, d_gate, d_up, hidden, block)
    got, grads_sent = lax.optimization_barrier((got, grads_sent))
    grads_got = swap(grads_sent, 1)
    sums = []
    for r in range(n_chips):
        at = slice(r * item_dev, (r + 1) * item_dev)
        sums.append(kept[at].astype(F32) + got[at].astype(F32))
    pieces = [swap(sums[r].astype(BF16), r << 1) for r in range(1, n_chips)]

    group = min(8, n_wide)
    forwards = [
        item_forward(place, item_gain, feats[k : k + group], item_gate, item_up, block)
        for k in range(0, n_wide, group)
    ]

    kept_table, places = grad_tables(n_chips, chip, core, order_a, order_b)
    grads_got, _ = lax.optimization_barrier((grads_got, forwards[-1][0]))
    sent_a, kept_a, sent_b, kept_b = kept_grads(
        kept_table, normed, masked, d_gate, d_up, hidden, grads_got, block
    )
    pieces[0], sent_a, sent_b = lax.optimization_barrier((pieces[0], sent_a, sent_b))
    mine = functools.reduce(jnp.add, [p.astype(F32) for p in pieces], sums[0]).astype(BF16)
    sent_a, sent_b, mine = lax.optimization_barrier((sent_a, sent_b, mine))

    got_a, got_b = swap(sent_a, order_a[0]), swap(sent_b, order_b[0])

    quarter = item_dev // n_narrow

    def narrow_scatter(value):
        parts = lax.all_to_all(
            value.reshape(n_narrow, quarter, width), "narrow", split_axis=0, concat_axis=0, tiled=True
        )
        return jnp.sum(parts.astype(F32), axis=0)

    def narrow_slots(piece):
        return [piece] + [
            lax.ppermute(piece, "narrow", [(i, i ^ k) for i in range(n_narrow)])
            for k in range(1, n_narrow)
        ]

    def narrow_gather(piece):
        return place_rows(here, narrow_slots(piece))

    item_in = narrow_scatter(mine)
    item_cot = narrow_gather(item_in.astype(BF16))
    cots = near(item_cot)
    item_part = item_own(
        item_cot, forwards[0][2], forwards[0][3], item_gate, item_up, item_down
    )
    item_dn = narrow_scatter(item_part)

    got_a, got_b, _ = lax.optimization_barrier((got_a, got_b, item_part))
    total_a = first_sums(got_a, kept_a, places["a"])
    total_b = first_sums(got_b, kept_b, places["b"])
    for a, b in zip(order_a[1:], order_b[1:]):
        away_a, away_b = sent_away(total_a, a), sent_away(total_b, b)
        away_a, away_b, cots[-1] = lax.optimization_barrier((away_a, away_b, cots[-1]))
        got_a, got_b = swap(away_a, a), swap(away_b, b)
        if a != order_a[-1]:
            total_a, total_b = next_sums(total_a, got_a, a), next_sums(total_b, got_b, b)
    cots = cots + [swap(piece, 1) for piece in cots]

    item_scaled = item_gain.astype(F32)[None, :] * item_dn
    own = lax.dynamic_slice_in_dim(item_feat, here * quarter, quarter, axis=0).astype(F32)
    own_inv = lax.rsqrt(jnp.mean(own * own, axis=1, keepdims=True) + 1e-05)
    own_unit = own * own_inv
    item_mean = jnp.mean(item_scaled * own_unit, axis=1, keepdims=True)
    feat_rows = (item_in + own_inv * (item_scaled - own_unit * item_mean)).astype(BF16)
    feat_slots = narrow_slots(feat_rows)

    item_grads = None
    for k, (normed_k, hidden_k, slope_up_k, slope_gate_k) in enumerate(forwards):
        parts = cots[k * group : (k + 1) * group]
        column = parts[0]
        if block % 128:
            normed_k = lax.dynamic_slice_in_dim(normed_k, me * block, block, axis=1)
            column = jnp.concatenate(
                [lax.dynamic_slice_in_dim(p, me * block, block, axis=1) for p in parts], axis=0
            )
        found = item_late(
            place, parts, column, normed_k, hidden_k, slope_up_k, slope_gate_k, item_down, 1.0 / n_wide
        )
        item_grads = list(found) if item_grads is None else [a + b for a, b in zip(item_grads, found)]

    got_a, got_b, item_grads[0], *feat_slots = lax.optimization_barrier(
        (got_a, got_b, item_grads[0], *feat_slots)
    )
    feat_grad = place_rows(here, feat_slots)
    if len(order_a) > 1:
        total_a, total_b = next_sums(total_a, got_a, order_a[-1]), next_sums(total_b, got_b, order_b[-1])
    user_grads = jnp.concatenate([total_a[0], total_b[0]], axis=0) * (1.0 / n_wide)
    return (
        feat_grad,
        user_grads[:, :hid],
        user_grads[:, hid : 2 * hid],
        user_grads[:, 2 * hid :].T,
        *item_grads,
    )


def solution(mesh):
    placed = (
        P("wide", None, None),
        P("wide", None, None),
        P("wide"),
        P("wide", None),
        P(),
        P("wide", None),
        P(),
        P(None, "narrow"),
        P(None, "narrow"),
        P("narrow", None),
        P(),
        P(None, "narrow"),
        P(None, "narrow"),
        P("narrow", None),
    )
    return jax.shard_map(
        body,
        mesh=mesh,
        in_specs=placed,
        out_specs=(
            P("wide", None),
            P("wide", "narrow"),
            P("wide", "narrow"),
            P("narrow", "wide"),
            P("wide", "narrow"),
            P("wide", "narrow"),
            P("narrow", "wide"),
        ),
        check_vma=False,
    )
```

time: 220 us -> 173 us (0.79)
  blocking collectives: 30.8 us -> 0 us
  local copies, waits for them, and re-layouts: 20.3 us -> 4.48 us
  starting transfers between devices: 26.1 us -> 33.7 us
  waiting for transfers between devices: 46.6 us -> 42.5 us
  Pallas kernels: 80.9 us -> 77.2 us
    all_gather x2 -> x0, blocking collectives: 30.8 us -> none  [narrow_gather(): return lax.all_gather(piece, 'narrow', axis=0, tiled=True)]
    ppermute x17 -> x23, waiting for transfers between devices: 45.4 us -> 15.8 us  [swap(): return lax.ppermute(value, 'wide', [(i, i ^ bit) for i in range(count)])]
    all_to_all x2, waiting for transfers between devices: 1.18 us -> 18.7 us  [narrow_scatter(): lax.all_to_all(value.reshape(n_narrow, quarter, width), 'narrow', split_a...]
    ppermute x0 -> x6, starting transfers between devices: none -> 8.88 us  [narrow_slots(): lax.ppermute(piece, 'narrow', [(i, i ^ k) for i in range(n_narrow)])]
    ppermute x0 -> x6, waiting for transfers between devices: none -> 8.11 us  [narrow_slots(): lax.ppermute(piece, 'narrow', [(i, i ^ k) for i in range(n_narrow)])]
    unnamed x40 -> x59, local copies, waits for them, and re-layouts: 7.81 us -> 2.48 us
    convert_element_type x6 -> x5, other arithmetic: 4.75 us -> 9.59 us  [the longest x2 4.1 us: sent_away(): return jnp.stack([total[r].astype(BF16) for r in away])]
    pallas_call x5 -> x6, Pallas kernels: 63.7 us -> 60 us  [the longest x1 19.2 us: user_layer(): pl.pallas_call(functools.partial(user_kernel, share, item_dev), in_specs=...]
  transfers between devices with their start and end apart: 19 -> 31, of which waited for: 9 -> 7; matrix products, arithmetic and copies ran while one was open for 10% -> 5% of each run, Pallas kernels for 25% -> 44%
where the time goes in v2:
time: 173 us
  Pallas kernels  77.2 us (45%)
  waiting for transfers between devices  42.5 us (25%)
  starting transfers between devices  33.7 us (19%)
  other arithmetic  13.5 us (8%)
  local copies, waits for them, and re-layouts  4.48 us (3%)
    pallas_call x1, Pallas kernels, user_layer(): pl.pallas_call(functools.partial(user_kernel, share, item_dev), in_specs=...  19.2 us
    all_to_all x2, waiting for transfers between devices, narrow_scatter(): lax.all_to_all(value.reshape(n_narrow, quarter, width), 'narrow', split_a...  18.7 us
    ppermute x23, starting transfers between devices, swap(): return lax.ppermute(value, 'wide', [(i, i ^ bit) for i in range(count)])  16.5 us
    ppermute x23, waiting for transfers between devices, swap(): return lax.ppermute(value, 'wide', [(i, i ^ bit) for i in range(count)])  15.8 us
    pallas_call x1, Pallas kernels, item_forward(): pl.pallas_call(functools.partial(forward_kernel, count), in_specs=[smem()...  14.5 us
    pallas_call x1, Pallas kernels, item_late(): pl.pallas_call(functools.partial(late_kernel, count, scale), in_specs=[sm...  14.5 us
    pallas_call x1, Pallas kernels, kept_grads(): pl.pallas_call(kept_kernel, grid_spec=pltpu.PrefetchScalarGridSpec(num_sc...  9.6 us
    ppermute x6, starting transfers between devices, narrow_slots(): lax.ppermute(piece, 'narrow', [(i, i ^ k) for i in range(n_narrow)])  8.88 us
  transfers between devices with their start and end apart: 31, of which 7 were waited for; matrix products, arithmetic and copies ran while one was open for 5% of the time, Pallas kernels for 44%

profile of v2, /device:TPU:0, one launch (start us, length us, event | category | flops | bytes accessed | tf_op | source)
XLA Modules:
  0.0 172.6 jit_solution(7689426655351677626)
XLA Ops:
  0.6 3.0 %collective-permute-start = (bf16[128,2048]{1,0:T(8,128)(2,1)}, bf16[128,2048]{1,0:T(8,128)(2,1)S(1)}, u32[]{:S(2)}, u32[]{:S(2)}) collective-permute-start(bf16[128,2048]{1,0:T(8,128)(2,1)} %refs_0_.1), channel_id=1, source_target_pairs={{0,8},{4,12},{8,0},{12,4},{16,24},{20,28},{24,16},{28,20},{1,9},{5... | collective-permute-start | bytes 1572872 | tf_op jit(solution)/shard_map/ppermute | solution.py:48
  3.6 1.5 collective-permute-start.1
  5.2 0.6 pad_add_fusion.place_ref
  5.7 19.2 %user_layer.1 = (bf16[512,2048]{1,0:T(8,128)(2,1)}, bf16[512,2048]{1,0:T(8,128)(2,1)}, bf16[512,768]{1,0:T(8,128)(2,1)}, bf16[512,768]{1,0:T(8,128)(2,1)}, bf16[...) custom-call(s32[3]{0:T(128)} %pad_add_fusion.place_ref, s32[8]{0:T(128)} %hist_len_ref.1, ...), custom_call_target="tpu_custom_call" | custom-call | flops 1342177280 | bytes 4000000 | tf_op jit(solution)/shard_map/user_layer/pallas_call | solution.py:172
  25.0 0.1 collective-permute-start.2
  25.1 0.6 add_subtract_fusion.table_ref
  25.7 7.6 %sent_grads.1 = bf16[4,256,2304]{2,1,0:T(8,128)(2,1)} custom-call(s32[1,4]{1,0:T(1,128)} %add_subtract_fusion.table_ref, bf16[512,2048]{1,0:T(8,128)(2,1)} %get-tuple-element.47.normed_ref, bf16[512,2048]{1,0:T(8,128)(2,1)} %get-tuple-element.48.masked_ref, bf16[512,768]{1,0:T(8,128)(2,1)} %get-tuple-element.49.d_gate_ref, ...), custom_call_target="tpu_custom_call" | custom-call | flops 402653184 | bytes 1666666 | tf_op jit(solution)/shard_map/sent_grads/pallas_call | solution.py:260
  33.3 0.4 collective-permute-start.3
  33.7 0.0 collective-permute-start.4
  33.7 0.1 collective-permute-start.5
  33.9 0.4 collective-permute-start.6
  34.2 0.1 collective-permute-start.7
  34.4 14.3 %collective-permute-done.4.refs_3_ = bf16[128,2048]{1,0:T(8,128)(2,1)} collective-permute-done((bf16[128,2048]{1,0:T(8,128)(2,1)S(1)}, bf16[128,2048]{1,0:T(8,128)(2,1)}, u32[]{:S(2)}, u32[]{:S(2)}) %collective-permute-start.4) | collective-permute-done | bytes 524320 | tf_op jit(solution)/shard_map/ppermute | solution.py:48
  48.7 0.0 copy-start.22
  48.8 2.9 %add_convert_fusion.4 = (bf16[128,2048]{1,0:T(8,128)(2,1)}, bf16[128,2048]{1,0:T(8,128)(2,1)}, bf16[128,2048]{1,0:T(8,128)(2,1)}) fusion(bf16[512,2048]{1,0:T(8,128)(2,1)} %collective-permute-done.2, bf16[512,2048]{1,0:T(8,128)(2,1)S(1)} %copy-done.1), kind=kLoop, calls=%fused_computation.9 | loop fusion | flops 3145728 | bytes 4718592 | tf_op jit(solution)/shard_map/convert_element_type | solution.py:653
  51.6 0.5 collective-permute-start.9
  52.2 0.3 collective-permute-start.10
  52.5 0.5 copy-done.11
  53.0 2.2 %collective-permute-start.11 = (bf16[128,2048]{1,0:T(8,128)(2,1)}, bf16[128,2048]{1,0:T(8,128)(2,1)S(1)}, u32[]{:S(2)}, u32[]{:S(2)}) collective-permute-start(bf16[128,2048]{1,0:T(8,128)(2,1)} %get-tuple-element.95), channel_id=1, source_target_pairs={{0,24},{4,28},{8,16},{12,20},{16,8},{20,12},{24,0},{28,4},{1,25},{... | collective-permute-start | bytes 1572872 | tf_op jit(solution)/shard_map/ppermute | solution.py:48
  55.3 0.6 stack.50.table_ref
  55.9 14.5 %item_forward.1 = (bf16[1024,256]{1,0:T(8,128)(2,1)}, bf16[1024,768]{1,0:T(8,128)(2,1)}, bf16[1024,768]{1,0:T(8,128)(2,1)}, bf16[1024,768]{1,0:T(8,128)(2,1)}) custom-call(s32[3]{0:T(128)} %pad_add_fusion.place_ref, bf16[2048]{0:T(1024)(128)(2,1)} %gain_ref.3, bf16[128,2048]{1,0:T(8,128)(2,1)} %refs_0_.1, bf16[128,2048]{1,0:T(8,128)(2,1)} %copy-done.7, ...), custom_call_target="tpu_custom_call" | custom-call | flops 1073741824 | bytes 2666666 | tf_op jit(solution)/shard_map/item_forward/pallas_call | solution.py:370
  70.4 9.6 %kept_grads.1 = (bf16[2,128,2304]{2,1,0:T(8,128)(2,1)}, bf16[2,128,2304]{2,1,0:T(8,128)(2,1)}, bf16[2,128,2304]{2,1,0:T(8,128)(2,1)}, bf16[2,128,2304]{2,1,0:T(8,128)(2,1)}) custom-call(s32[8,4]{1,0:T(8,128)} %stack.50.table_ref, bf16[512,2048]{1,0:T(8,128)(2,1)} %get-tuple-element.47.normed_ref, bf16[512,2048]{1,0:T(8,128)(2,1)} %get-tuple-element.48.masked_ref, ...), custom_call_target="tpu_custom_call" | custom-call | flops 402653184 | bytes 2500000 | tf_op jit(solution)/shard_map/kept_grads/pallas_call | solution.py:283
  80.1 2.6 %add_convert_fusion.2 = bf16[128,2048]{1,0:T(8,128)(2,1)} fusion(bf16[128,2048]{1,0:T(8,128)(2,1)S(1)} %collective-permute-done.11, bf16[128,2048]{1,0:T(8,128)(2,1)} %collective-permute-done.10, bf16[128,2048]{1,0:T(8,128)(2,1)} %collective-permute-done.9, bf16[512,2048]{1,0:T(8,128)(2,1)} %collective-permute-done.2, bf16[512,2048]{1,0:T(8,128)(2,1)S(1)} %copy-done.1), kind=kLoop, calls=%fused_computation.7 | loop fusion | flops 2621440 | bytes 3145728 | tf_op jit(solution)/shard_map/convert_element_type | solution.py:667
  82.7 0.5 collective-permute-start.12
  83.2 0.8 collective-permute-start.13
  84.0 4.9 %all-to-all-start = ((bf16[4,32,2048]{2,1,0:T(8,128)(2,1)}), bf16[4,32,2048]{2,1,0:T(8,128)(2,1)S(1)}, u32[]{:S(2)}, u32[]{:S(2)}) async-start(bf16[4,32,2048]{2,1,0:T(8,128)(2,1)} %bitcast.7), calls=%async_computation | async-start | bytes 1048576 | tf_op jit(solution)/shard_map/all_to_all | solution.py:675
  88.9 0.1 fusion.7
  89.1 13.9 %all-to-all-done = bf16[4,32,2048]{2,1,0:T(8,128)(2,1)S(1)} async-done(((bf16[4,32,2048]{2,1,0:T(8,128)(2,1)}), bf16[4,32,2048]{2,1,0:T(8,128)(2,1)S(1)}, u32[]{:S(2)}, u32[]{:S(2)}) %all-to-all-start) | async-done | bytes 524320 | tf_op jit(solution)/shard_map/all_to_all | solution.py:675
  102.9 0.1 convert_reduce_fusion.1
  103.0 0.1 collective-permute-start.14
  103.1 2.0 %collective-permute-start.15 = (bf16[32,2048]{1,0:T(8,128)(2,1)S(1)}, bf16[32,2048]{1,0:T(8,128)(2,1)S(1)}, u32[]{:S(2)}, u32[]{:S(2)}) collective-permute-start(bf16[32,2048]{1,0:T(8,128)(2,1)S(1)} %convert_element_type.128.refs_0_), channel_id=1, source_target_pairs={{0,2},{1,3},{2,0},{3,1},{4,6},{5,7},{6,4},{7,5},{8,10},{9,11},{10,... | collective-permute-start | bytes 393224 | tf_op jit(solution)/shard_map/ppermute | solution.py:682
  105.1 2.4 %collective-permute-start.16 = (bf16[32,2048]{1,0:T(8,128)(2,1)S(1)}, bf16[32,2048]{1,0:T(8,128)(2,1)S(1)}, u32[]{:S(2)}, u32[]{:S(2)}) collective-permute-start(bf16[32,2048]{1,0:T(8,128)(2,1)S(1)} %convert_element_type.128.refs_0_), channel_id=1, source_target_pairs={{0,3},{1,2},{2,1},{3,0},{4,7},{5,6},{6,5},{7,4},{8,11},{9,10},{10,... | collective-permute-start | bytes 393224 | tf_op jit(solution)/shard_map/ppermute | solution.py:682
  107.5 1.9 %collective-permute-done.14.refs_1_ = bf16[32,2048]{1,0:T(8,128)(2,1)S(1)} collective-permute-done((bf16[32,2048]{1,0:T(8,128)(2,1)S(1)}, bf16[32,2048]{1,0:T(8,128)(2,1)S(1)}, u32[]{:S(2)}, u32[]{:S(2)}) %collective-permute-start.14) | collective-permute-done | bytes 131104 | tf_op jit(solution)/shard_map/ppermute | solution.py:682
  109.4 6.2 %collective-permute-done.15.refs_2_ = bf16[32,2048]{1,0:T(8,128)(2,1)S(1)} collective-permute-done((bf16[32,2048]{1,0:T(8,128)(2,1)S(1)}, bf16[32,2048]{1,0:T(8,128)(2,1)S(1)}, u32[]{:S(2)}, u32[]{:S(2)}) %collective-permute-start.15) | collective-permute-done | bytes 131104 | tf_op jit(solution)/shard_map/ppermute | solution.py:682
  115.6 0.6 copy-done.19
  116.3 0.0 copy-done.20
  116.3 1.9 %place_rows.2.cot.refs_0_.refs_8_ = bf16[128,2048]{1,0:T(8,128)(2,1)} custom-call(s32[1]{0:T(128)} %bitcast.here_ref, bf16[32,2048]{1,0:T(8,128)(2,1)} %copy-done.13, bf16[32,2048]{1,0:T(8,128)(2,1)} %copy-done.18, bf16[32,2048]{1,0:T(8,128)(2,1)} %copy-done.19, bf16[32,2048]{1,0:T(8,128)(2,1)} %copy-done.20), custom_call_target="tpu_custom_call" | custom-call | bytes 174762 | tf_op jit(solution)/shard_map/place_rows/pallas_call | solution.py:539
  118.2 1.9 %collective-permute-start.17 = (bf16[128,2048]{1,0:T(8,128)(2,1)}, bf16[128,2048]{1,0:T(8,128)(2,1)S(1)}, u32[]{:S(2)}, u32[]{:S(2)}) collective-permute-start(bf16[128,2048]{1,0:T(8,128)(2,1)} %place_rows.2.cot.refs_0_.refs_8_), channel_id=1, source_target_pairs={{0,24},{4,28},{8,16},{12,20},{16,8},{20,12},{24,0},{28,4},{1,25},{... | collective-permute-start | bytes 1572872 | tf_op jit(solution)/shard_map/ppermute | solution.py:48
  120.1 0.5 collective-permute-start.20
  120.6 1.1 collective-permute-start.21
  121.7 8.0 %item_own.1 = bf16[128,2048]{1,0:T(8,128)(2,1)} custom-call(bf16[128,2048]{1,0:T(8,128)(2,1)} %place_rows.2.cot.refs_0_.refs_8_, bf16[1024,768]{1,0:T(8,128)(2,1)} %get-tuple-element.68.slope_up.refs_11_, bf16[1024,768]{1,0:T(8,128)(2,1)} %get-tuple-element.69.slope_gate.refs_12_, bf16[2048,768]{1,0:T(8,128)(2,1)} %gate_hbm.3, bf16[2048,768]{1,0:T(8,128)(2,1)} %up_hbm.3, ...), custom_call_target="tpu_custom_call" | custom-call | flops 201326592 | bytes 1833333 | tf_op jit(solution)/shard_map/item_own/pallas_call | solution.py:414
  129.7 3.5 %all-to-all-start.1 = ((bf16[4,32,2048]{2,1,0:T(8,128)(2,1)}), bf16[4,32,2048]{2,1,0:T(8,128)(2,1)S(1)}, u32[]{:S(2)}, u32[]{:S(2)}) async-start(bf16[4,32,2048]{2,1,0:T(8,128)(2,1)} %bitcast.18), calls=%async_computation.1 | async-start | bytes 1048576 | tf_op jit(solution)/shard_map/all_to_all | solution.py:675
  133.3 0.1 collective-permute-start.22
  133.4 2.1 %add_convert_fusion = bf16[1,128,2304]{2,1,0:T(8,128)(2,1)} fusion(bf16[2,128,2304]{2,1,0:T(8,128)(2,1)} %collective-permute-done.13, bf16[2,128,2304]{2,1,0:T(8,128)(2,1)S(1)} %copy-done.6), kind=kLoop, calls=%fused_computation.3 | loop fusion | flops 1179648 | bytes 1769472 | tf_op jit(solution)/shard_map/convert_element_type | solution.py:581
  135.5 2.0 %add_convert_fusion.1 = bf16[1,128,2304]{2,1,0:T(8,128)(2,1)} fusion(bf16[2,128,2304]{2,1,0:T(8,128)(2,1)} %collective-permute-done.12, bf16[2,128,2304]{2,1,0:T(8,128)(2,1)S(1)} %copy-done.4), kind=kLoop, calls=%fused_computation.4 | loop fusion | flops 1179648 | bytes 1769472 | tf_op jit(solution)/shard_map/convert_element_type | solution.py:581
  137.5 0.4 collective-permute-start.25
  137.9 0.9 collective-permute-start.18
  138.8 0.9 collective-permute-done.20.refs_1_
  139.8 0.5 collective-permute-done.21.refs_2_
  140.2 0.0 collective-permute-start.24
  140.3 4.8 %all-to-all-done.1 = bf16[4,32,2048]{2,1,0:T(8,128)(2,1)S(1)} async-done(((bf16[4,32,2048]{2,1,0:T(8,128)(2,1)}), bf16[4,32,2048]{2,1,0:T(8,128)(2,1)S(1)}, u32[]{:S(2)}, u32[]{:S(2)}) %all-to-all-start.1) | async-done | bytes 524320 | tf_op jit(solution)/shard_map/all_to_all | solution.py:675
  145.1 0.1 convert_reduce_fusion
  145.1 0.2 fusion.2
  145.4 1.5 collective-permute-start.19
  146.9 0.1 fusion.6.refs_0_
  147.0 0.1 collective-permute-start.26
  147.1 2.7 %collective-permute-start.27 = (bf16[32,2048]{1,0:T(8,128)(2,1)S(1)}, bf16[32,2048]{1,0:T(8,128)(2,1)S(1)}, u32[]{:S(2)}, u32[]{:S(2)}) collective-permute-start(bf16[32,2048]{1,0:T(8,128)(2,1)S(1)} %fusion.6.refs_0_), channel_id=1, source_target_pairs={{0,2},{1,3},{2,0},{3,1},{4,6},{5,7},{6,4},{7,5},{8,10},{9,11},{10,... | collective-permute-start | bytes 393224 | tf_op jit(solution)/shard_map/ppermute | solution.py:682
  149.9 1.6 collective-permute-start.28
  151.5 14.5 %item_late.1 = (f32[256,768]{1,0:T(8,128)}, f32[256,768]{1,0:T(8,128)}, f32[768,256]{1,0:T(8,128)}) custom-call(s32[3]{0:T(128)} %pad_add_fusion.place_ref, bf16[128,2048]{1,0:T(8,128)(2,1)} %place_rows.2.cot.refs_0_.refs_8_, bf16[128,2048]{1,0:T(8,128)(2,1)} %collective-permute-done.20.refs_1_, bf16[128,2048]{1,0:T(8,128)(2,1)} %collective-permute-done.21.refs_2_, ...), custom_call_target="tpu_custom_call" | custom-call | flops 1476395008 | bytes 2666666 | tf_op jit(solution)/shard_map/item_late/pallas_call | solution.py:504
  166.1 1.9 %add_bitcast_fusion = (f32[128,2304]{1,0:T(8,128)S(1)}, f32[128,2304]{1,0:T(8,128)S(1)}) fusion(bf16[1,128,2304]{2,1,0:T(8,128)(2,1)S(1)} %collective-permute-done.19, bf16[2,128,2304]{2,1,0:T(8,128)(2,1)} %collective-permute-done.13, bf16[2,128,2304]{2,1,0:T(8,128)(2,1)S(1)} %copy-done.6, bf16[1,128,2304]{2,1,0:T(8,128)(2,1)} %collective-permute-done.18, ...), kind=kLoop, calls=%fused_computation.1 | loop fusion | flops 2949120 | bytes 5898240 | tf_op jit(solution)/shard_map/add | solution.py:586
  168.0 0.2 maximum_multiply_fusion
  168.2 1.4 slice_bitcast_fusion
  169.6 1.1 copy.28
  170.7 1.9 %place_rows.3 = bf16[128,2048]{1,0:T(8,128)(2,1)} custom-call(s32[1]{0:T(128)} %bitcast.here_ref, bf16[32,2048]{1,0:T(8,128)(2,1)} %copy-done.14, bf16[32,2048]{1,0:T(8,128)(2,1)} %copy-done.15, bf16[32,2048]{1,0:T(8,128)(2,1)} %copy-done.16, bf16[32,2048]{1,0:T(8,128)(2,1)} %copy-done.17), custom_call_target="tpu_custom_call" | custom-call | bytes 174762 | tf_op jit(solution)/shard_map/place_rows/pallas_call | solution.py:539
  (85 shorter events, 0.2 us)
Async XLA Ops:
  0.6 24.3 %collective-permute-start = (bf16[128,2048]{1,0:T(8,128)(2,1)}, bf16[128,2048]{1,0:T(8,128)(2,1)S(1)}, u32[]{:S(2)}, u32[]{:S(2)}) collective-permute-start(bf16[128,2048]{1,0:T(8,128)(2,1)} %refs_0_.1), channel_id=1, source_target_pairs={{0,8},{4,12},{8,0},{12,4},{16,24},{20,28},{24,16},{28,20},{1,9},{5... | collective-permute-start | bytes 1572872 | tf_op jit(solution)/shard_map/ppermute | solution.py:48
  3.6 21.3 %collective-permute-start.1 = (bf16[128,2048]{1,0:T(8,128)(2,1)}, bf16[128,2048]{1,0:T(8,128)(2,1)S(1)}, u32[]{:S(2)}, u32[]{:S(2)}) collective-permute-start(bf16[128,2048]{1,0:T(8,128)(2,1)} %refs_0_.1), channel_id=1, source_target_pairs={{0,16},{4,20},{8,24},{12,28},{16,0},{20,4},{24,8},{28,12},{1,17},{... | collective-permute-start | bytes 1572872 | tf_op jit(solution)/shard_map/ppermute | solution.py:48
  25.0 8.9 %copy-start.7 = (bf16[128,2048]{1,0:T(8,128)(2,1)}, bf16[128,2048]{1,0:T(8,128)(2,1)S(1)}, u32[]{:S(2)}) copy-start(bf16[128,2048]{1,0:T(8,128)(2,1)S(1)} %collective-permute-done.refs_1_) | copy-start | bytes 1572868
  25.0 9.3 %copy-start.8 = (bf16[128,2048]{1,0:T(8,128)(2,1)}, bf16[128,2048]{1,0:T(8,128)(2,1)S(1)}, u32[]{:S(2)}) copy-start(bf16[128,2048]{1,0:T(8,128)(2,1)S(1)} %collective-permute-done.1.refs_2_) | copy-start | bytes 1572868
  25.0 8.3 %collective-permute-start.2 = (bf16[512,2048]{1,0:T(8,128)(2,1)}, bf16[512,2048]{1,0:T(8,128)(2,1)}, u32[]{:S(2)}, u32[]{:S(2)}) collective-permute-start(bf16[512,2048]{1,0:T(8,128)(2,1)} %get-tuple-element.53), channel_id=1, source_target_pairs={{0,4},{4,0},{8,12},{12,8},{16,20},{20,16},{24,28},{28,24},{1,5},{5... | collective-permute-start | bytes 6291464 | tf_op jit(solution)/shard_map/ppermute | solution.py:48
  25.7 8.0 %copy-start.2 = (bf16[128,2048]{1,0:T(8,128)(2,1)S(1)}, bf16[128,2048]{1,0:T(8,128)(2,1)}, u32[]{:S(2)}) copy-start(bf16[128,2048]{1,0:T(8,128)(2,1)} %refs_0_.1) | copy-start | bytes 1572868
  25.7 23.0 %copy-start.1 = (bf16[512,2048]{1,0:T(8,128)(2,1)S(1)}, bf16[512,2048]{1,0:T(8,128)(2,1)}, u32[]{:S(2)}) copy-start(bf16[512,2048]{1,0:T(8,128)(2,1)} %get-tuple-element.58) | copy-start | bytes 6291460
  33.3 37.1 %collective-permute-start.3 = (bf16[4,256,2304]{2,1,0:T(8,128)(2,1)}, bf16[4,256,2304]{2,1,0:T(8,128)(2,1)}, u32[]{:S(2)}, u32[]{:S(2)}) collective-permute-start(bf16[4,256,2304]{2,1,0:T(8,128)(2,1)} %sent_grads.1), channel_id=1, source_target_pairs={{0,4},{4,0},{8,12},{12,8},{16,20},{20,16},{24,28},{28,24},{1,5},{5... | collective-permute-start | bytes 14155784 | tf_op jit(solution)/shard_map/ppermute | solution.py:48
  33.7 15.0 %collective-permute-start.4 = (bf16[128,2048]{1,0:T(8,128)(2,1)S(1)}, bf16[128,2048]{1,0:T(8,128)(2,1)}, u32[]{:S(2)}, u32[]{:S(2)}) collective-permute-start(bf16[128,2048]{1,0:T(8,128)(2,1)S(1)} %copy-done.2), channel_id=1, source_target_pairs={{0,24},{4,28},{8,16},{12,20},{16,8},{20,12},{24,0},{28,4},{1,25},{... | collective-permute-start | bytes 1572872 | tf_op jit(solution)/shard_map/ppermute | solution.py:48
  33.7 17.9 %collective-permute-start.5 = (bf16[128,2048]{1,0:T(8,128)(2,1)S(1)}, bf16[128,2048]{1,0:T(8,128)(2,1)S(1)}, u32[]{:S(2)}, u32[]{:S(2)}) collective-permute-start(bf16[128,2048]{1,0:T(8,128)(2,1)S(1)} %copy-done.2), channel_id=1, source_target_pairs={{0,4},{4,0},{8,12},{12,8},{16,20},{20,16},{24,28},{28,24},{1,5},{5... | collective-permute-start | bytes 1572872 | tf_op jit(solution)/shard_map/ppermute | solution.py:48
  33.9 18.3 %collective-permute-start.6 = (bf16[128,2048]{1,0:T(8,128)(2,1)S(1)}, bf16[128,2048]{1,0:T(8,128)(2,1)S(1)}, u32[]{:S(2)}, u32[]{:S(2)}) collective-permute-start(bf16[128,2048]{1,0:T(8,128)(2,1)S(1)} %collective-permute-done.refs_1_), channel_id=1, source_target_pairs={{0,4},{4,0},{8,12},{12,8},{16,20},{20,16},{24,28},{28,24},{1,5},{5... | collective-permute-start | bytes 1572872 | tf_op jit(solution)/shard_map/ppermute | solution.py:48
  34.2 18.2 %collective-permute-start.7 = (bf16[128,2048]{1,0:T(8,128)(2,1)S(1)}, bf16[128,2048]{1,0:T(8,128)(2,1)S(1)}, u32[]{:S(2)}, u32[]{:S(2)}) collective-permute-start(bf16[128,2048]{1,0:T(8,128)(2,1)S(1)} %collective-permute-done.1.refs_2_), channel_id=1, source_target_pairs={{0,4},{4,0},{8,12},{12,8},{16,20},{20,16},{24,28},{28,24},{1,5},{5... | collective-permute-start | bytes 1572872 | tf_op jit(solution)/shard_map/ppermute | solution.py:48
  48.7 7.2 %collective-permute-start.8 = (bf16[128,2048]{1,0:T(8,128)(2,1)}, bf16[128,2048]{1,0:T(8,128)(2,1)}, u32[]{:S(2)}, u32[]{:S(2)}) collective-permute-start(bf16[128,2048]{1,0:T(8,128)(2,1)} %collective-permute-done.4.refs_3_), channel_id=1, source_target_pairs={{0,4},{4,0},{8,12},{12,8},{16,20},{20,16},{24,28},{28,24},{1,5},{5... | collective-permute-start | bytes 1572872 | tf_op jit(solution)/shard_map/ppermute | solution.py:48
  48.7 6.5 %copy-start.28 = (s32[4]{0:T(128)S(1)}, s32[4]{0:T(128)}, u32[]{:S(2)}) copy-start(s32[4]{0:T(128)} %constant.62.clone) | copy-start | bytes 52
  48.7 6.5 %copy-start.22 = (s32[1,4]{1,0:T(1,128)S(1)}, s32[1,4]{1,0:T(1,128)}, u32[]{:S(2)}) copy-start(s32[1,4]{1,0:T(1,128)} %constant.69) | copy-start | bytes 52
  48.7 6.5 %copy-start.23 = (s32[1,4]{1,0:T(1,128)S(1)}, s32[1,4]{1,0:T(1,128)}, u32[]{:S(2)}) copy-start(s32[1,4]{1,0:T(1,128)} %constant.68) | copy-start | bytes 52
  48.7 6.5 %copy-start.24 = (s32[1,4]{1,0:T(1,128)S(1)}, s32[1,4]{1,0:T(1,128)}, u32[]{:S(2)}) copy-start(s32[1,4]{1,0:T(1,128)} %constant.70) | copy-start | bytes 52
  48.7 6.5 %copy-start.25 = (s32[1,4]{1,0:T(1,128)S(1)}, s32[1,4]{1,0:T(1,128)}, u32[]{:S(2)}) copy-start(s32[1,4]{1,0:T(1,128)} %constant.71) | copy-start | bytes 52
  48.7 6.5 %copy-start.26 = (s32[1,4]{1,0:T(1,128)S(1)}, s32[1,4]{1,0:T(1,128)}, u32[]{:S(2)}) copy-start(s32[1,4]{1,0:T(1,128)} %constant.72) | copy-start | bytes 52
  48.7 6.5 %copy-start.27 = (s32[1,4]{1,0:T(1,128)S(1)}, s32[1,4]{1,0:T(1,128)}, u32[]{:S(2)}) copy-start(s32[1,4]{1,0:T(1,128)} %constant.73) | copy-start | bytes 52
  51.6 0.9 copy-start.10
  51.6 28.4 %collective-permute-start.9 = (bf16[128,2048]{1,0:T(8,128)(2,1)}, bf16[128,2048]{1,0:T(8,128)(2,1)}, u32[]{:S(2)}, u32[]{:S(2)}) collective-permute-start(bf16[128,2048]{1,0:T(8,128)(2,1)} %get-tuple-element.96), channel_id=1, source_target_pairs={{0,8},{4,12},{8,0},{12,4},{16,24},{20,28},{24,16},{28,20},{1,9},{5... | collective-permute-start | bytes 1572872 | tf_op jit(solution)/shard_map/ppermute | solution.py:48
  52.2 0.9 copy-start.11
  52.2 27.9 %collective-permute-start.10 = (bf16[128,2048]{1,0:T(8,128)(2,1)}, bf16[128,2048]{1,0:T(8,128)(2,1)}, u32[]{:S(2)}, u32[]{:S(2)}) collective-permute-start(bf16[128,2048]{1,0:T(8,128)(2,1)} %get-tuple-element.94), channel_id=1, source_target_pairs={{0,16},{4,20},{8,24},{12,28},{16,0},{20,4},{24,8},{28,12},{1,17},{... | collective-permute-start | bytes 1572872 | tf_op jit(solution)/shard_map/ppermute | solution.py:48
  52.5 2.7 %copy-start.12 = (bf16[128,2048]{1,0:T(8,128)(2,1)}, bf16[128,2048]{1,0:T(8,128)(2,1)S(1)}, u32[]{:S(2)}) copy-start(bf16[128,2048]{1,0:T(8,128)(2,1)S(1)} %collective-permute-done.7.refs_6_) | copy-start | bytes 1572868
  53.0 27.0 %collective-permute-start.11 = (bf16[128,2048]{1,0:T(8,128)(2,1)}, bf16[128,2048]{1,0:T(8,128)(2,1)S(1)}, u32[]{:S(2)}, u32[]{:S(2)}) collective-permute-start(bf16[128,2048]{1,0:T(8,128)(2,1)} %get-tuple-element.95), channel_id=1, source_target_pairs={{0,24},{4,28},{8,16},{12,20},{16,8},{20,12},{24,0},{28,4},{1,25},{... | collective-permute-start | bytes 1572872 | tf_op jit(solution)/shard_map/ppermute | solution.py:48
  80.0 8.9 %copy-start.21 = (bf16[2048]{0:T(1024)(128)(2,1)S(1)}, bf16[2048]{0:T(1024)(128)(2,1)}, u32[]{:S(2)}) copy-start(bf16[2048]{0:T(1024)(128)(2,1)} %gain_ref.3) | copy-start | bytes 12292
  80.0 8.9 %copy-start.3 = (bf16[128,2048]{1,0:T(8,128)(2,1)S(1)}, bf16[128,2048]{1,0:T(8,128)(2,1)}, u32[]{:S(2)}) copy-start(bf16[128,2048]{1,0:T(8,128)(2,1)} %refs_0_.1) | copy-start | bytes 1572868
  82.7 50.6 %collective-permute-start.12 = (bf16[2,128,2304]{2,1,0:T(8,128)(2,1)}, bf16[2,128,2304]{2,1,0:T(8,128)(2,1)}, u32[]{:S(2)}, u32[]{:S(2)}) collective-permute-start(bf16[2,128,2304]{2,1,0:T(8,128)(2,1)} %get-tuple-element.65), channel_id=1, source_target_pairs={{0,8},{4,12},{8,0},{12,4},{16,24},{20,28},{24,16},{28,20},{1,9},{5... | collective-permute-start | bytes 3538952 | tf_op jit(solution)/shard_map/ppermute | solution.py:48
  83.2 50.1 %collective-permute-start.13 = (bf16[2,128,2304]{2,1,0:T(8,128)(2,1)}, bf16[2,128,2304]{2,1,0:T(8,128)(2,1)}, u32[]{:S(2)}, u32[]{:S(2)}) collective-permute-start(bf16[2,128,2304]{2,1,0:T(8,128)(2,1)} %get-tuple-element.66), channel_id=1, source_target_pairs={{0,16},{4,20},{8,24},{12,28},{16,0},{20,4},{24,8},{28,12},{1,17},{... | collective-permute-start | bytes 3538952 | tf_op jit(solution)/shard_map/ppermute | solution.py:48
  84.0 18.9 %all-to-all-start = ((bf16[4,32,2048]{2,1,0:T(8,128)(2,1)}), bf16[4,32,2048]{2,1,0:T(8,128)(2,1)S(1)}, u32[]{:S(2)}, u32[]{:S(2)}) async-start(bf16[4,32,2048]{2,1,0:T(8,128)(2,1)} %bitcast.7), calls=%async_computation | async-start | bytes 1048576 | tf_op jit(solution)/shard_map/all_to_all | solution.py:675
  103.0 12.6 %copy-start.13 = (bf16[32,2048]{1,0:T(8,128)(2,1)}, bf16[32,2048]{1,0:T(8,128)(2,1)S(1)}, u32[]{:S(2)}) copy-start(bf16[32,2048]{1,0:T(8,128)(2,1)S(1)} %convert_element_type.128.refs_0_) | copy-start | bytes 393220
  103.0 6.4 %collective-permute-start.14 = (bf16[32,2048]{1,0:T(8,128)(2,1)S(1)}, bf16[32,2048]{1,0:T(8,128)(2,1)S(1)}, u32[]{:S(2)}, u32[]{:S(2)}) collective-permute-start(bf16[32,2048]{1,0:T(8,128)(2,1)S(1)} %convert_element_type.128.refs_0_), channel_id=1, source_target_pairs={{0,1},{1,0},{2,3},{3,2},{4,5},{5,4},{6,7},{7,6},{8,9},{9,8},{10,11... | collective-permute-start | bytes 393224 | tf_op jit(solution)/shard_map/ppermute | solution.py:682
  103.1 12.5 %collective-permute-start.15 = (bf16[32,2048]{1,0:T(8,128)(2,1)S(1)}, bf16[32,2048]{1,0:T(8,128)(2,1)S(1)}, u32[]{:S(2)}, u32[]{:S(2)}) collective-permute-start(bf16[32,2048]{1,0:T(8,128)(2,1)S(1)} %convert_element_type.128.refs_0_), channel_id=1, source_target_pairs={{0,2},{1,3},{2,0},{3,1},{4,6},{5,7},{6,4},{7,5},{8,10},{9,11},{10,... | collective-permute-start | bytes 393224 | tf_op jit(solution)/shard_map/ppermute | solution.py:682
  105.1 10.5 %collective-permute-start.16 = (bf16[32,2048]{1,0:T(8,128)(2,1)S(1)}, bf16[32,2048]{1,0:T(8,128)(2,1)S(1)}, u32[]{:S(2)}, u32[]{:S(2)}) collective-permute-start(bf16[32,2048]{1,0:T(8,128)(2,1)S(1)} %convert_element_type.128.refs_0_), channel_id=1, source_target_pairs={{0,3},{1,2},{2,1},{3,0},{4,7},{5,6},{6,5},{7,4},{8,11},{9,10},{10,... | collective-permute-start | bytes 393224 | tf_op jit(solution)/shard_map/ppermute | solution.py:682
  109.4 6.2 %copy-start.18 = (bf16[32,2048]{1,0:T(8,128)(2,1)}, bf16[32,2048]{1,0:T(8,128)(2,1)S(1)}, u32[]{:S(2)}) copy-start(bf16[32,2048]{1,0:T(8,128)(2,1)S(1)} %collective-permute-done.14.refs_1_) | copy-start | bytes 393220
  115.6 0.7 copy-start.19
  115.6 0.7 copy-start.20
  118.2 19.2 %collective-permute-start.17 = (bf16[128,2048]{1,0:T(8,128)(2,1)}, bf16[128,2048]{1,0:T(8,128)(2,1)S(1)}, u32[]{:S(2)}, u32[]{:S(2)}) collective-permute-start(bf16[128,2048]{1,0:T(8,128)(2,1)} %place_rows.2.cot.refs_0_.refs_8_), channel_id=1, source_target_pairs={{0,24},{4,28},{8,16},{12,20},{16,8},{20,12},{24,0},{28,4},{1,25},{... | collective-permute-start | bytes 1572872 | tf_op jit(solution)/shard_map/ppermute | solution.py:48
  120.1 19.7 %collective-permute-start.20 = (bf16[128,2048]{1,0:T(8,128)(2,1)}, bf16[128,2048]{1,0:T(8,128)(2,1)}, u32[]{:S(2)}, u32[]{:S(2)}) collective-permute-start(bf16[128,2048]{1,0:T(8,128)(2,1)} %place_rows.2.cot.refs_0_.refs_8_), channel_id=1, source_target_pairs={{0,8},{4,12},{8,0},{12,4},{16,24},{20,28},{24,16},{28,20},{1,9},{5... | collective-permute-start | bytes 1572872 | tf_op jit(solution)/shard_map/ppermute | solution.py:48
  120.6 19.6 %collective-permute-start.21 = (bf16[128,2048]{1,0:T(8,128)(2,1)}, bf16[128,2048]{1,0:T(8,128)(2,1)}, u32[]{:S(2)}, u32[]{:S(2)}) collective-permute-start(bf16[128,2048]{1,0:T(8,128)(2,1)} %place_rows.2.cot.refs_0_.refs_8_), channel_id=1, source_target_pairs={{0,16},{4,20},{8,24},{12,28},{16,0},{20,4},{24,8},{28,12},{1,17},{... | collective-permute-start | bytes 1572872 | tf_op jit(solution)/shard_map/ppermute | solution.py:48
  121.7 11.5 %copy-start = (bf16[128,2048]{1,0:T(8,128)(2,1)S(1)}, bf16[128,2048]{1,0:T(8,128)(2,1)}, u32[]{:S(2)}) copy-start(bf16[128,2048]{1,0:T(8,128)(2,1)} %place_rows.2.cot.refs_0_.refs_8_) | copy-start | bytes 1572868
  121.7 11.6 %copy-start.6 = (bf16[2,128,2304]{2,1,0:T(8,128)(2,1)S(1)}, bf16[2,128,2304]{2,1,0:T(8,128)(2,1)}, u32[]{:S(2)}) copy-start(bf16[2,128,2304]{2,1,0:T(8,128)(2,1)} %get-tuple-element.71) | copy-start | bytes 3538948
  129.7 15.3 %all-to-all-start.1 = ((bf16[4,32,2048]{2,1,0:T(8,128)(2,1)}), bf16[4,32,2048]{2,1,0:T(8,128)(2,1)S(1)}, u32[]{:S(2)}, u32[]{:S(2)}) async-start(bf16[4,32,2048]{2,1,0:T(8,128)(2,1)} %bitcast.18), calls=%async_computation.1 | async-start | bytes 1048576 | tf_op jit(solution)/shard_map/all_to_all | solution.py:675
  133.2 2.2 %copy-start.4 = (bf16[2,128,2304]{2,1,0:T(8,128)(2,1)S(1)}, bf16[2,128,2304]{2,1,0:T(8,128)(2,1)}, u32[]{:S(2)}) copy-start(bf16[2,128,2304]{2,1,0:T(8,128)(2,1)} %get-tuple-element.57) | copy-start | bytes 3538948
  133.3 12.1 %collective-permute-start.22 = (bf16[128,2048]{1,0:T(8,128)(2,1)S(1)}, bf16[128,2048]{1,0:T(8,128)(2,1)}, u32[]{:S(2)}, u32[]{:S(2)}) collective-permute-start(bf16[128,2048]{1,0:T(8,128)(2,1)S(1)} %copy-done), channel_id=1, source_target_pairs={{0,4},{4,0},{8,12},{12,8},{16,20},{20,16},{24,28},{28,24},{1,5},{5... | collective-permute-start | bytes 1572872 | tf_op jit(solution)/shard_map/ppermute | solution.py:48
  137.5 14.0 %copy-start.9 = (bf16[128,2048]{1,0:T(8,128)(2,1)}, bf16[128,2048]{1,0:T(8,128)(2,1)S(1)}, u32[]{:S(2)}) copy-start(bf16[128,2048]{1,0:T(8,128)(2,1)S(1)} %collective-permute-done.17.refs_3_) | copy-start | bytes 1572868
  137.5 9.6 %collective-permute-start.25 = (bf16[128,2048]{1,0:T(8,128)(2,1)S(1)}, bf16[128,2048]{1,0:T(8,128)(2,1)}, u32[]{:S(2)}, u32[]{:S(2)}) collective-permute-start(bf16[128,2048]{1,0:T(8,128)(2,1)S(1)} %collective-permute-done.17.refs_3_), channel_id=1, source_target_pairs={{0,4},{4,0},{8,12},{12,8},{16,20},{20,16},{24,28},{28,24},{1,5},{5... | collective-permute-start | bytes 1572872 | tf_op jit(solution)/shard_map/ppermute | solution.py:48
  137.9 28.2 %collective-permute-start.18 = (bf16[1,128,2304]{2,1,0:T(8,128)(2,1)}, bf16[1,128,2304]{2,1,0:T(8,128)(2,1)}, u32[]{:S(2)}, u32[]{:S(2)}) collective-permute-start(bf16[1,128,2304]{2,1,0:T(8,128)(2,1)} %add_convert_fusion.1), channel_id=1, source_target_pairs={{0,16},{4,20},{8,24},{12,28},{16,0},{20,4},{24,8},{28,12},{1,17},{... | collective-permute-start | bytes 1769480 | tf_op jit(solution)/shard_map/ppermute | solution.py:48
  139.8 7.4 %collective-permute-start.23 = (bf16[128,2048]{1,0:T(8,128)(2,1)}, bf16[128,2048]{1,0:T(8,128)(2,1)}, u32[]{:S(2)}, u32[]{:S(2)}) collective-permute-start(bf16[128,2048]{1,0:T(8,128)(2,1)} %collective-permute-done.20.refs_1_), channel_id=1, source_target_pairs={{0,4},{4,0},{8,12},{12,8},{16,20},{20,16},{24,28},{28,24},{1,5},{5... | collective-permute-start | bytes 1572872 | tf_op jit(solution)/shard_map/ppermute | solution.py:48
  140.2 9.6 %collective-permute-start.24 = (bf16[128,2048]{1,0:T(8,128)(2,1)}, bf16[128,2048]{1,0:T(8,128)(2,1)}, u32[]{:S(2)}, u32[]{:S(2)}) collective-permute-start(bf16[128,2048]{1,0:T(8,128)(2,1)} %collective-permute-done.21.refs_2_), channel_id=1, source_target_pairs={{0,4},{4,0},{8,12},{12,8},{16,20},{20,16},{24,28},{28,24},{1,5},{5... | collective-permute-start | bytes 1572872 | tf_op jit(solution)/shard_map/ppermute | solution.py:48
  145.4 20.7 %collective-permute-start.19 = (bf16[1,128,2304]{2,1,0:T(8,128)(2,1)}, bf16[1,128,2304]{2,1,0:T(8,128)(2,1)S(1)}, u32[]{:S(2)}, u32[]{:S(2)}) collective-permute-start(bf16[1,128,2304]{2,1,0:T(8,128)(2,1)} %add_convert_fusion), channel_id=1, source_target_pairs={{0,8},{4,12},{8,0},{12,4},{16,24},{20,28},{24,16},{28,20},{1,9},{5... | collective-permute-start | bytes 1769480 | tf_op jit(solution)/shard_map/ppermute | solution.py:48
  147.0 19.0 %copy-start.14 = (bf16[32,2048]{1,0:T(8,128)(2,1)}, bf16[32,2048]{1,0:T(8,128)(2,1)S(1)}, u32[]{:S(2)}) copy-start(bf16[32,2048]{1,0:T(8,128)(2,1)S(1)} %fusion.6.refs_0_) | copy-start | bytes 393220
  147.0 19.0 %collective-permute-start.26 = (bf16[32,2048]{1,0:T(8,128)(2,1)S(1)}, bf16[32,2048]{1,0:T(8,128)(2,1)S(1)}, u32[]{:S(2)}, u32[]{:S(2)}) collective-permute-start(bf16[32,2048]{1,0:T(8,128)(2,1)S(1)} %fusion.6.refs_0_), channel_id=1, source_target_pairs={{0,1},{1,0},{2,3},{3,2},{4,5},{5,4},{6,7},{7,6},{8,9},{9,8},{10,11... | collective-permute-start | bytes 393224 | tf_op jit(solution)/shard_map/ppermute | solution.py:682
  147.1 18.9 %collective-permute-start.27 = (bf16[32,2048]{1,0:T(8,128)(2,1)S(1)}, bf16[32,2048]{1,0:T(8,128)(2,1)S(1)}, u32[]{:S(2)}, u32[]{:S(2)}) collective-permute-start(bf16[32,2048]{1,0:T(8,128)(2,1)S(1)} %fusion.6.refs_0_), channel_id=1, source_target_pairs={{0,2},{1,3},{2,0},{3,1},{4,6},{5,7},{6,4},{7,5},{8,10},{9,11},{10,... | collective-permute-start | bytes 393224 | tf_op jit(solution)/shard_map/ppermute | solution.py:682
  149.9 16.2 %collective-permute-start.28 = (bf16[32,2048]{1,0:T(8,128)(2,1)S(1)}, bf16[32,2048]{1,0:T(8,128)(2,1)S(1)}, u32[]{:S(2)}, u32[]{:S(2)}) collective-permute-start(bf16[32,2048]{1,0:T(8,128)(2,1)S(1)} %fusion.6.refs_0_), channel_id=1, source_target_pairs={{0,3},{1,2},{2,1},{3,0},{4,7},{5,6},{6,5},{7,4},{8,11},{9,10},{10,... | collective-permute-start | bytes 393224 | tf_op jit(solution)/shard_map/ppermute | solution.py:682
  151.5 14.6 %copy-start.5 = (bf16[2,128,2304]{2,1,0:T(8,128)(2,1)S(1)}, bf16[2,128,2304]{2,1,0:T(8,128)(2,1)}, u32[]{:S(2)}) copy-start(bf16[2,128,2304]{2,1,0:T(8,128)(2,1)} %get-tuple-element.57) | copy-start | bytes 3538948
  166.0 2.0 %copy-start.15 = (bf16[32,2048]{1,0:T(8,128)(2,1)}, bf16[32,2048]{1,0:T(8,128)(2,1)S(1)}, u32[]{:S(2)}) copy-start(bf16[32,2048]{1,0:T(8,128)(2,1)S(1)} %collective-permute-done.26.refs_1_) | copy-start | bytes 393220
  166.0 2.0 %copy-start.16 = (bf16[32,2048]{1,0:T(8,128)(2,1)}, bf16[32,2048]{1,0:T(8,128)(2,1)S(1)}, u32[]{:S(2)}) copy-start(bf16[32,2048]{1,0:T(8,128)(2,1)S(1)} %collective-permute-done.27.refs_2_) | copy-start | bytes 393220
  166.1 1.9 %copy-start.17 = (bf16[32,2048]{1,0:T(8,128)(2,1)}, bf16[32,2048]{1,0:T(8,128)(2,1)S(1)}, u32[]{:S(2)}) copy-start(bf16[32,2048]{1,0:T(8,128)(2,1)S(1)} %collective-permute-done.28.refs_3_) | copy-start | bytes 393220

commit v3 on v2

--- a/solution.py
+++ b/solution.py
@@ -389,9 +389,8 @@
     )(place, gain, *feats, w_gate, w_up)
 
 
-def own_kernel(
-    cot, slope_up, slope_gate, gate_hbm, up_hbm, down_hbm, out_ref, gate, up, down, sems
-):
+def own_kernel(here_ref, cot, slope_up, slope_gate, gate_hbm, up_hbm, down_hbm, *refs):
+    outs, (total, gate, up, down, sems) = refs[:-5], refs[-5:]
     loads = [
         pltpu.make_async_copy(src, dst, sems.at[k])
         for k, (src, dst) in enumerate(((down_hbm, down), (gate_hbm, gate), (up_hbm, up)))
@@ -404,21 +403,24 @@
     d_gate = (d_hidden * slope_gate[...].astype(F32)).astype(BF16)
     loads[1].wait()
     loads[2].wait()
-    for at in tiles(out_ref.shape[1], 512):
-        out_ref[:, at] = (mm(d_gate, gate[at, :], LAST) + mm(d_up, up[at, :], LAST)).astype(BF16)
-
-
-def item_own(cot, slope_up, slope_gate, w_gate, w_up, w_down):
+    for at in tiles(total.shape[1], 512):
+        total[:, at] = (mm(d_gate, gate[at, :], LAST) + mm(d_up, up[at, :], LAST)).astype(BF16)
+    cut_rows(here_ref[0], total, outs)
+
+
+def item_own(here, cot, slope_up, slope_gate, w_gate, w_up, w_down, n_narrow):
     rows, width = cot.shape
     hid = w_gate.shape[1]
+    part = (rows // n_narrow, width)
     return pl.pallas_call(
         own_kernel,
         grid=(1,),
-        in_specs=[whole_spec((rows, width)), whole_spec((rows, hid)), whole_spec((rows, hid))]
+        in_specs=[smem(), whole_spec((rows, width)), whole_spec((rows, hid)), whole_spec((rows, hid))]
         + [hbm()] * 3,
-        out_specs=whole_spec((rows, width)),
-        out_shape=jax.ShapeDtypeStruct((rows, width), BF16),
+        out_specs=[whole_spec(part)] * n_narrow,
+        out_shape=[jax.ShapeDtypeStruct(part, BF16)] * n_narrow,
         scratch_shapes=[
+            pltpu.VMEM((rows, width), BF16),
             pltpu.VMEM((width, hid), BF16),
             pltpu.VMEM((width, hid), BF16),
             pltpu.VMEM((hid, width), BF16),
@@ -427,83 +429,65 @@
         compiler_params=params(),
         cost_estimate=cost(6 * rows * width * hid, 11e6),
         name="item_own",
-    )(cot, slope_up, slope_gate, w_gate, w_up, w_down)
-
-
-def late_kernel(count, scale, place_ref, *refs):
+    )(jnp.reshape(here, (1,)), cot, slope_up, slope_gate, w_gate, w_up, w_down)
+
+
+def late_kernel(slots, before, scale, place_ref, *refs):
+    count = len(slots)
     pieces, (column_hbm, normed_hbm, hidden_hbm, slope_up_hbm, slope_gate_hbm, down_hbm) = (
         refs[:count],
         refs[count : count + 6],
     )
-    gate_out, up_out, down_out = refs[count + 6 : count + 9]
-    cot, column, normed, hidden, slope_up, slope_gate, down, sems = refs[count + 9 :]
+    earlier, refs = (refs[count + 6 : count + 9], refs[count + 9 :]) if before else (None, refs[count + 6 :])
+    outs, (cot, column, normed, hidden, slope_up, slope_gate, down, sems) = refs[:3], refs[3:]
     rows = cot.shape[0] // count
-    half = cot.shape[0] // 2
-    used = 0
-
-    def load(src, dst):
-        nonlocal used
-        copy = pltpu.make_async_copy(src, dst, sems.at[used])
-        used += 1
-        return copy
-
-    narrow = normed.shape[1] % 128 != 0
-    parts = []
-    down_load = load(down_hbm, down)
-    for h in range(2):
-        at = pl.ds(h * half, half)
-        waits = [
-            load(pieces[k], cot.at[pl.ds(k * rows, rows)])
-            for k in range(h * count // 2, (h + 1) * count // 2)
-        ]
-        for src, dst in (
-            (slope_up_hbm, slope_up),
-            (slope_gate_hbm, slope_gate),
-            (normed_hbm, normed),
-            (hidden_hbm, hidden),
-        ):
-            waits.append(load(src.at[at], dst.at[at]))
-        if narrow:
-            waits.append(load(column_hbm.at[at], column.at[at]))
-        parts.append(waits)
-    down_load.start()
-    for copy in parts[0]:
-        copy.start()
     block = column.shape[1]
-    for h in range(2):
-        for copy in parts[h]:
-            copy.wait()
-        if h == 0:
-            down_load.wait()
-            for copy in parts[1]:
-                copy.start()
-        at = slice(h * half, (h + 1) * half)
-        if not narrow:
-            column[at, :] = cot[at, pl.ds(pl.multiple_of(place_ref[2] * block, 128), block)]
-        for to in tiles(hidden.shape[1], TILE):
-            d_hidden = mm(cot[at, :], down[to, :], LAST)
-            d_up = (d_hidden * slope_up[at, to].astype(F32)).astype(BF16)
-            d_gate = (d_hidden * slope_gate[at, to].astype(F32)).astype(BF16)
-            gate_part = mm(normed[at, :], d_gate, FIRST) * scale
-            up_part = mm(normed[at, :], d_up, FIRST) * scale
-            down_part = mm(hidden[at, to], column[at, :], FIRST) * scale
-            if h == 0:
-                gate_out[:, to] = gate_part
-                up_out[:, to] = up_part
-                down_out[to, :] = down_part
-            else:
-                gate_out[:, to] += gate_part
-                up_out[:, to] += up_part
-                down_out[to, :] += down_part
-
-
-def item_late(place, pieces, column, normed, hidden, slope_up, slope_gate, w_down, scale):
+    narrow = block % 128 != 0
+    hid = hidden.shape[1]
+    copies = [(piece, cot.at[pl.ds(k * rows, rows)]) for k, piece in enumerate(pieces)]
+    copies += [(down_hbm.at[to], down.at[to]) for to in tiles(hid, TILE)]
+    for k, slot in enumerate(slots):
+        at, to = pl.ds(slot * rows, rows), pl.ds(k * rows, rows)
+        copies += [(slope_up_hbm.at[at], slope_up.at[to]), (slope_gate_hbm.at[at], slope_gate.at[to])]
+        copies += [(normed_hbm.at[at], normed.at[to]), (hidden_hbm.at[at], hidden.at[to])]
+    if narrow:
+        copies.append((column_hbm, column))
+    loads = [pltpu.make_async_copy(src, dst, sems.at[k]) for k, (src, dst) in enumerate(copies)]
+    for load in loads:
+        load.start()
+    for load in loads[:count]:
+        load.wait()
+    if not narrow:
+        column[...] = cot[:, pl.ds(pl.multiple_of(place_ref[2] * block, 128), block)]
+    downs, rest = loads[count : count + len(tiles(hid, TILE))], loads[count + len(tiles(hid, TILE)) :]
+    for k, to in enumerate(tiles(hid, TILE)):
+        downs[k].wait()
+        d_hidden = mm(cot[...], down[to, :], LAST)
+        if k == 0:
+            for load in rest:
+                load.wait()
+        d_up = (d_hidden * slope_up[:, to].astype(F32)).astype(BF16)
+        d_gate = (d_hidden * slope_gate[:, to].astype(F32)).astype(BF16)
+        gate_part = mm(normed[...], d_gate, FIRST) * scale
+        up_part = mm(normed[...], d_up, FIRST) * scale
+        down_part = mm(hidden[:, to], column[...], FIRST) * scale
+        if before:
+            gate_part += earlier[0][:, to]
+            up_part += earlier[1][:, to]
+            down_part += earlier[2][to, :]
+        outs[0][:, to] = gate_part
+        outs[1][:, to] = up_part
+        outs[2][to, :] = down_part
+
+
+def item_late(place, slots, pieces, column, normed, hidden, slope_up, slope_gate, w_down, before, scale):
     count = len(pieces)
     rows, width = count * pieces[0].shape[0], pieces[0].shape[1]
     hid, block = w_down.shape[0], normed.shape[1]
+    before = list(before) if before is not None else []
     return pl.pallas_call(
-        functools.partial(late_kernel, count, scale),
-        in_specs=[smem()] + [hbm()] * (count + 6),
+        functools.partial(late_kernel, tuple(slots), bool(before), scale),
+        in_specs=[smem()] + [hbm()] * (count + 6) + [vmem()] * len(before),
         out_specs=[vmem()] * 3,
         out_shape=[
             jax.ShapeDtypeStruct((block, hid), F32),
@@ -518,12 +502,80 @@
             pltpu.VMEM((rows, hid), BF16),
             pltpu.VMEM((rows, hid), BF16),
             pltpu.VMEM((hid, width), BF16),
-            pltpu.SemaphoreType.DMA((count + 11,)),
+            pltpu.SemaphoreType.DMA((5 * count + 1 + len(tiles(hid, TILE)),)),
         ],
         compiler_params=params(),
         cost_estimate=cost(4 * rows * width * hid + 12 * rows * block * hid, 16e6),
         name="item_late",
-    )(place, *pieces, column, normed, hidden, slope_up, slope_gate, w_down)
+    )(
+        place, *pieces, column, normed, hidden, slope_up, slope_gate, w_down, *before,
+    )
+
+
+def merge_kernel(here_ref, kept_ref, got_ref, *refs):
+    count = sum(1 for r in refs if r.shape == kept_ref.shape) - 1
+    pieces, outs, total = refs[:count], refs[count:-1], refs[-1]
+    value = kept_ref[...].astype(F32) + got_ref[...].astype(F32)
+    for piece in pieces:
+        value = value + piece[...].astype(F32)
+    total[...] = value.astype(BF16)
+    cut_rows(here_ref[0], total, outs)
+
+
+def cut_rows(here, total, outs):
+    rows = outs[0].shape[0]
+    for k, out in enumerate(outs):
+        out[...] = total[pl.ds(pl.multiple_of((here ^ k) * rows, rows), rows), :]
+
+
+def merge_chips(here, kept, got, pieces, n_narrow):
+    rows, width = pieces[0].shape
+    spec = whole_spec((rows, width))
+    part = (rows // n_narrow, width)
+    return pl.pallas_call(
+        merge_kernel,
+        grid=(1,),
+        in_specs=[smem()] + [spec] * (2 + len(pieces)),
+        out_specs=[whole_spec(part)] * n_narrow,
+        out_shape=[jax.ShapeDtypeStruct(part, BF16)] * n_narrow,
+        scratch_shapes=[pltpu.VMEM((rows, width), BF16)],
+        compiler_params=params(),
+        cost_estimate=cost(0, 2 * (4 + len(pieces)) * rows * width),
+        name="merge_chips",
+    )(jnp.reshape(here, (1,)), kept, got, *pieces)
+
+
+def final_kernel(scale, here_ref, kept_a, got_a, kept_b, got_b, *refs):
+    slots, (feat_out, gate_out, up_out, down_out) = refs[:-4], refs[-4:]
+    cut, hid = kept_a.shape[0], gate_out.shape[1]
+    for half, (kept, got) in enumerate(((kept_a, got_a), (kept_b, got_b))):
+        total = (kept[...] + got[...].astype(F32)) * scale
+        at = slice(half * cut, (half + 1) * cut)
+        gate_out[at, :] = total[:, :hid]
+        up_out[at, :] = total[:, hid : 2 * hid]
+        down_out[:, at] = total[:, 2 * hid :].T
+    rows = slots[0].shape[0]
+    for k, slot in enumerate(slots):
+        feat_out[pl.ds(pl.multiple_of((here_ref[0] ^ k) * rows, rows), rows), :] = slot[...]
+
+
+def final_sums(here, kept_a, got_a, kept_b, got_b, slots, scale):
+    cut, hid = kept_a.shape[0], kept_a.shape[1] // 3
+    rows, width = slots[0].shape
+    return pl.pallas_call(
+        functools.partial(final_kernel, scale),
+        in_specs=[smem()] + [vmem()] * (4 + len(slots)),
+        out_specs=[vmem()] * 4,
+        out_shape=[
+            jax.ShapeDtypeStruct((len(slots) * rows, width), BF16),
+            jax.ShapeDtypeStruct((2 * cut, hid), F32),
+            jax.ShapeDtypeStruct((2 * cut, hid), F32),
+            jax.ShapeDtypeStruct((hid, 2 * cut), F32),
+        ],
+        compiler_params=params(),
+        cost_estimate=cost(0, 30 * cut * hid),
+        name="final_sums",
+    )(jnp.reshape(here, (1,)), kept_a, got_a, kept_b, got_b, *slots)
 
 
 def place_kernel(here_ref, *refs):
@@ -640,17 +692,17 @@
         1.0 / n_narrow,
         item_dev,
     )
-    sent, *_ = lax.optimization_barrier((sent, feats[1], feats[2 % n_wide]))
+    sent, *_ = lax.optimization_barrier((sent, *feats[1:n_chips]))
     got = swap(sent, 1)
     sent_table = jnp.stack([(chip ^ rels) * 2 + 1 - core])
     grads_sent = sent_grads(sent_table, normed, masked, d_gate, d_up, hidden, block)
     got, grads_sent = lax.optimization_barrier((got, grads_sent))
     grads_got = swap(grads_sent, 1)
     sums = []
-    for r in range(n_chips):
+    for r in range(1, n_chips):
         at = slice(r * item_dev, (r + 1) * item_dev)
-        sums.append(kept[at].astype(F32) + got[at].astype(F32))
-    pieces = [swap(sums[r].astype(BF16), r << 1) for r in range(1, n_chips)]
+        sums.append((kept[at].astype(F32) + got[at].astype(F32)).astype(BF16))
+    pieces = [swap(total, r << 1) for r, total in enumerate(sums, 1)]
 
     group = min(8, n_wide)
     forwards = [
@@ -664,18 +716,18 @@
         kept_table, normed, masked, d_gate, d_up, hidden, grads_got, block
     )
     pieces[0], sent_a, sent_b = lax.optimization_barrier((pieces[0], sent_a, sent_b))
-    mine = functools.reduce(jnp.add, [p.astype(F32) for p in pieces], sums[0]).astype(BF16)
-    sent_a, sent_b, mine = lax.optimization_barrier((sent_a, sent_b, mine))
-
+    mine = list(merge_chips(here, kept, got, pieces, n_narrow))
+    sent_a, sent_b, mine[0] = lax.optimization_barrier((sent_a, sent_b, mine[0]))
     got_a, got_b = swap(sent_a, order_a[0]), swap(sent_b, order_b[0])
 
     quarter = item_dev // n_narrow
 
-    def narrow_scatter(value):
-        parts = lax.all_to_all(
-            value.reshape(n_narrow, quarter, width), "narrow", split_axis=0, concat_axis=0, tiled=True
-        )
-        return jnp.sum(parts.astype(F32), axis=0)
+    def narrow_scatter(parts):
+        got = [
+            part if k == 0 else lax.ppermute(part, "narrow", [(i, i ^ k) for i in range(n_narrow)])
+            for k, part in enumerate(parts)
+        ]
+        return functools.reduce(jnp.add, [part.astype(F32) for part in got])
 
     def narrow_slots(piece):
         return [piece] + [
@@ -688,59 +740,70 @@
 
     item_in = narrow_scatter(mine)
     item_cot = narrow_gather(item_in.astype(BF16))
-    cots = near(item_cot)
+    cots = [item_cot] + [swap(item_cot, r << 1) for r in range(1, n_chips - 1)]
+    last_cot, *cots[1:] = lax.optimization_barrier((item_cot, *cots[1:]))
+    cots.append(swap(last_cot, (n_chips - 1) << 1))
     item_part = item_own(
-        item_cot, forwards[0][2], forwards[0][3], item_gate, item_up, item_down
+        here, item_cot, forwards[0][2], forwards[0][3], item_gate, item_up, item_down, n_narrow
     )
     item_dn = narrow_scatter(item_part)
 
-    got_a, got_b, _ = lax.optimization_barrier((got_a, got_b, item_part))
+    got_a, got_b, _ = lax.optimization_barrier((got_a, got_b, item_part[0]))
+    assert len(order_a) > 1
     total_a = first_sums(got_a, kept_a, places["a"])
     total_b = first_sums(got_b, kept_b, places["b"])
     for a, b in zip(order_a[1:], order_b[1:]):
         away_a, away_b = sent_away(total_a, a), sent_away(total_b, b)
-        away_a, away_b, cots[-1] = lax.optimization_barrier((away_a, away_b, cots[-1]))
+        away_a, away_b, cots[1] = lax.optimization_barrier((away_a, away_b, cots[1]))
         got_a, got_b = swap(away_a, a), swap(away_b, b)
         if a != order_a[-1]:
             total_a, total_b = next_sums(total_a, got_a, a), next_sums(total_b, got_b, b)
     cots = cots + [swap(piece, 1) for piece in cots]
 
-    item_scaled = item_gain.astype(F32)[None, :] * item_dn
-    own = lax.dynamic_slice_in_dim(item_feat, here * quarter, quarter, axis=0).astype(F32)
-    own_inv = lax.rsqrt(jnp.mean(own * own, axis=1, keepdims=True) + 1e-05)
-    own_unit = own * own_inv
-    item_mean = jnp.mean(item_scaled * own_unit, axis=1, keepdims=True)
-    feat_rows = (item_in + own_inv * (item_scaled - own_unit * item_mean)).astype(BF16)
-    feat_slots = narrow_slots(feat_rows)
-
-    item_grads = None
-    for k, (normed_k, hidden_k, slope_up_k, slope_gate_k) in enumerate(forwards):
-        parts = cots[k * group : (k + 1) * group]
+    slots = range(n_wide)
+    if n_wide == group:
+        arrived = [k for k in slots if k % n_chips != n_chips - 1]
+        lots = [arrived, [k for k in slots if k not in arrived]]
+    else:
+        lots = [list(slots[k : k + group]) for k in range(0, n_wide, group)]
+
+    def late(lot, before):
+        normed_k, hidden_k, slope_up_k, slope_gate_k = forwards[lot[0] // group]
+        parts = [cots[k] for k in lot]
         column = parts[0]
         if block % 128:
             normed_k = lax.dynamic_slice_in_dim(normed_k, me * block, block, axis=1)
             column = jnp.concatenate(
                 [lax.dynamic_slice_in_dim(p, me * block, block, axis=1) for p in parts], axis=0
             )
-        found = item_late(
-            place, parts, column, normed_k, hidden_k, slope_up_k, slope_gate_k, item_down, 1.0 / n_wide
+        return list(
+            item_late(
+                place, [k % group for k in lot], parts, column, normed_k, hidden_k, slope_up_k,
+                slope_gate_k, item_down, before, 1.0 / n_wide,
+            )
         )
-        item_grads = list(found) if item_grads is None else [a + b for a, b in zip(item_grads, found)]
+
+    item_grads = late(lots[0], None)
+    own_feat = lax.dynamic_slice_in_dim(item_feat, here * quarter, quarter, axis=0)
+    own_feat, item_in, item_grads[0] = lax.optimization_barrier((own_feat, item_in, item_grads[0]))
+    item_scaled = item_gain.astype(F32)[None, :] * item_dn
+    own = own_feat.astype(F32)
+    own_inv = lax.rsqrt(jnp.mean(own * own, axis=1, keepdims=True) + 1e-05)
+    own_unit = own * own_inv
+    item_mean = jnp.mean(item_scaled * own_unit, axis=1, keepdims=True)
+    feat_rows = (item_in + own_inv * (item_scaled - own_unit * item_mean)).astype(BF16)
+    feat_slots = narrow_slots(feat_rows)
+
+    for lot in lots[1:]:
+        item_grads = late(lot, item_grads)
 
     got_a, got_b, item_grads[0], *feat_slots = lax.optimization_barrier(
         (got_a, got_b, item_grads[0], *feat_slots)
     )
-    feat_grad = place_rows(here, feat_slots)
-    if len(order_a) > 1:
-        total_a, total_b = next_sums(total_a, got_a, order_a[-1]), next_sums(total_b, got_b, order_b[-1])
-    user_grads = jnp.concatenate([total_a[0], total_b[0]], axis=0) * (1.0 / n_wide)
-    return (
-        feat_grad,
-        user_grads[:, :hid],
-        user_grads[:, hid : 2 * hid],
-        user_grads[:, 2 * hid :].T,
-        *item_grads,
-    )
+    feat_grad, *user_grads = final_sums(
+        here, total_a[0], got_a[0], total_b[0], got_b[0], feat_slots, 1.0 / n_wide
+    )
+    return (feat_grad, *user_grads, *item_grads)
 
 
 def solution(mesh):

time: 173 us -> 168 us (0.971)
  waiting for transfers between devices: 42.5 us -> 24.9 us
  Pallas kernels: 77.2 us -> 87.1 us
  starting transfers between devices: 33.7 us -> 39.1 us
  other arithmetic: 13.5 us -> 9.41 us
    all_to_all x2 -> x0, waiting for transfers between devices: 18.7 us -> none  [narrow_scatter(): lax.all_to_all(value.reshape(n_narrow, quarter, width), 'narrow', split_a...]
    ppermute x0 -> x6, starting transfers between devices: none -> 11.9 us  [narrow_scatter(): lax.ppermute(part, 'narrow', [(i, i ^ k) for i in range(n_narrow)])]
    pallas_call x2 -> x5, Pallas kernels: 22.5 us -> 34.2 us  [the longest x2 19.1 us: item_late(): pl.pallas_call(functools.partial(late_kernel, tuple(slots), bool(before),...]
    ppermute x23, waiting for transfers between devices: 15.8 us -> 6.32 us  [swap(): return lax.ppermute(value, 'wide', [(i, i ^ bit) for i in range(count)])]
    all_to_all x2 -> x0, starting transfers between devices: 8.35 us -> none  [narrow_scatter(): lax.all_to_all(value.reshape(n_narrow, quarter, width), 'narrow', split_a...]
    ppermute x0 -> x6, waiting for transfers between devices: none -> 8.23 us  [narrow_scatter(): lax.ppermute(part, 'narrow', [(i, i ^ k) for i in range(n_narrow)])]
    convert_element_type x4 -> x1, other arithmetic: 9.59 us -> 2.89 us  [body(): sums.append((kept[at].astype(F32) + got[at].astype(F32)).astype(BF16))]
    ppermute x6, waiting for transfers between devices: 8.11 us -> 10.3 us  [narrow_slots(): lax.ppermute(piece, 'narrow', [(i, i ^ k) for i in range(n_narrow)])]
  transfers between devices with their start and end apart: 31 -> 35, of which waited for: 7 -> 11; matrix products, arithmetic and copies ran while one was open for 5% -> 7% of each run, Pallas kernels for 44% -> 48%
where the time goes in v3:
time: 168 us
  Pallas kernels  87.1 us (52%)
  starting transfers between devices  39.1 us (23%)
  waiting for transfers between devices  24.9 us (15%)
  other arithmetic  9.41 us (6%)
  local copies, waits for them, and re-layouts  6.05 us (4%)
    pallas_call x1, Pallas kernels, user_layer(): pl.pallas_call(functools.partial(user_kernel, share, item_dev), in_specs=...  19.1 us
    pallas_call x2, Pallas kernels, item_late(): pl.pallas_call(functools.partial(late_kernel, tuple(slots), bool(before),...  19.1 us
    ppermute x23, starting transfers between devices, swap(): return lax.ppermute(value, 'wide', [(i, i ^ bit) for i in range(count)])  18 us
    pallas_call x1, Pallas kernels, item_forward(): pl.pallas_call(functools.partial(forward_kernel, count), in_specs=[smem()...  14.5 us
    ppermute x6, starting transfers between devices, narrow_scatter(): lax.ppermute(part, 'narrow', [(i, i ^ k) for i in range(n_narrow)])  11.9 us
    ppermute x6, waiting for transfers between devices, narrow_slots(): lax.ppermute(piece, 'narrow', [(i, i ^ k) for i in range(n_narrow)])  10.3 us
    pallas_call x1, Pallas kernels, kept_grads(): pl.pallas_call(kept_kernel, grid_spec=pltpu.PrefetchScalarGridSpec(num_sc...  9.66 us
    ppermute x6, starting transfers between devices, narrow_slots(): lax.ppermute(piece, 'narrow', [(i, i ^ k) for i in range(n_narrow)])  9.25 us
  transfers between devices with their start and end apart: 35, of which 11 were waited for; matrix products, arithmetic and copies ran while one was open for 7% of the time, Pallas kernels for 48%

profile of v3, /device:TPU:0, one launch (start us, length us, event | category | flops | bytes accessed | tf_op | source)
XLA Modules:
  0.0 167.6 jit_solution(18380862393851298711)
XLA Ops:
  0.6 3.0 %collective-permute-start = (bf16[128,2048]{1,0:T(8,128)(2,1)}, bf16[128,2048]{1,0:T(8,128)(2,1)S(1)}, u32[]{:S(2)}, u32[]{:S(2)}) collective-permute-start(bf16[128,2048]{1,0:T(8,128)(2,1)} %refs_0_.1), channel_id=1, source_target_pairs={{0,8},{4,12},{8,0},{12,4},{16,24},{20,28},{24,16},{28,20},{1,9},{5... | collective-permute-start | bytes 1572872 | tf_op jit(solution)/shard_map/ppermute | solution.py:48
  3.6 1.5 collective-permute-start.1
  5.2 0.7 pad_add_fusion.place_ref
  5.8 19.1 %user_layer.1 = (bf16[512,2048]{1,0:T(8,128)(2,1)}, bf16[512,2048]{1,0:T(8,128)(2,1)}, bf16[512,768]{1,0:T(8,128)(2,1)}, bf16[512,768]{1,0:T(8,128)(2,1)}, bf16[...) custom-call(s32[3]{0:T(128)} %pad_add_fusion.place_ref, s32[8]{0:T(128)} %hist_len_ref.1, ...), custom_call_target="tpu_custom_call" | custom-call | flops 1342177280 | bytes 4000000 | tf_op jit(solution)/shard_map/user_layer/pallas_call | solution.py:172
  25.0 3.5 %collective-permute-done.1.refs_2_ = bf16[128,2048]{1,0:T(8,128)(2,1)S(1)} collective-permute-done((bf16[128,2048]{1,0:T(8,128)(2,1)}, bf16[128,2048]{1,0:T(8,128)(2,1)S(1)}, u32[]{:S(2)}, u32[]{:S(2)}) %collective-permute-start.1) | collective-permute-done | bytes 524320 | tf_op jit(solution)/shard_map/ppermute | solution.py:48
  28.5 0.6 add_subtract_fusion.table_ref
  29.3 7.6 %sent_grads.1 = bf16[4,256,2304]{2,1,0:T(8,128)(2,1)} custom-call(s32[1,4]{1,0:T(1,128)} %add_subtract_fusion.table_ref, bf16[512,2048]{1,0:T(8,128)(2,1)} %get-tuple-element.68.normed_ref, bf16[512,2048]{1,0:T(8,128)(2,1)} %get-tuple-element.69.masked_ref, bf16[512,768]{1,0:T(8,128)(2,1)} %get-tuple-element.70.d_gate_ref, ...), custom_call_target="tpu_custom_call" | custom-call | flops 402653184 | bytes 1666666 | tf_op jit(solution)/shard_map/sent_grads/pallas_call | solution.py:260
  37.0 0.2 collective-permute-start.4
  37.2 0.3 collective-permute-start.5
  37.5 0.2 collective-permute-start.6
  37.7 0.3 collective-permute-start.7
  38.0 0.2 collective-permute-start.8
  38.3 2.9 %add_convert_fusion.2 = (bf16[128,2048]{1,0:T(8,128)(2,1)}, bf16[128,2048]{1,0:T(8,128)(2,1)}, bf16[128,2048]{1,0:T(8,128)(2,1)}) fusion(bf16[512,2048]{1,0:T(8,128)(2,1)} %collective-permute-done.3.got_ref, bf16[512,2048]{1,0:T(8,128)(2,1)S(1)} %copy-done.1), kind=kLoop, calls=%fused_computation.4 | loop fusion | flops 3145728 | bytes 4718592 | tf_op jit(solution)/shard_map/convert_element_type | solution.py:704
  41.2 1.3 collective-permute-done.5.refs_4_
  42.4 1.4 collective-permute-start.9
  43.9 1.4 collective-permute-start.10
  45.5 0.8 copy-done.17
  46.2 1.4 collective-permute-start.11
  47.7 0.6 stack.50.table_ref
  48.3 14.5 %item_forward.1 = (bf16[1024,256]{1,0:T(8,128)(2,1)}, bf16[1024,768]{1,0:T(8,128)(2,1)}, bf16[1024,768]{1,0:T(8,128)(2,1)}, bf16[1024,768]{1,0:T(8,128)(2,1)}) custom-call(s32[3]{0:T(128)} %pad_add_fusion.place_ref, bf16[2048]{0:T(1024)(128)(2,1)} %gain_ref.3, bf16[128,2048]{1,0:T(8,128)(2,1)} %refs_0_.1, bf16[128,2048]{1,0:T(8,128)(2,1)} %copy-done.9, ...), custom_call_target="tpu_custom_call" | custom-call | flops 1073741824 | bytes 2666666 | tf_op jit(solution)/shard_map/item_forward/pallas_call | solution.py:370
  62.8 9.7 %kept_grads.1 = (bf16[2,128,2304]{2,1,0:T(8,128)(2,1)}, bf16[2,128,2304]{2,1,0:T(8,128)(2,1)}, bf16[2,128,2304]{2,1,0:T(8,128)(2,1)}, bf16[2,128,2304]{2,1,0:T(8,128)(2,1)}) custom-call(s32[8,4]{1,0:T(8,128)} %stack.50.table_ref, bf16[512,2048]{1,0:T(8,128)(2,1)} %get-tuple-element.68.normed_ref, bf16[512,2048]{1,0:T(8,128)(2,1)} %get-tuple-element.69.masked_ref, ...), custom_call_target="tpu_custom_call" | custom-call | flops 402653184 | bytes 2500000 | tf_op jit(solution)/shard_map/kept_grads/pallas_call | solution.py:283
  72.6 0.7 copy-done.12
  73.6 3.1 %merge_chips.1 = (bf16[32,2048]{1,0:T(8,128)(2,1)}, bf16[32,2048]{1,0:T(8,128)(2,1)}, bf16[32,2048]{1,0:T(8,128)(2,1)}, bf16[32,2048]{1,0:T(8,128)(2,1)}) custom-call(s32[1]{0:T(128)} %bitcast.here_ref, bf16[512,2048]{1,0:T(8,128)(2,1)} %get-tuple-element.79.kept_ref, bf16[512,2048]{1,0:T(8,128)(2,1)} %collective-permute-done.3.got_ref, ...), custom_call_target="tpu_custom_call" | custom-call | bytes 611669 | tf_op jit(solution)/shard_map/merge_chips/pallas_call | solution.py:535
  76.7 1.6 collective-permute-start.14
  78.3 2.6 %collective-permute-start.15 = (bf16[32,2048]{1,0:T(8,128)(2,1)}, bf16[32,2048]{1,0:T(8,128)(2,1)S(1)}, u32[]{:S(2)}, u32[]{:S(2)}) collective-permute-start(bf16[32,2048]{1,0:T(8,128)(2,1)} %get-tuple-element.91), channel_id=1, source_target_pairs={{0,2},{1,3},{2,0},{3,1},{4,6},{5,7},{6,4},{7,5},{8,10},{9,11},{10,... | collective-permute-start | bytes 393224 | tf_op jit(solution)/shard_map/ppermute | solution.py:727
  80.9 0.2 collective-permute-start.16
  81.1 1.4 collective-permute-start.12
  82.6 0.6 collective-permute-start.13
  83.2 1.1 collective-permute-done.14
  84.3 7.1 %collective-permute-done.15 = bf16[32,2048]{1,0:T(8,128)(2,1)S(1)} collective-permute-done((bf16[32,2048]{1,0:T(8,128)(2,1)}, bf16[32,2048]{1,0:T(8,128)(2,1)S(1)}, u32[]{:S(2)}, u32[]{:S(2)}) %collective-permute-start.15) | collective-permute-done | bytes 131104 | tf_op jit(solution)/shard_map/ppermute | solution.py:727
  91.4 1.0 fusion.8
  92.4 2.3 %collective-permute-start.17 = (bf16[32,2048]{1,0:T(8,128)(2,1)S(1)}, bf16[32,2048]{1,0:T(8,128)(2,1)S(1)}, u32[]{:S(2)}, u32[]{:S(2)}) collective-permute-start(bf16[32,2048]{1,0:T(8,128)(2,1)S(1)} %get-tuple-element.129.refs_0_), channel_id=1, source_target_pairs={{0,1},{1,0},{2,3},{3,2},{4,5},{5,4},{6,7},{7,6},{8,9},{9,8},{10,11... | collective-permute-start | bytes 393224 | tf_op jit(solution)/shard_map/ppermute | solution.py:734
  94.7 1.1 collective-permute-start.18
  95.8 1.4 collective-permute-start.19
  97.2 1.8 %collective-permute-done.17.refs_1_ = bf16[32,2048]{1,0:T(8,128)(2,1)S(1)} collective-permute-done((bf16[32,2048]{1,0:T(8,128)(2,1)S(1)}, bf16[32,2048]{1,0:T(8,128)(2,1)S(1)}, u32[]{:S(2)}, u32[]{:S(2)}) %collective-permute-start.17) | collective-permute-done | bytes 131104 | tf_op jit(solution)/shard_map/ppermute | solution.py:734
  99.0 7.9 %collective-permute-done.18.refs_2_ = bf16[32,2048]{1,0:T(8,128)(2,1)S(1)} collective-permute-done((bf16[32,2048]{1,0:T(8,128)(2,1)S(1)}, bf16[32,2048]{1,0:T(8,128)(2,1)S(1)}, u32[]{:S(2)}, u32[]{:S(2)}) %collective-permute-start.18) | collective-permute-done | bytes 131104 | tf_op jit(solution)/shard_map/ppermute | solution.py:734
  106.9 0.6 copy-done.27
  107.6 0.7 copy-done.28
  108.2 1.9 %place_rows.1.cot.refs_0_.refs_6_ = bf16[128,2048]{1,0:T(8,128)(2,1)} custom-call(s32[1]{0:T(128)} %bitcast.here_ref, bf16[32,2048]{1,0:T(8,128)(2,1)} %copy-done.22, bf16[32,2048]{1,0:T(8,128)(2,1)} %copy-done.26, bf16[32,2048]{1,0:T(8,128)(2,1)} %copy-done.27, bf16[32,2048]{1,0:T(8,128)(2,1)} %copy-done.28), custom_call_target="tpu_custom_call" | custom-call | bytes 174762 | tf_op jit(solution)/shard_map/place_rows/pallas_call | solution.py:591
  110.2 1.4 collective-permute-start.20
  111.5 0.6 collective-permute-start.21
  112.2 8.0 %item_own.1 = (bf16[32,2048]{1,0:T(8,128)(2,1)}, bf16[32,2048]{1,0:T(8,128)(2,1)}, bf16[32,2048]{1,0:T(8,128)(2,1)}, bf16[32,2048]{1,0:T(8,128)(2,1)}) custom-call(s32[1]{0:T(128)} %bitcast.here_ref, bf16[128,2048]{1,0:T(8,128)(2,1)} %place_rows.1.cot.refs_0_.refs_6_, bf16[1024,768]{1,0:T(8,128)(2,1)} %get-tuple-element.93.slope_up.refs_9_.refs_5_, ...), custom_call_target="tpu_custom_call" | custom-call | flops 201326592 | bytes 1833333 | tf_op jit(solution)/shard_map/item_own/pallas_call | solution.py:415
  120.3 0.9 collective-permute-done.21.refs_2_
  121.2 3.8 %add_bitcast_fusion = (f32[128,2304]{1,0:T(8,128)}, bf16[1,128,2304]{2,1,0:T(8,128)(2,1)}, f32[128,2304]{1,0:T(8,128)}, bf16[1,128,2304]{2,1,0:T(8,128)(2,1)}) fusion(bf16[2,128,2304]{2,1,0:T(8,128)(2,1)} %collective-permute-done.13, bf16[2,128,2304]{2,1,0:T(8,128)(2,1)S(1)} %copy-done.4, bf16[2,128,2304]{2,1,0:T(8,128)(2,1)} %collective-permute-done.12, ...), kind=kLoop, calls=%fused_computation | loop fusion | flops 4128768 | bytes 8257536 | tf_op jit(solution)/shard_map/add | solution.py:628
  125.0 0.5 collective-permute-start.27
  125.5 1.7 %collective-permute-start.24 = (bf16[128,2048]{1,0:T(8,128)(2,1)S(1)}, bf16[128,2048]{1,0:T(8,128)(2,1)S(1)}, u32[]{:S(2)}, u32[]{:S(2)}) collective-permute-start(bf16[128,2048]{1,0:T(8,128)(2,1)S(1)} %copy-done), channel_id=1, source_target_pairs={{0,24},{4,28},{8,16},{12,20},{16,8},{20,12},{24,0},{28,4},{1,25},{... | collective-permute-start | bytes 1572872 | tf_op jit(solution)/shard_map/ppermute | solution.py:48
  127.2 0.9 constant_dynamic-slice_fusion
  128.1 4.4 %collective-permute-start.29 = (bf16[32,2048]{1,0:T(8,128)(2,1)}, bf16[32,2048]{1,0:T(8,128)(2,1)S(1)}, u32[]{:S(2)}, u32[]{:S(2)}) collective-permute-start(bf16[32,2048]{1,0:T(8,128)(2,1)} %get-tuple-element.113), channel_id=1, source_target_pairs={{0,1},{1,0},{2,3},{3,2},{4,5},{5,4},{6,7},{7,6},{8,9},{9,8},{10,11... | collective-permute-start | bytes 393224 | tf_op jit(solution)/shard_map/ppermute | solution.py:727
  132.5 1.6 collective-permute-start.30
  134.1 1.5 collective-permute-start.31
  135.6 0.5 collective-permute-start.22
  136.1 0.3 copy-done.18
  136.4 11.2 %item_late.2 = (f32[256,768]{1,0:T(8,128)}, f32[256,768]{1,0:T(8,128)}, f32[768,256]{1,0:T(8,128)}) custom-call(s32[3]{0:T(128)} %pad_add_fusion.place_ref, bf16[128,2048]{1,0:T(8,128)(2,1)} %place_rows.1.cot.refs_0_.refs_6_, bf16[128,2048]{1,0:T(8,128)(2,1)} %collective-permute-done.20.refs_1_, bf16[128,2048]{1,0:T(8,128)(2,1)} %collective-permute-done.21.refs_2_, ...), custom_call_target="tpu_custom_call" | custom-call | flops 1107296256 | bytes 2666666 | tf_op jit(solution)/shard_map/item_late/pallas_call | solution.py:488
  147.8 1.2 collective-permute-start.23
  149.0 0.2 fusion.2
  149.3 0.6 collective-permute-start.32
  150.0 2.4 %collective-permute-start.33 = (bf16[32,2048]{1,0:T(8,128)(2,1)S(1)}, bf16[32,2048]{1,0:T(8,128)(2,1)S(1)}, u32[]{:S(2)}, u32[]{:S(2)}) collective-permute-start(bf16[32,2048]{1,0:T(8,128)(2,1)S(1)} %fusion.6.refs_0_), channel_id=1, source_target_pairs={{0,2},{1,3},{2,0},{3,1},{4,6},{5,7},{6,4},{7,5},{8,10},{9,11},{10,... | collective-permute-start | bytes 393224 | tf_op jit(solution)/shard_map/ppermute | solution.py:734
  152.4 1.5 collective-permute-start.34
  153.8 7.9 %item_late.3 = (f32[256,768]{1,0:T(8,128)}, f32[256,768]{1,0:T(8,128)}, f32[768,256]{1,0:T(8,128)}) custom-call(s32[3]{0:T(128)} %pad_add_fusion.place_ref, bf16[128,2048]{1,0:T(8,128)(2,1)} %copy-done.2, bf16[128,2048]{1,0:T(8,128)(2,1)} %copy-done.19, bf16[128,2048]{1,0:T(8,128)(2,1)} %copy-done.2, bf16[1024,256]{1,0:T(8,128)(2,1)} %get-tuple-element.76.refs_7_.refs_3_, ...), custom_call_target="tpu_custom_call" | custom-call | flops 369098752 | bytes 2666666 | tf_op jit(solution)/shard_map/item_late/pallas_call | solution.py:488
  161.8 0.5 collective-permute-done.23
  162.3 0.6 collective-permute-done.33.refs_2_
  162.9 0.2 copy-done.8
  163.2 0.4 copy-done.24
  163.6 4.0 %final_sums.1 = (bf16[128,2048]{1,0:T(8,128)(2,1)}, f32[256,768]{1,0:T(8,128)}, f32[256,768]{1,0:T(8,128)}, f32[768,256]{1,0:T(8,128)}) custom-call(s32[1]{0:T(128)} %bitcast.here_ref, f32[128,2304]{1,0:T(8,128)} %get-tuple-element.138.kept_a, bf16[128,2304]{1,0:T(8,128)(2,1)} %bitcast.16, f32[128,2304]{1,0:T(8,128)} %get-tuple-element.134.kept_b, ...), custom_call_target="tpu_custom_call" | custom-call | bytes 491520 | tf_op jit(solution)/shard_map/final_sums/pallas_call | solution.py:565
  (106 shorter events, 1.4 us)
Async XLA Ops:
  0.6 24.3 %collective-permute-start = (bf16[128,2048]{1,0:T(8,128)(2,1)}, bf16[128,2048]{1,0:T(8,128)(2,1)S(1)}, u32[]{:S(2)}, u32[]{:S(2)}) collective-permute-start(bf16[128,2048]{1,0:T(8,128)(2,1)} %refs_0_.1), channel_id=1, source_target_pairs={{0,8},{4,12},{8,0},{12,4},{16,24},{20,28},{24,16},{28,20},{1,9},{5... | collective-permute-start | bytes 1572872 | tf_op jit(solution)/shard_map/ppermute | solution.py:48
  3.6 24.8 %collective-permute-start.1 = (bf16[128,2048]{1,0:T(8,128)(2,1)}, bf16[128,2048]{1,0:T(8,128)(2,1)S(1)}, u32[]{:S(2)}, u32[]{:S(2)}) collective-permute-start(bf16[128,2048]{1,0:T(8,128)(2,1)} %refs_0_.1), channel_id=1, source_target_pairs={{0,16},{4,20},{8,24},{12,28},{16,0},{20,4},{24,8},{28,12},{1,17},{... | collective-permute-start | bytes 1572872 | tf_op jit(solution)/shard_map/ppermute | solution.py:48
  5.2 23.3 %collective-permute-start.2 = (bf16[128,2048]{1,0:T(8,128)(2,1)}, bf16[128,2048]{1,0:T(8,128)(2,1)S(1)}, u32[]{:S(2)}, u32[]{:S(2)}) collective-permute-start(bf16[128,2048]{1,0:T(8,128)(2,1)} %refs_0_.1), channel_id=1, source_target_pairs={{0,24},{4,28},{8,16},{12,20},{16,8},{20,12},{24,0},{28,4},{1,25},{... | collective-permute-start | bytes 1572872 | tf_op jit(solution)/shard_map/ppermute | solution.py:48
  25.0 12.5 %copy-start.9 = (bf16[128,2048]{1,0:T(8,128)(2,1)}, bf16[128,2048]{1,0:T(8,128)(2,1)S(1)}, u32[]{:S(2)}) copy-start(bf16[128,2048]{1,0:T(8,128)(2,1)S(1)} %collective-permute-done.refs_1_) | copy-start | bytes 1572868
  28.5 9.3 %copy-start.10 = (bf16[128,2048]{1,0:T(8,128)(2,1)}, bf16[128,2048]{1,0:T(8,128)(2,1)S(1)}, u32[]{:S(2)}) copy-start(bf16[128,2048]{1,0:T(8,128)(2,1)S(1)} %collective-permute-done.1.refs_2_) | copy-start | bytes 1572868
  28.5 0.9 copy-start.11
  28.5 8.5 %collective-permute-start.3 = (bf16[512,2048]{1,0:T(8,128)(2,1)}, bf16[512,2048]{1,0:T(8,128)(2,1)}, u32[]{:S(2)}, u32[]{:S(2)}) collective-permute-start(bf16[512,2048]{1,0:T(8,128)(2,1)} %get-tuple-element.74), channel_id=1, source_target_pairs={{0,4},{4,0},{8,12},{12,8},{16,20},{20,16},{24,28},{28,24},{1,5},{5... | collective-permute-start | bytes 6291464 | tf_op jit(solution)/shard_map/ppermute | solution.py:48
  29.3 7.9 %copy-start.5 = (bf16[128,2048]{1,0:T(8,128)(2,1)S(1)}, bf16[128,2048]{1,0:T(8,128)(2,1)}, u32[]{:S(2)}) copy-start(bf16[128,2048]{1,0:T(8,128)(2,1)} %refs_0_.1) | copy-start | bytes 1572868
  29.3 8.9 %copy-start.1 = (bf16[512,2048]{1,0:T(8,128)(2,1)S(1)}, bf16[512,2048]{1,0:T(8,128)(2,1)}, u32[]{:S(2)}) copy-start(bf16[512,2048]{1,0:T(8,128)(2,1)} %get-tuple-element.79.kept_ref) | copy-start | bytes 6291460
  37.0 25.8 %collective-permute-start.4 = (bf16[4,256,2304]{2,1,0:T(8,128)(2,1)}, bf16[4,256,2304]{2,1,0:T(8,128)(2,1)}, u32[]{:S(2)}, u32[]{:S(2)}) collective-permute-start(bf16[4,256,2304]{2,1,0:T(8,128)(2,1)} %sent_grads.1), channel_id=1, source_target_pairs={{0,4},{4,0},{8,12},{12,8},{16,20},{20,16},{24,28},{28,24},{1,5},{5... | collective-permute-start | bytes 14155784 | tf_op jit(solution)/shard_map/ppermute | solution.py:48
  37.2 5.2 %collective-permute-start.5 = (bf16[128,2048]{1,0:T(8,128)(2,1)S(1)}, bf16[128,2048]{1,0:T(8,128)(2,1)S(1)}, u32[]{:S(2)}, u32[]{:S(2)}) collective-permute-start(bf16[128,2048]{1,0:T(8,128)(2,1)S(1)} %copy-done.5), channel_id=1, source_target_pairs={{0,4},{4,0},{8,12},{12,8},{16,20},{20,16},{24,28},{28,24},{1,5},{5... | collective-permute-start | bytes 1572872 | tf_op jit(solution)/shard_map/ppermute | solution.py:48
  37.5 6.4 %collective-permute-start.6 = (bf16[128,2048]{1,0:T(8,128)(2,1)S(1)}, bf16[128,2048]{1,0:T(8,128)(2,1)S(1)}, u32[]{:S(2)}, u32[]{:S(2)}) collective-permute-start(bf16[128,2048]{1,0:T(8,128)(2,1)S(1)} %collective-permute-done.refs_1_), channel_id=1, source_target_pairs={{0,4},{4,0},{8,12},{12,8},{16,20},{20,16},{24,28},{28,24},{1,5},{5... | collective-permute-start | bytes 1572872 | tf_op jit(solution)/shard_map/ppermute | solution.py:48
  37.7 7.7 %collective-permute-start.7 = (bf16[128,2048]{1,0:T(8,128)(2,1)S(1)}, bf16[128,2048]{1,0:T(8,128)(2,1)S(1)}, u32[]{:S(2)}, u32[]{:S(2)}) collective-permute-start(bf16[128,2048]{1,0:T(8,128)(2,1)S(1)} %collective-permute-done.1.refs_2_), channel_id=1, source_target_pairs={{0,4},{4,0},{8,12},{12,8},{16,20},{20,16},{24,28},{28,24},{1,5},{5... | collective-permute-start | bytes 1572872 | tf_op jit(solution)/shard_map/ppermute | solution.py:48
  38.0 10.3 %collective-permute-start.8 = (bf16[128,2048]{1,0:T(8,128)(2,1)}, bf16[128,2048]{1,0:T(8,128)(2,1)}, u32[]{:S(2)}, u32[]{:S(2)}) collective-permute-start(bf16[128,2048]{1,0:T(8,128)(2,1)} %copy-done.11), channel_id=1, source_target_pairs={{0,4},{4,0},{8,12},{12,8},{16,20},{20,16},{24,28},{28,24},{1,5},{5... | collective-permute-start | bytes 1572872 | tf_op jit(solution)/shard_map/ppermute | solution.py:48
  38.2 9.4 %copy-start.36 = (s32[4]{0:T(128)S(1)}, s32[4]{0:T(128)}, u32[]{:S(2)}) copy-start(s32[4]{0:T(128)} %constant.60.clone) | copy-start | bytes 52
  38.2 9.4 %copy-start.30 = (s32[1,4]{1,0:T(1,128)S(1)}, s32[1,4]{1,0:T(1,128)}, u32[]{:S(2)}) copy-start(s32[1,4]{1,0:T(1,128)} %constant.67) | copy-start | bytes 52
  38.2 9.4 %copy-start.31 = (s32[1,4]{1,0:T(1,128)S(1)}, s32[1,4]{1,0:T(1,128)}, u32[]{:S(2)}) copy-start(s32[1,4]{1,0:T(1,128)} %constant.66) | copy-start | bytes 52
  38.3 9.4 %copy-start.32 = (s32[1,4]{1,0:T(1,128)S(1)}, s32[1,4]{1,0:T(1,128)}, u32[]{:S(2)}) copy-start(s32[1,4]{1,0:T(1,128)} %constant.68) | copy-start | bytes 52
  38.3 9.4 %copy-start.33 = (s32[1,4]{1,0:T(1,128)S(1)}, s32[1,4]{1,0:T(1,128)}, u32[]{:S(2)}) copy-start(s32[1,4]{1,0:T(1,128)} %constant.69) | copy-start | bytes 52
  38.3 9.4 %copy-start.34 = (s32[1,4]{1,0:T(1,128)S(1)}, s32[1,4]{1,0:T(1,128)}, u32[]{:S(2)}) copy-start(s32[1,4]{1,0:T(1,128)} %constant.70) | copy-start | bytes 52
  38.3 9.4 %copy-start.35 = (s32[1,4]{1,0:T(1,128)S(1)}, s32[1,4]{1,0:T(1,128)}, u32[]{:S(2)}) copy-start(s32[1,4]{1,0:T(1,128)} %constant.71) | copy-start | bytes 52
  42.4 3.0 %copy-start.15 = (bf16[128,2048]{1,0:T(8,128)(2,1)}, bf16[128,2048]{1,0:T(8,128)(2,1)S(1)}, u32[]{:S(2)}) copy-start(bf16[128,2048]{1,0:T(8,128)(2,1)S(1)} %collective-permute-done.5.refs_4_) | copy-start | bytes 1572868
  42.4 30.1 %collective-permute-start.9 = (bf16[128,2048]{1,0:T(8,128)(2,1)}, bf16[128,2048]{1,0:T(8,128)(2,1)S(1)}, u32[]{:S(2)}, u32[]{:S(2)}) collective-permute-start(bf16[128,2048]{1,0:T(8,128)(2,1)} %get-tuple-element.133), channel_id=1, source_target_pairs={{0,8},{4,12},{8,0},{12,4},{16,24},{20,28},{24,16},{28,20},{1,9},{5... | collective-permute-start | bytes 1572872 | tf_op jit(solution)/shard_map/ppermute | solution.py:48
  43.9 1.5 copy-start.16
  43.9 28.6 %collective-permute-start.10 = (bf16[128,2048]{1,0:T(8,128)(2,1)}, bf16[128,2048]{1,0:T(8,128)(2,1)S(1)}, u32[]{:S(2)}, u32[]{:S(2)}) collective-permute-start(bf16[128,2048]{1,0:T(8,128)(2,1)} %get-tuple-element.132), channel_id=1, source_target_pairs={{0,16},{4,20},{8,24},{12,28},{16,0},{20,4},{24,8},{28,12},{1,17},{... | collective-permute-start | bytes 1572872 | tf_op jit(solution)/shard_map/ppermute | solution.py:48
  46.2 26.3 %collective-permute-start.11 = (bf16[128,2048]{1,0:T(8,128)(2,1)}, bf16[128,2048]{1,0:T(8,128)(2,1)S(1)}, u32[]{:S(2)}, u32[]{:S(2)}) collective-permute-start(bf16[128,2048]{1,0:T(8,128)(2,1)} %get-tuple-element.131), channel_id=1, source_target_pairs={{0,24},{4,28},{8,16},{12,20},{16,8},{20,12},{24,0},{28,4},{1,25},{... | collective-permute-start | bytes 1572872 | tf_op jit(solution)/shard_map/ppermute | solution.py:48
  72.5 0.9 copy-start.13
  72.6 1.1 copy-start.14
  76.7 7.6 %collective-permute-start.14 = (bf16[32,2048]{1,0:T(8,128)(2,1)}, bf16[32,2048]{1,0:T(8,128)(2,1)S(1)}, u32[]{:S(2)}, u32[]{:S(2)}) collective-permute-start(bf16[32,2048]{1,0:T(8,128)(2,1)} %get-tuple-element.90), channel_id=1, source_target_pairs={{0,1},{1,0},{2,3},{3,2},{4,5},{5,4},{6,7},{7,6},{8,9},{9,8},{10,11... | collective-permute-start | bytes 393224 | tf_op jit(solution)/shard_map/ppermute | solution.py:727
  78.3 13.1 %collective-permute-start.15 = (bf16[32,2048]{1,0:T(8,128)(2,1)}, bf16[32,2048]{1,0:T(8,128)(2,1)S(1)}, u32[]{:S(2)}, u32[]{:S(2)}) collective-permute-start(bf16[32,2048]{1,0:T(8,128)(2,1)} %get-tuple-element.91), channel_id=1, source_target_pairs={{0,2},{1,3},{2,0},{3,1},{4,6},{5,7},{6,4},{7,5},{8,10},{9,11},{10,... | collective-permute-start | bytes 393224 | tf_op jit(solution)/shard_map/ppermute | solution.py:727
  80.9 10.5 %collective-permute-start.16 = (bf16[32,2048]{1,0:T(8,128)(2,1)}, bf16[32,2048]{1,0:T(8,128)(2,1)S(1)}, u32[]{:S(2)}, u32[]{:S(2)}) collective-permute-start(bf16[32,2048]{1,0:T(8,128)(2,1)} %get-tuple-element.92), channel_id=1, source_target_pairs={{0,3},{1,2},{2,1},{3,0},{4,7},{5,6},{6,5},{7,4},{8,11},{9,10},{10,... | collective-permute-start | bytes 393224 | tf_op jit(solution)/shard_map/ppermute | solution.py:727
  81.1 40.0 %collective-permute-start.12 = (bf16[2,128,2304]{2,1,0:T(8,128)(2,1)}, bf16[2,128,2304]{2,1,0:T(8,128)(2,1)}, u32[]{:S(2)}, u32[]{:S(2)}) collective-permute-start(bf16[2,128,2304]{2,1,0:T(8,128)(2,1)} %get-tuple-element.87), channel_id=1, source_target_pairs={{0,8},{4,12},{8,0},{12,4},{16,24},{20,28},{24,16},{28,20},{1,9},{5... | collective-permute-start | bytes 3538952 | tf_op jit(solution)/shard_map/ppermute | solution.py:48
  82.6 38.6 %collective-permute-start.13 = (bf16[2,128,2304]{2,1,0:T(8,128)(2,1)}, bf16[2,128,2304]{2,1,0:T(8,128)(2,1)}, u32[]{:S(2)}, u32[]{:S(2)}) collective-permute-start(bf16[2,128,2304]{2,1,0:T(8,128)(2,1)} %get-tuple-element.88), channel_id=1, source_target_pairs={{0,16},{4,20},{8,24},{12,28},{16,0},{20,4},{24,8},{28,12},{1,17},{... | collective-permute-start | bytes 3538952 | tf_op jit(solution)/shard_map/ppermute | solution.py:48
  92.4 14.5 %copy-start.22 = (bf16[32,2048]{1,0:T(8,128)(2,1)}, bf16[32,2048]{1,0:T(8,128)(2,1)S(1)}, u32[]{:S(2)}) copy-start(bf16[32,2048]{1,0:T(8,128)(2,1)S(1)} %get-tuple-element.129.refs_0_) | copy-start | bytes 393220
  92.4 6.6 %collective-permute-start.17 = (bf16[32,2048]{1,0:T(8,128)(2,1)S(1)}, bf16[32,2048]{1,0:T(8,128)(2,1)S(1)}, u32[]{:S(2)}, u32[]{:S(2)}) collective-permute-start(bf16[32,2048]{1,0:T(8,128)(2,1)S(1)} %get-tuple-element.129.refs_0_), channel_id=1, source_target_pairs={{0,1},{1,0},{2,3},{3,2},{4,5},{5,4},{6,7},{7,6},{8,9},{9,8},{10,11... | collective-permute-start | bytes 393224 | tf_op jit(solution)/shard_map/ppermute | solution.py:734
  94.7 12.2 %collective-permute-start.18 = (bf16[32,2048]{1,0:T(8,128)(2,1)S(1)}, bf16[32,2048]{1,0:T(8,128)(2,1)S(1)}, u32[]{:S(2)}, u32[]{:S(2)}) collective-permute-start(bf16[32,2048]{1,0:T(8,128)(2,1)S(1)} %get-tuple-element.129.refs_0_), channel_id=1, source_target_pairs={{0,2},{1,3},{2,0},{3,1},{4,6},{5,7},{6,4},{7,5},{8,10},{9,11},{10,... | collective-permute-start | bytes 393224 | tf_op jit(solution)/shard_map/ppermute | solution.py:734
  95.8 11.1 %collective-permute-start.19 = (bf16[32,2048]{1,0:T(8,128)(2,1)S(1)}, bf16[32,2048]{1,0:T(8,128)(2,1)S(1)}, u32[]{:S(2)}, u32[]{:S(2)}) collective-permute-start(bf16[32,2048]{1,0:T(8,128)(2,1)S(1)} %get-tuple-element.129.refs_0_), channel_id=1, source_target_pairs={{0,3},{1,2},{2,1},{3,0},{4,7},{5,6},{6,5},{7,4},{8,11},{9,10},{10,... | collective-permute-start | bytes 393224 | tf_op jit(solution)/shard_map/ppermute | solution.py:734
  99.0 7.9 %copy-start.26 = (bf16[32,2048]{1,0:T(8,128)(2,1)}, bf16[32,2048]{1,0:T(8,128)(2,1)S(1)}, u32[]{:S(2)}) copy-start(bf16[32,2048]{1,0:T(8,128)(2,1)S(1)} %collective-permute-done.17.refs_1_) | copy-start | bytes 393220
  110.2 10.1 %collective-permute-start.20 = (bf16[128,2048]{1,0:T(8,128)(2,1)}, bf16[128,2048]{1,0:T(8,128)(2,1)}, u32[]{:S(2)}, u32[]{:S(2)}) collective-permute-start(bf16[128,2048]{1,0:T(8,128)(2,1)} %place_rows.1.cot.refs_0_.refs_6_), channel_id=1, source_target_pairs={{0,8},{4,12},{8,0},{12,4},{16,24},{20,28},{24,16},{28,20},{1,9},{5... | collective-permute-start | bytes 1572872 | tf_op jit(solution)/shard_map/ppermute | solution.py:48
  111.5 9.6 %collective-permute-start.21 = (bf16[128,2048]{1,0:T(8,128)(2,1)}, bf16[128,2048]{1,0:T(8,128)(2,1)}, u32[]{:S(2)}, u32[]{:S(2)}) collective-permute-start(bf16[128,2048]{1,0:T(8,128)(2,1)} %place_rows.1.cot.refs_0_.refs_6_), channel_id=1, source_target_pairs={{0,16},{4,20},{8,24},{12,28},{16,0},{20,4},{24,8},{28,12},{1,17},{... | collective-permute-start | bytes 1572872 | tf_op jit(solution)/shard_map/ppermute | solution.py:48
  112.2 20.3 %collective-permute-start.26 = (bf16[128,2048]{1,0:T(8,128)(2,1)}, bf16[128,2048]{1,0:T(8,128)(2,1)}, u32[]{:S(2)}, u32[]{:S(2)}) collective-permute-start(bf16[128,2048]{1,0:T(8,128)(2,1)} %place_rows.1.cot.refs_0_.refs_6_), channel_id=1, source_target_pairs={{0,4},{4,0},{8,12},{12,8},{16,20},{20,16},{24,28},{28,24},{1,5},{5... | collective-permute-start | bytes 1572872 | tf_op jit(solution)/shard_map/ppermute | solution.py:48
  112.2 8.9 %copy-start.3 = (bf16[2,128,2304]{2,1,0:T(8,128)(2,1)S(1)}, bf16[2,128,2304]{2,1,0:T(8,128)(2,1)}, u32[]{:S(2)}) copy-start(bf16[2,128,2304]{2,1,0:T(8,128)(2,1)} %get-tuple-element.78) | copy-start | bytes 3538948
  112.2 8.9 %copy-start.4 = (bf16[2,128,2304]{2,1,0:T(8,128)(2,1)S(1)}, bf16[2,128,2304]{2,1,0:T(8,128)(2,1)}, u32[]{:S(2)}) copy-start(bf16[2,128,2304]{2,1,0:T(8,128)(2,1)} %get-tuple-element.97) | copy-start | bytes 3538948
  121.1 13.0 %collective-permute-start.28 = (bf16[128,2048]{1,0:T(8,128)(2,1)}, bf16[128,2048]{1,0:T(8,128)(2,1)}, u32[]{:S(2)}, u32[]{:S(2)}) collective-permute-start(bf16[128,2048]{1,0:T(8,128)(2,1)} %collective-permute-done.21.refs_2_), channel_id=1, source_target_pairs={{0,4},{4,0},{8,12},{12,8},{16,20},{20,16},{24,28},{28,24},{1,5},{5... | collective-permute-start | bytes 1572872 | tf_op jit(solution)/shard_map/ppermute | solution.py:48
  121.2 4.3 %copy-start = (bf16[128,2048]{1,0:T(8,128)(2,1)S(1)}, bf16[128,2048]{1,0:T(8,128)(2,1)}, u32[]{:S(2)}) copy-start(bf16[128,2048]{1,0:T(8,128)(2,1)} %place_rows.1.cot.refs_0_.refs_6_) | copy-start | bytes 1572868
  121.2 6.9 %copy-start.29 = (bf16[2048]{0:T(1024)(128)(2,1)S(1)}, bf16[2048]{0:T(1024)(128)(2,1)}, u32[]{:S(2)}) copy-start(bf16[2048]{0:T(1024)(128)(2,1)} %gain_ref.3) | copy-start | bytes 12292
  121.2 13.0 %copy-start.37 = (bf16[32,2048]{1,0:T(8,128)(2,1)S(1)}, bf16[32,2048]{1,0:T(8,128)(2,1)}, u32[]{:S(2)}) copy-start(bf16[32,2048]{1,0:T(8,128)(2,1)} %get-tuple-element.115) | copy-start | bytes 393220
  125.0 10.6 %collective-permute-start.27 = (bf16[128,2048]{1,0:T(8,128)(2,1)}, bf16[128,2048]{1,0:T(8,128)(2,1)S(1)}, u32[]{:S(2)}, u32[]{:S(2)}) collective-permute-start(bf16[128,2048]{1,0:T(8,128)(2,1)} %collective-permute-done.20.refs_1_), channel_id=1, source_target_pairs={{0,4},{4,0},{8,12},{12,8},{16,20},{20,16},{24,28},{28,24},{1,5},{5... | collective-permute-start | bytes 1572872 | tf_op jit(solution)/shard_map/ppermute | solution.py:48
  125.5 23.5 %collective-permute-start.24 = (bf16[128,2048]{1,0:T(8,128)(2,1)S(1)}, bf16[128,2048]{1,0:T(8,128)(2,1)S(1)}, u32[]{:S(2)}, u32[]{:S(2)}) collective-permute-start(bf16[128,2048]{1,0:T(8,128)(2,1)S(1)} %copy-done), channel_id=1, source_target_pairs={{0,24},{4,28},{8,16},{12,20},{16,8},{20,12},{24,0},{28,4},{1,25},{... | collective-permute-start | bytes 1572872 | tf_op jit(solution)/shard_map/ppermute | solution.py:48
  128.1 19.7 %collective-permute-start.29 = (bf16[32,2048]{1,0:T(8,128)(2,1)}, bf16[32,2048]{1,0:T(8,128)(2,1)S(1)}, u32[]{:S(2)}, u32[]{:S(2)}) collective-permute-start(bf16[32,2048]{1,0:T(8,128)(2,1)} %get-tuple-element.113), channel_id=1, source_target_pairs={{0,1},{1,0},{2,3},{3,2},{4,5},{5,4},{6,7},{7,6},{8,9},{9,8},{10,11... | collective-permute-start | bytes 393224 | tf_op jit(solution)/shard_map/ppermute | solution.py:727
  132.5 16.4 %collective-permute-start.30 = (bf16[32,2048]{1,0:T(8,128)(2,1)}, bf16[32,2048]{1,0:T(8,128)(2,1)S(1)}, u32[]{:S(2)}, u32[]{:S(2)}) collective-permute-start(bf16[32,2048]{1,0:T(8,128)(2,1)} %get-tuple-element.114), channel_id=1, source_target_pairs={{0,2},{1,3},{2,0},{3,1},{4,6},{5,7},{6,4},{7,5},{8,10},{9,11},{10,... | collective-permute-start | bytes 393224 | tf_op jit(solution)/shard_map/ppermute | solution.py:727
  134.1 14.8 %collective-permute-start.31 = (bf16[32,2048]{1,0:T(8,128)(2,1)S(1)}, bf16[32,2048]{1,0:T(8,128)(2,1)S(1)}, u32[]{:S(2)}, u32[]{:S(2)}) collective-permute-start(bf16[32,2048]{1,0:T(8,128)(2,1)S(1)} %copy-done.37), channel_id=1, source_target_pairs={{0,3},{1,2},{2,1},{3,0},{4,7},{5,6},{6,5},{7,4},{8,11},{9,10},{10,... | collective-permute-start | bytes 393224 | tf_op jit(solution)/shard_map/ppermute | solution.py:727
  135.6 26.2 %collective-permute-start.22 = (bf16[1,128,2304]{2,1,0:T(8,128)(2,1)}, bf16[1,128,2304]{2,1,0:T(8,128)(2,1)S(1)}, u32[]{:S(2)}, u32[]{:S(2)}) collective-permute-start(bf16[1,128,2304]{2,1,0:T(8,128)(2,1)} %get-tuple-element.100), channel_id=1, source_target_pairs={{0,16},{4,20},{8,24},{12,28},{16,0},{20,4},{24,8},{28,12},{1,17},{... | collective-permute-start | bytes 1769480 | tf_op jit(solution)/shard_map/ppermute | solution.py:48
  136.4 11.4 %copy-start.6 = (bf16[1,128,2304]{2,1,0:T(8,128)(2,1)S(1)}, bf16[1,128,2304]{2,1,0:T(8,128)(2,1)}, u32[]{:S(2)}) copy-start(bf16[1,128,2304]{2,1,0:T(8,128)(2,1)} %get-tuple-element.101) | copy-start | bytes 1769476
  136.4 12.6 %copy-start.21 = (bf16[32,2048]{1,0:T(8,128)(2,1)S(1)}, bf16[32,2048]{1,0:T(8,128)(2,1)}, u32[]{:S(2)}) copy-start(bf16[32,2048]{1,0:T(8,128)(2,1)} %get-tuple-element.95) | copy-start | bytes 393220
  147.8 14.5 %collective-permute-start.23 = (bf16[1,128,2304]{2,1,0:T(8,128)(2,1)S(1)}, bf16[1,128,2304]{2,1,0:T(8,128)(2,1)S(1)}, u32[]{:S(2)}, u32[]{:S(2)}) collective-permute-start(bf16[1,128,2304]{2,1,0:T(8,128)(2,1)S(1)} %copy-done.6), channel_id=1, source_target_pairs={{0,8},{4,12},{8,0},{12,4},{16,24},{20,28},{24,16},{28,20},{1,9},{5... | collective-permute-start | bytes 1769480 | tf_op jit(solution)/shard_map/ppermute | solution.py:48
  148.9 4.9 %copy-start.2 = (bf16[128,2048]{1,0:T(8,128)(2,1)}, bf16[128,2048]{1,0:T(8,128)(2,1)S(1)}, u32[]{:S(2)}) copy-start(bf16[128,2048]{1,0:T(8,128)(2,1)S(1)} %collective-permute-done.24.refs_0_.refs_2_) | copy-start | bytes 1572868
  148.9 3.4 %collective-permute-start.25 = (bf16[128,2048]{1,0:T(8,128)(2,1)S(1)}, bf16[128,2048]{1,0:T(8,128)(2,1)S(1)}, u32[]{:S(2)}, u32[]{:S(2)}) collective-permute-start(bf16[128,2048]{1,0:T(8,128)(2,1)S(1)} %collective-permute-done.24.refs_0_.refs_2_), channel_id=1, source_target_pairs={{0,4},{4,0},{8,12},{12,8},{16,20},{20,16},{24,28},{28,24},{1,5},{5... | collective-permute-start | bytes 1572872 | tf_op jit(solution)/shard_map/ppermute | solution.py:48
  149.3 12.4 %copy-start.20 = (bf16[32,2048]{1,0:T(8,128)(2,1)}, bf16[32,2048]{1,0:T(8,128)(2,1)S(1)}, u32[]{:S(2)}) copy-start(bf16[32,2048]{1,0:T(8,128)(2,1)S(1)} %fusion.6.refs_0_) | copy-start | bytes 393220
  149.3 12.9 %collective-permute-start.32 = (bf16[32,2048]{1,0:T(8,128)(2,1)S(1)}, bf16[32,2048]{1,0:T(8,128)(2,1)S(1)}, u32[]{:S(2)}, u32[]{:S(2)}) collective-permute-start(bf16[32,2048]{1,0:T(8,128)(2,1)S(1)} %fusion.6.refs_0_), channel_id=1, source_target_pairs={{0,1},{1,0},{2,3},{3,2},{4,5},{5,4},{6,7},{7,6},{8,9},{9,8},{10,11... | collective-permute-start | bytes 393224 | tf_op jit(solution)/shard_map/ppermute | solution.py:734
  150.0 12.9 %collective-permute-start.33 = (bf16[32,2048]{1,0:T(8,128)(2,1)S(1)}, bf16[32,2048]{1,0:T(8,128)(2,1)S(1)}, u32[]{:S(2)}, u32[]{:S(2)}) collective-permute-start(bf16[32,2048]{1,0:T(8,128)(2,1)S(1)} %fusion.6.refs_0_), channel_id=1, source_target_pairs={{0,2},{1,3},{2,0},{3,1},{4,6},{5,7},{6,4},{7,5},{8,10},{9,11},{10,... | collective-permute-start | bytes 393224 | tf_op jit(solution)/shard_map/ppermute | solution.py:734
  152.3 1.5 copy-start.19
  152.4 10.5 %collective-permute-start.34 = (bf16[32,2048]{1,0:T(8,128)(2,1)S(1)}, bf16[32,2048]{1,0:T(8,128)(2,1)S(1)}, u32[]{:S(2)}, u32[]{:S(2)}) collective-permute-start(bf16[32,2048]{1,0:T(8,128)(2,1)S(1)} %fusion.6.refs_0_), channel_id=1, source_target_pairs={{0,3},{1,2},{2,1},{3,0},{4,7},{5,6},{6,5},{7,4},{8,11},{9,10},{10,... | collective-permute-start | bytes 393224 | tf_op jit(solution)/shard_map/ppermute | solution.py:734
  161.8 1.1 copy-start.7
  (9 other events, 6.8 us)

commit v4 on v3

--- a/solution.py
+++ b/solution.py
@@ -2,6 +2,7 @@
 
 import jax
 import jax.numpy as jnp
+import numpy as np
 from jax import lax
 from jax.experimental import pallas as pl
 from jax.experimental.pallas import tpu as pltpu
@@ -66,8 +67,8 @@
 def user_kernel(
     share, item_dev, place_ref, hist_len_ref, x_hbm, og_hbm, hist_ref, item_row_ref, gain_ref,
     gate_hbm, up_hbm, down_hbm,
-    normed_out, masked_out, hidden_out, d_gate_out, d_up_out, sent_out, kept_out,
-    x, og, gate, up, down, normed, hidden, d_gate, d_up, gate_act, up_act, total, sent, kept, inv_ref,
+    normed_out, masked_out, hidden_out, d_both_out, sent_out, kept_out,
+    x, og, gate, up, down, normed, hidden, d_both, gate_act, up_act, total, sent, kept, inv_ref,
     sems,
 ):
     loads = [
@@ -85,8 +86,7 @@
                 (normed, normed_out),
                 (og, masked_out),
                 (hidden, hidden_out),
-                (d_gate, d_gate_out),
-                (d_up, d_up_out),
+                (d_both, d_both_out),
             )
         )
     ]
@@ -133,14 +133,14 @@
         sig = 1.0 / (1.0 + jnp.exp(-gate_part))
         silu = gate_part * sig
         hidden[:, at] = (silu * up_part).astype(BF16)
-        d_up[:, at] = (d_hidden * silu).astype(BF16)
-        d_gate[:, at] = (d_hidden * up_part * sig * (1.0 + gate_part * (1.0 - sig))).astype(BF16)
-    for k in (2, 3, 4):
+        d_both[:, hid + at.start : hid + at.stop] = (d_hidden * silu).astype(BF16)
+        d_both[:, at] = (d_hidden * up_part * sig * (1.0 + gate_part * (1.0 - sig))).astype(BF16)
+    for k in (2, 3):
         stores[k].start()
     mean = jnp.zeros((rows, 1), F32)
     inv = inv_ref[...]
     for at in tiles(width, 512):
-        part = mm(d_gate[...], gate[at, :], LAST) + mm(d_up[...], up[at, :], LAST)
+        part = mm(d_both[:, :hid], gate[at, :], LAST) + mm(d_both[:, hid:], up[at, :], LAST)
         part = part * gain[:, at]
         total[:, at] = part
         mean = mean + jnp.sum(part * (x[:, at].astype(F32) * inv), axis=1, keepdims=True)
@@ -172,8 +172,8 @@
     return pl.pallas_call(
         functools.partial(user_kernel, share, item_dev),
         in_specs=[smem()] * 2 + [hbm()] * 2 + [vmem()] * 3 + [hbm()] * 3,
-        out_specs=[hbm()] * 7,
-        out_shape=[wide, wide, narrow, narrow, narrow, summed, summed],
+        out_specs=[hbm()] * 6,
+        out_shape=[wide, wide, narrow, jax.ShapeDtypeStruct((rows, 2 * hid), BF16), summed, summed],
         scratch_shapes=[
             pltpu.VMEM((rows, width), BF16),
             pltpu.VMEM((rows, width), BF16),
@@ -182,8 +182,7 @@
             pltpu.VMEM((hid, width), BF16),
             pltpu.VMEM((rows, width), BF16),
             pltpu.VMEM((rows, hid), BF16),
-            pltpu.VMEM((rows, hid), BF16),
-            pltpu.VMEM((rows, hid), BF16),
+            pltpu.VMEM((rows, 2 * hid), BF16),
             pltpu.VMEM((rows, hid), F32),
             pltpu.VMEM((rows, hid), F32),
             pltpu.VMEM((rows, width), F32),
@@ -198,33 +197,30 @@
     )(place, hist_len, x, og, hist, item_row, gain, w_gate, w_up, w_down)
 
 
-def grad_rows(normed_ref, masked_ref, d_gate_ref, d_up_ref, hidden_ref):
-    left, right = normed_ref[...], masked_ref[...]
+def grad_rows(normed_ref, masked_ref, d_both_ref, hidden_ref):
     return (
-        mm(left, d_gate_ref[...], FIRST),
-        mm(left, d_up_ref[...], FIRST),
-        mm(right, hidden_ref[...], FIRST),
-    )
-
-
-def sent_kernel(table_ref, normed_ref, masked_ref, d_gate_ref, d_up_ref, hidden_ref, out_ref):
-    hid = hidden_ref.shape[1]
-    found = grad_rows(normed_ref, masked_ref, d_gate_ref, d_up_ref, hidden_ref)
-    for k, piece in enumerate(found):
-        out_ref[0, :, k * hid : (k + 1) * hid] = piece.astype(BF16)
+        mm(normed_ref[...], d_both_ref[...], FIRST),
+        mm(masked_ref[...], hidden_ref[...], FIRST),
+    )
+
+
+def sent_kernel(table_ref, normed_ref, masked_ref, d_both_ref, hidden_ref, out_ref):
+    cut = d_both_ref.shape[1]
+    both, down = grad_rows(normed_ref, masked_ref, d_both_ref, hidden_ref)
+    out_ref[0, :, :cut] = both.astype(BF16)
+    out_ref[0, :, cut:] = down.astype(BF16)
 
 
 def kept_kernel(
-    table_ref, normed_ref, masked_ref, d_gate_ref, d_up_ref, hidden_ref, got_ref,
+    place_ref, table_ref, normed_ref, masked_ref, d_both_ref, hidden_ref, got_ref,
     sent_a, kept_a, sent_b, kept_b,
 ):
     step = pl.program_id(0)
     hid = hidden_ref.shape[1]
     cut = got_ref.shape[1] // 2
-    found = grad_rows(normed_ref, masked_ref, d_gate_ref, d_up_ref, hidden_ref)
+    found = grad_rows(normed_ref, masked_ref, d_both_ref, hidden_ref)
     for first, sent, kept, flag in ((0, sent_a, kept_a, 3), (cut, sent_b, kept_b, 6)):
-        for k, piece in enumerate(found):
-            at = slice(k * hid, (k + 1) * hid)
+        for piece, at in zip(found, (slice(0, 2 * hid), slice(2 * hid, 3 * hid))):
             value = piece[first : first + cut] + got_ref[0, first : first + cut, at].astype(F32)
             value = value.astype(BF16)
 
@@ -237,80 +233,86 @@
                 kept[0, :, at] = value
 
 
-def lhs_specs(rows, block, hid):
+def lhs_specs(rows, block, hid, column_of):
     if block % 128:
-        column = pl.BlockSpec((None, rows, block), lambda s, t: (s, 0, 0))
+        column = pl.BlockSpec((None, rows, block), lambda s, *t: (s, 0, 0))
     else:
-        column = pl.BlockSpec((rows, block), lambda s, t: (0, t[0, s]))
-    return [column, column] + [whole_spec((rows, hid))] * 3
-
-
-def lhs_arrays(table, normed, masked, block):
+        column = pl.BlockSpec((rows, block), lambda s, *t: (0, column_of(s, *t)))
+    return [column, column, whole_spec((rows, 2 * hid)), whole_spec((rows, hid))]
+
+
+def lhs_arrays(columns, normed, masked, block):
     if block % 128 == 0:
         return normed, masked
     return tuple(
-        jnp.take(jnp.swapaxes(a.reshape(a.shape[0], -1, block), 0, 1), table[0], axis=0)
+        jnp.take(jnp.swapaxes(a.reshape(a.shape[0], -1, block), 0, 1), columns, axis=0)
         for a in (normed, masked)
     )
 
 
-def sent_grads(table, normed, masked, d_gate, d_up, hidden, block):
+def sent_grads(place, columns, normed, masked, d_both, hidden, block):
     rows, hid = hidden.shape
-    count = table.shape[1]
+    count = columns.shape[0]
     return pl.pallas_call(
         sent_kernel,
         grid_spec=pltpu.PrefetchScalarGridSpec(
             num_scalar_prefetch=1,
             grid=(count,),
-            in_specs=lhs_specs(rows, block, hid),
+            in_specs=lhs_specs(rows, block, hid, lambda s, t: (t[0] ^ s) * 2 + 1 - t[1]),
             out_specs=pl.BlockSpec((1, block, 3 * hid), lambda s, t: (s, 0, 0)),
         ),
         out_shape=jax.ShapeDtypeStruct((count, block, 3 * hid), BF16),
         compiler_params=params(),
         cost_estimate=cost(6 * rows * block * count * hid, 10e6),
         name="sent_grads",
-    )(table, *lhs_arrays(table, normed, masked, block), d_gate, d_up, hidden)
-
-
-def kept_grads(table, normed, masked, d_gate, d_up, hidden, got, block):
+    )(place, *lhs_arrays(columns, normed, masked, block), d_both, hidden)
+
+
+def kept_grads(place, table, columns, normed, masked, d_both, hidden, got, block):
     rows, hid = hidden.shape
     count = table.shape[1]
     piece = jax.ShapeDtypeStruct((count // 2, block // 2, 3 * hid), BF16)
 
     def out(row):
-        return pl.BlockSpec((1, block // 2, 3 * hid), lambda s, t: (t[row, s], 0, 0))
+        return pl.BlockSpec((1, block // 2, 3 * hid), lambda s, p, t: (t[row, s], 0, 0))
 
     return pl.pallas_call(
         kept_kernel,
         grid_spec=pltpu.PrefetchScalarGridSpec(
-            num_scalar_prefetch=1,
+            num_scalar_prefetch=2,
             grid=(count,),
-            in_specs=lhs_specs(rows, block, hid)
-            + [pl.BlockSpec((1, block, 3 * hid), lambda s, t: (t[7, s], 0, 0))],
+            in_specs=lhs_specs(rows, block, hid, lambda s, p, t: (p[0] ^ t[0, s]) * 2 + p[1])
+            + [pl.BlockSpec((1, block, 3 * hid), lambda s, p, t: (t[0, s], 0, 0))],
             out_specs=[out(1), out(2), out(4), out(5)],
         ),
         out_shape=[piece] * 4,
         compiler_params=params(),
         cost_estimate=cost(6 * rows * block * count * hid, 15e6),
         name="kept_grads",
-    )(table, *lhs_arrays(table, normed, masked, block), d_gate, d_up, hidden, got)
-
-
-def forward_kernel(count, place_ref, gain_ref, *refs):
+    )(place, jnp.asarray(table), *lhs_arrays(columns, normed, masked, block), d_both, hidden, got)
+
+
+def forward_kernel(count, n_narrow, place_ref, gain_ref, *refs):
     feats, (gate_hbm, up_hbm) = refs[:count], refs[count : count + 2]
     normed_out, hidden_out, slope_up_out, slope_gate_out = refs[count + 2 : count + 6]
     x, normed, gate, up, gate_act, hidden, slope_up, slope_gate, sems = refs[count + 6 :]
     width, hid = gate.shape
     all_rows = x.shape[0]
+    first_sem = count + 3 + 3 * len(tiles(hid, TILE))
     rows = all_rows // count
-    pieces = [
-        pltpu.make_async_copy(feats[k], x.at[pl.ds(k * rows, rows)], sems.at[k]) for k in range(count)
-    ]
+    share = rows // n_narrow
+    pieces = []
+    for k in range(count):
+        for j in range(n_narrow):
+            src = feats[k].at[pl.ds(pl.multiple_of((place_ref[3] ^ j) * share, share), share)]
+            to = x.at[pl.ds(k * rows + j * share, share)]
+            pieces.append(pltpu.make_async_copy(src, to, sems.at[first_sem + k * n_narrow + j]))
     gate_load = pltpu.make_async_copy(gate_hbm, gate, sems.at[count])
     up_load = pltpu.make_async_copy(up_hbm, up, sems.at[count + 1])
     halves = [range(count // 2), range(count // 2, count)]
     for k in halves[0]:
-        pieces[k].start()
+        for j in range(n_narrow):
+            pieces[k * n_narrow + j].start()
     gate_load.start()
     gain = gain_ref[...].reshape(1, width).astype(F32)
 
@@ -322,9 +324,11 @@
             normed[at, :] = (part * inv * gain).astype(BF16)
 
     for k in halves[0]:
-        pieces[k].wait()
+        for j in range(n_narrow):
+            pieces[k * n_narrow + j].wait()
     for k in halves[1]:
-        pieces[k].start()
+        for j in range(n_narrow):
+            pieces[k * n_narrow + j].start()
     up_load.start()
     for k in halves[0]:
         normalise(k)
@@ -333,7 +337,8 @@
         part = slice(h * all_rows // 2, (h + 1) * all_rows // 2)
         if h == 1:
             for k in halves[1]:
-                pieces[k].wait()
+                for j in range(n_narrow):
+                    pieces[k * n_narrow + j].wait()
             for k in halves[1]:
                 normalise(k)
         for at in tiles(hid, TILE):
@@ -361,14 +366,14 @@
         store.wait()
 
 
-def item_forward(place, gain, feats, w_gate, w_up, block):
+def item_forward(place, gain, feats, w_gate, w_up, block, n_narrow):
     count = len(feats)
     rows, width = count * feats[0].shape[0], feats[0].shape[1]
     hid = w_gate.shape[1]
     kept = width if block % 128 else block
     narrow = jax.ShapeDtypeStruct((rows, hid), BF16)
     return pl.pallas_call(
-        functools.partial(forward_kernel, count),
+        functools.partial(forward_kernel, count, n_narrow),
         in_specs=[smem(), vmem()] + [hbm()] * (count + 2),
         out_specs=[hbm()] * 4,
         out_shape=[jax.ShapeDtypeStruct((rows, kept), BF16)] + [narrow] * 3,
@@ -381,7 +386,7 @@
             pltpu.VMEM((rows, hid), BF16),
             pltpu.VMEM((rows, hid), BF16),
             pltpu.VMEM((rows, hid), BF16),
-            pltpu.SemaphoreType.DMA((count + 3 + 3 * len(tiles(hid, TILE)),)),
+            pltpu.SemaphoreType.DMA((count + 3 + 3 * len(tiles(hid, TILE)) + count * n_narrow,)),
         ],
         compiler_params=params(),
         cost_estimate=cost(4 * rows * width * hid, 16e6),
@@ -389,7 +394,7 @@
     )(place, gain, *feats, w_gate, w_up)
 
 
-def own_kernel(here_ref, cot, slope_up, slope_gate, gate_hbm, up_hbm, down_hbm, *refs):
+def own_kernel(cot, slope_up, slope_gate, gate_hbm, up_hbm, down_hbm, *refs):
     outs, (total, gate, up, down, sems) = refs[:-5], refs[-5:]
     loads = [
         pltpu.make_async_copy(src, dst, sems.at[k])
@@ -405,17 +410,19 @@
     loads[2].wait()
     for at in tiles(total.shape[1], 512):
         total[:, at] = (mm(d_gate, gate[at, :], LAST) + mm(d_up, up[at, :], LAST)).astype(BF16)
-    cut_rows(here_ref[0], total, outs)
-
-
-def item_own(here, cot, slope_up, slope_gate, w_gate, w_up, w_down, n_narrow):
+    share = outs[0].shape[0]
+    for k, out in enumerate(outs):
+        out[...] = total[k * share : (k + 1) * share, :]
+
+
+def item_own(cot, slope_up, slope_gate, w_gate, w_up, w_down, n_narrow):
     rows, width = cot.shape
     hid = w_gate.shape[1]
     part = (rows // n_narrow, width)
     return pl.pallas_call(
         own_kernel,
         grid=(1,),
-        in_specs=[smem(), whole_spec((rows, width)), whole_spec((rows, hid)), whole_spec((rows, hid))]
+        in_specs=[whole_spec((rows, width)), whole_spec((rows, hid)), whole_spec((rows, hid))]
         + [hbm()] * 3,
         out_specs=[whole_spec(part)] * n_narrow,
         out_shape=[jax.ShapeDtypeStruct(part, BF16)] * n_narrow,
@@ -429,7 +436,7 @@
         compiler_params=params(),
         cost_estimate=cost(6 * rows * width * hid, 11e6),
         name="item_own",
-    )(jnp.reshape(here, (1,)), cot, slope_up, slope_gate, w_gate, w_up, w_down)
+    )(cot, slope_up, slope_gate, w_gate, w_up, w_down)
 
 
 def late_kernel(slots, before, scale, place_ref, *refs):
@@ -439,7 +446,7 @@
         refs[count : count + 6],
     )
     earlier, refs = (refs[count + 6 : count + 9], refs[count + 9 :]) if before else (None, refs[count + 6 :])
-    outs, (cot, column, normed, hidden, slope_up, slope_gate, down, sems) = refs[:3], refs[3:]
+    outs, (cot, column, normed, hidden, slope_up, slope_gate, d_both, down, sems) = refs[:3], refs[3:]
     rows = cot.shape[0] // count
     block = column.shape[1]
     narrow = block % 128 != 0
@@ -466,18 +473,14 @@
         if k == 0:
             for load in rest:
                 load.wait()
-        d_up = (d_hidden * slope_up[:, to].astype(F32)).astype(BF16)
-        d_gate = (d_hidden * slope_gate[:, to].astype(F32)).astype(BF16)
-        gate_part = mm(normed[...], d_gate, FIRST) * scale
-        up_part = mm(normed[...], d_up, FIRST) * scale
-        down_part = mm(hidden[:, to], column[...], FIRST) * scale
-        if before:
-            gate_part += earlier[0][:, to]
-            up_part += earlier[1][:, to]
-            down_part += earlier[2][to, :]
-        outs[0][:, to] = gate_part
-        outs[1][:, to] = up_part
-        outs[2][to, :] = down_part
+        d_both[:, to] = (d_hidden * slope_gate[:, to].astype(F32)).astype(BF16)
+        at = slice(hid + to.start, hid + to.stop)
+        d_both[:, at] = (d_hidden * slope_up[:, to].astype(F32)).astype(BF16)
+    both_part = mm(normed[...], d_both[...], FIRST) * scale
+    down_part = mm(column[...], hidden[...], FIRST).T * scale
+    parts = (both_part[:, :hid], both_part[:, hid:], down_part)
+    for k, part in enumerate(parts):
+        outs[k][...] = part + earlier[k][...] if before else part
 
 
 def item_late(place, slots, pieces, column, normed, hidden, slope_up, slope_gate, w_down, before, scale):
@@ -501,6 +504,7 @@
             pltpu.VMEM((rows, hid), BF16),
             pltpu.VMEM((rows, hid), BF16),
             pltpu.VMEM((rows, hid), BF16),
+            pltpu.VMEM((rows, 2 * hid), BF16),
             pltpu.VMEM((hid, width), BF16),
             pltpu.SemaphoreType.DMA((5 * count + 1 + len(tiles(hid, TILE)),)),
         ],
@@ -549,7 +553,7 @@
     slots, (feat_out, gate_out, up_out, down_out) = refs[:-4], refs[-4:]
     cut, hid = kept_a.shape[0], gate_out.shape[1]
     for half, (kept, got) in enumerate(((kept_a, got_a), (kept_b, got_b))):
-        total = (kept[...] + got[...].astype(F32)) * scale
+        total = (kept[...].astype(F32) + got[...].astype(F32)) * scale
         at = slice(half * cut, (half + 1) * cut)
         gate_out[at, :] = total[:, :hid]
         up_out[at, :] = total[:, hid : 2 * hid]
@@ -578,28 +582,7 @@
     )(jnp.reshape(here, (1,)), kept_a, got_a, kept_b, got_b, *slots)
 
 
-def place_kernel(here_ref, *refs):
-    slots, out = refs[:-1], refs[-1]
-    rows = slots[0].shape[0]
-    for k, slot in enumerate(slots):
-        out[pl.ds(pl.multiple_of((here_ref[0] ^ k) * rows, rows), rows), :] = slot[...]
-
-
-def place_rows(here, slots):
-    rows, width = slots[0].shape
-    count = len(slots)
-    return pl.pallas_call(
-        place_kernel,
-        in_specs=[smem()] + [vmem()] * count,
-        out_specs=vmem(),
-        out_shape=jax.ShapeDtypeStruct((count * rows, width), slots[0].dtype),
-        compiler_params=params(),
-        cost_estimate=cost(0, 4 * count * rows * width),
-        name="place_rows",
-    )(jnp.reshape(here, (1,)), *slots)
-
-
-def grad_tables(n_chips, chip, core, order_a, order_b):
+def grad_tables(n_chips, order_a, order_b):
     first_a, first_b = order_a[0] >> 1, order_b[0] >> 1
     rels = sorted(range(n_chips), key=lambda r: (not (r & first_a), not (r & first_b), r))
     rows = [[], [], [], [], [], [], []]
@@ -618,24 +601,24 @@
             rows[row + 1].append(last_kept)
             rows[row + 2].append(int(is_sent))
         places[name] = kept_order
-    rel = jnp.array(rels, jnp.int32)
-    fixed = [jnp.array(r, jnp.int32) for r in rows[:6]]
-    table = jnp.stack([(chip ^ rel) * 2 + core, *fixed, rel])
-    return table, places
+    return np.array([rels, *rows[:6]], np.int32), places
 
 
 def first_sums(got, kept, slots):
-    return {r: kept[i].astype(F32) + got[i].astype(F32) for i, r in enumerate(slots)}
+    return {r: (kept[i].astype(F32) + got[i].astype(F32)).astype(BF16) for i, r in enumerate(slots)}
 
 
 def sent_away(total, bit):
     away = sorted(r for r in total if r & (bit >> 1))
-    return jnp.stack([total[r].astype(BF16) for r in away])
+    return jnp.stack([total[r] for r in away])
 
 
 def next_sums(total, got, bit):
     away = sorted(r for r in total if r & (bit >> 1))
-    return {r ^ (bit >> 1): total[r ^ (bit >> 1)] + got[i].astype(F32) for i, r in enumerate(away)}
+    return {
+        r ^ (bit >> 1): (total[r ^ (bit >> 1)].astype(F32) + got[i].astype(F32)).astype(BF16)
+        for i, r in enumerate(away)
+    }
 
 
 def body(
@@ -667,7 +650,7 @@
     hid = user_gate.shape[1]
     block = width // n_wide
     rels = jnp.arange(n_chips, dtype=jnp.int32)
-    place = jnp.stack([chip, core, me])
+    place = jnp.stack([chip, core, me, here])
 
     def near(value):
         return [value] + [swap(value, r << 1) for r in range(1, n_chips)]
@@ -678,7 +661,7 @@
 
     feats = gather_wide(item_feat)
 
-    normed, masked, hidden, d_gate, d_up, sent, kept = user_layer(
+    normed, masked, hidden, d_both, sent, kept = user_layer(
         place,
         hist_len,
         user_input.reshape(rows, width),
@@ -694,8 +677,7 @@
     )
     sent, *_ = lax.optimization_barrier((sent, *feats[1:n_chips]))
     got = swap(sent, 1)
-    sent_table = jnp.stack([(chip ^ rels) * 2 + 1 - core])
-    grads_sent = sent_grads(sent_table, normed, masked, d_gate, d_up, hidden, block)
+    grads_sent = sent_grads(place, (chip ^ rels) * 2 + 1 - core, normed, masked, d_both, hidden, block)
     got, grads_sent = lax.optimization_barrier((got, grads_sent))
     grads_got = swap(grads_sent, 1)
     sums = []
@@ -706,14 +688,15 @@
 
     group = min(8, n_wide)
     forwards = [
-        item_forward(place, item_gain, feats[k : k + group], item_gate, item_up, block)
+        item_forward(place, item_gain, feats[k : k + group], item_gate, item_up, block, n_narrow)
         for k in range(0, n_wide, group)
     ]
 
-    kept_table, places = grad_tables(n_chips, chip, core, order_a, order_b)
+    kept_table, places = grad_tables(n_chips, order_a, order_b)
     grads_got, _ = lax.optimization_barrier((grads_got, forwards[-1][0]))
     sent_a, kept_a, sent_b, kept_b = kept_grads(
-        kept_table, normed, masked, d_gate, d_up, hidden, grads_got, block
+        place, kept_table, (chip ^ jnp.asarray(kept_table[0])) * 2 + core,
+        normed, masked, d_both, hidden, grads_got, block,
     )
     pieces[0], sent_a, sent_b = lax.optimization_barrier((pieces[0], sent_a, sent_b))
     mine = list(merge_chips(here, kept, got, pieces, n_narrow))
@@ -735,16 +718,13 @@
             for k in range(1, n_narrow)
         ]
 
-    def narrow_gather(piece):
-        return place_rows(here, narrow_slots(piece))
-
     item_in = narrow_scatter(mine)
-    item_cot = narrow_gather(item_in.astype(BF16))
+    item_cot = jnp.concatenate(narrow_slots(item_in.astype(BF16)), axis=0)
     cots = [item_cot] + [swap(item_cot, r << 1) for r in range(1, n_chips - 1)]
     last_cot, *cots[1:] = lax.optimization_barrier((item_cot, *cots[1:]))
     cots.append(swap(last_cot, (n_chips - 1) << 1))
     item_part = item_own(
-        here, item_cot, forwards[0][2], forwards[0][3], item_gate, item_up, item_down, n_narrow
+        item_cot, forwards[0][2], forwards[0][3], item_gate, item_up, item_down, n_narrow
     )
     item_dn = narrow_scatter(item_part)
 

time: 168 us -> 166 us (0.988)
  waiting for transfers between devices: 24.9 us -> 28.2 us
  Pallas kernels: 87.1 us -> 84.6 us
  local copies, waits for them, and re-layouts: 6.05 us -> 4.21 us
    add x1 -> x0, other arithmetic: 3.77 us -> none  [first_sums(): kept[i].astype(F32) + got[i].astype(F32)]
    ppermute x23, waiting for transfers between devices: 6.32 us -> 9.47 us  [swap(): return lax.ppermute(value, 'wide', [(i, i ^ bit) for i in range(count)])]
    convert_element_type x1 -> x2, other arithmetic: 0.97 us -> 4 us  [the longest x1 3.03 us: first_sums(): (kept[i].astype(F32) + got[i].astype(F32)).astype(BF16)]
    ppermute x6, starting transfers between devices: 11.9 us -> 10.1 us  [narrow_scatter(): lax.ppermute(part, 'narrow', [(i, i ^ k) for i in range(n_narrow)])]
    pallas_call x3 -> x2, Pallas kernels: 24.5 us -> 23 us  [the longest x1 15 us: item_forward(): pl.pallas_call(functools.partial(forward_kernel, count, n_narrow), in_spe...]
    unnamed x76 -> x50, local copies, waits for them, and re-layouts: 4.52 us -> 3.3 us
  transfers between devices with their start and end apart: 35 -> 35, of which waited for: 11 -> 10; matrix products, arithmetic and copies ran while one was open for 7% -> 6% of each run, Pallas kernels for 48% -> 47%
where the time goes in v4:
time: 166 us; the launch traced here: 165 us
  Pallas kernels  84.6 us (51%)
  starting transfers between devices  38.3 us (23%)
  waiting for transfers between devices  28.2 us (17%)
  other arithmetic  8.85 us (5%)
  local copies, waits for them, and re-layouts  4.21 us (3%)
    ppermute x23, starting transfers between devices, swap(): return lax.ppermute(value, 'wide', [(i, i ^ bit) for i in range(count)])  19.2 us
    pallas_call x1, Pallas kernels, user_layer(): pl.pallas_call(functools.partial(user_kernel, share, item_dev), in_specs=...  19.1 us
    pallas_call x2, Pallas kernels, item_late(): pl.pallas_call(functools.partial(late_kernel, tuple(slots), bool(before),...  18.4 us
    pallas_call x1, Pallas kernels, item_forward(): pl.pallas_call(functools.partial(forward_kernel, count, n_narrow), in_spe...  15 us
    ppermute x6, waiting for transfers between devices, narrow_slots(): lax.ppermute(piece, 'narrow', [(i, i ^ k) for i in range(n_narrow)])  10.1 us
    ppermute x6, starting transfers between devices, narrow_scatter(): lax.ppermute(part, 'narrow', [(i, i ^ k) for i in range(n_narrow)])  10.1 us
    pallas_call x1, Pallas kernels, kept_grads(): pl.pallas_call(kept_kernel, grid_spec=pltpu.PrefetchScalarGridSpec(num_sc...  9.64 us
    ppermute x23, waiting for transfers between devices, swap(): return lax.ppermute(value, 'wide', [(i, i ^ bit) for i in range(count)])  9.47 us
  transfers between devices with their start and end apart: 35, of which 10 were waited for; matrix products, arithmetic and copies ran while one was open for 6% of the time, Pallas kernels for 47%

profile of v4, /device:TPU:0, one launch (start us, length us, event | category | flops | bytes accessed | tf_op | source)
XLA Modules:
  0.0 165.1 jit_solution(14021585950220224482)
XLA Ops:
  0.6 3.0 %collective-permute-start = (bf16[128,2048]{1,0:T(8,128)(2,1)}, bf16[128,2048]{1,0:T(8,128)(2,1)S(1)}, u32[]{:S(2)}, u32[]{:S(2)}) collective-permute-start(bf16[128,2048]{1,0:T(8,128)(2,1)} %refs_0_.1), channel_id=1, source_target_pairs={{0,8},{4,12},{8,0},{12,4},{16,24},{20,28},{24,16},{28,20},{1,9},{5... | collective-permute-start | bytes 1572872 | tf_op jit(solution)/shard_map/ppermute | solution.py:49
  3.6 1.5 collective-permute-start.1
  5.2 0.7 pad_add_fusion.place_ref.table_ref
  5.8 19.1 %user_layer.1 = (bf16[512,2048]{1,0:T(8,128)(2,1)}, bf16[512,2048]{1,0:T(8,128)(2,1)}, bf16[512,768]{1,0:T(8,128)(2,1)}, bf16[512,1536]{1,0:T(8,128)(2,1)}, bf16...) custom-call(s32[4]{0:T(128)} %pad_add_fusion.place_ref.table_ref, s32[8]{0:T(128)} %hist_len_ref.1, ...), custom_call_target="tpu_custom_call" | custom-call | flops 1342177280 | bytes 4000000 | tf_op jit(solution)/shard_map/user_layer/pallas_call | solution.py:172
  25.0 3.5 %collective-permute-done.1.refs_2_ = bf16[128,2048]{1,0:T(8,128)(2,1)S(1)} collective-permute-done((bf16[128,2048]{1,0:T(8,128)(2,1)}, bf16[128,2048]{1,0:T(8,128)(2,1)S(1)}, u32[]{:S(2)}, u32[]{:S(2)}) %collective-permute-start.1) | collective-permute-done | bytes 524320 | tf_op jit(solution)/shard_map/ppermute | solution.py:49
  28.5 7.7 %sent_grads.1 = bf16[4,256,2304]{2,1,0:T(8,128)(2,1)} custom-call(s32[4]{0:T(128)} %pad_add_fusion.place_ref.table_ref, bf16[512,2048]{1,0:T(8,128)(2,1)} %get-tuple-element.67.normed_ref, bf16[512,2048]{1,0:T(8,128)(2,1)} %get-tuple-element.68.masked_ref, bf16[512,1536]{1,0:T(8,128)(2,1)} %get-tuple-element.69.d_both_ref, ...), custom_call_target="tpu_custom_call" | custom-call | flops 402653184 | bytes 1666666 | tf_op jit(solution)/shard_map/sent_grads/pallas_call | solution.py:256
  36.2 0.4 collective-permute-start.4
  36.6 0.1 collective-permute-start.5
  36.8 0.4 collective-permute-start.6
  37.1 0.1 collective-permute-start.7
  37.3 0.4 collective-permute-start.8
  37.6 2.8 %add_convert_fusion.4 = (bf16[128,2048]{1,0:T(8,128)(2,1)}, bf16[128,2048]{1,0:T(8,128)(2,1)}, bf16[128,2048]{1,0:T(8,128)(2,1)}) fusion(bf16[512,2048]{1,0:T(8,128)(2,1)} %collective-permute-done.3.got_ref, bf16[512,2048]{1,0:T(8,128)(2,1)S(1)} %copy-done), kind=kLoop, calls=%fused_computation.4 | loop fusion | flops 3145728 | bytes 4718592 | tf_op jit(solution)/shard_map/convert_element_type | solution.py:686
  40.5 2.1 %collective-permute-done.5.refs_4_ = bf16[128,2048]{1,0:T(8,128)(2,1)S(1)} collective-permute-done((bf16[128,2048]{1,0:T(8,128)(2,1)S(1)}, bf16[128,2048]{1,0:T(8,128)(2,1)S(1)}, u32[]{:S(2)}, u32[]{:S(2)}) %collective-permute-start.5) | collective-permute-done | bytes 524320 | tf_op jit(solution)/shard_map/ppermute | solution.py:49
  42.5 2.6 %collective-permute-start.9 = (bf16[128,2048]{1,0:T(8,128)(2,1)}, bf16[128,2048]{1,0:T(8,128)(2,1)S(1)}, u32[]{:S(2)}, u32[]{:S(2)}) collective-permute-start(bf16[128,2048]{1,0:T(8,128)(2,1)} %get-tuple-element.131), channel_id=1, source_target_pairs={{0,8},{4,12},{8,0},{12,4},{16,24},{20,28},{24,16},{28,20},{1,9},{5... | collective-permute-start | bytes 1572872 | tf_op jit(solution)/shard_map/ppermute | solution.py:49
  45.2 0.4 collective-permute-start.10
  45.6 0.4 copy-done.16
  46.0 2.2 %collective-permute-start.11 = (bf16[128,2048]{1,0:T(8,128)(2,1)}, bf16[128,2048]{1,0:T(8,128)(2,1)S(1)}, u32[]{:S(2)}, u32[]{:S(2)}) collective-permute-start(bf16[128,2048]{1,0:T(8,128)(2,1)} %get-tuple-element.129), channel_id=1, source_target_pairs={{0,24},{4,28},{8,16},{12,20},{16,8},{20,12},{24,0},{28,4},{1,25},{... | collective-permute-start | bytes 1572872 | tf_op jit(solution)/shard_map/ppermute | solution.py:49
  48.2 15.0 %item_forward.1 = (bf16[1024,256]{1,0:T(8,128)(2,1)}, bf16[1024,768]{1,0:T(8,128)(2,1)}, bf16[1024,768]{1,0:T(8,128)(2,1)}, bf16[1024,768]{1,0:T(8,128)(2,1)}) custom-call(s32[4]{0:T(128)} %pad_add_fusion.place_ref.table_ref, bf16[2048]{0:T(1024)(128)(2,1)} %gain_ref.3, bf16[128,2048]{1,0:T(8,128)(2,1)} %refs_0_.1, bf16[128,2048]{1,0:T(8,128)(2,1)} %copy-done.8, ...), custom_call_target="tpu_custom_call" | custom-call | flops 1073741824 | bytes 2666666 | tf_op jit(solution)/shard_map/item_forward/pallas_call | solution.py:375
  63.3 9.6 %kept_grads.1 = (bf16[2,128,2304]{2,1,0:T(8,128)(2,1)}, bf16[2,128,2304]{2,1,0:T(8,128)(2,1)}, bf16[2,128,2304]{2,1,0:T(8,128)(2,1)}, bf16[2,128,2304]{2,1,0:T(8,128)(2,1)}) custom-call(s32[4]{0:T(128)} %pad_add_fusion.place_ref.table_ref, s32[7,4]{1,0:T(8,128)} %constant.48.clone.table_ref, bf16[512,2048]{1,0:T(8,128)(2,1)} %get-tuple-element.67.normed_ref, ...), custom_call_target="tpu_custom_call" | custom-call | flops 402653184 | bytes 2500000 | tf_op jit(solution)/shard_map/kept_grads/pallas_call | solution.py:279
  73.0 0.8 copy-done.10
  73.7 0.2 copy-done.11
  73.9 0.8 copy-done.13
  74.7 3.1 %merge_chips.1 = (bf16[32,2048]{1,0:T(8,128)(2,1)}, bf16[32,2048]{1,0:T(8,128)(2,1)}, bf16[32,2048]{1,0:T(8,128)(2,1)}, bf16[32,2048]{1,0:T(8,128)(2,1)}) custom-call(s32[1]{0:T(128)} %bitcast.here_ref, bf16[512,2048]{1,0:T(8,128)(2,1)} %get-tuple-element.77.kept_ref, bf16[512,2048]{1,0:T(8,128)(2,1)} %collective-permute-done.3.got_ref, ...), custom_call_target="tpu_custom_call" | custom-call | bytes 611669 | tf_op jit(solution)/shard_map/merge_chips/pallas_call | solution.py:539
  77.8 1.6 collective-permute-start.14
  79.4 2.6 %collective-permute-start.15 = (bf16[32,2048]{1,0:T(8,128)(2,1)}, bf16[32,2048]{1,0:T(8,128)(2,1)S(1)}, u32[]{:S(2)}, u32[]{:S(2)}) collective-permute-start(bf16[32,2048]{1,0:T(8,128)(2,1)} %get-tuple-element.89), channel_id=1, source_target_pairs={{0,2},{1,3},{2,0},{3,1},{4,6},{5,7},{6,4},{7,5},{8,10},{9,11},{10,... | collective-permute-start | bytes 393224 | tf_op jit(solution)/shard_map/ppermute | solution.py:710
  82.0 0.2 collective-permute-start.16
  82.2 0.7 collective-permute-start.12
  82.9 0.7 collective-permute-start.13
  83.7 0.8 collective-permute-done.14
  84.5 7.8 %collective-permute-done.15 = bf16[32,2048]{1,0:T(8,128)(2,1)S(1)} collective-permute-done((bf16[32,2048]{1,0:T(8,128)(2,1)}, bf16[32,2048]{1,0:T(8,128)(2,1)S(1)}, u32[]{:S(2)}, u32[]{:S(2)}) %collective-permute-start.15) | collective-permute-done | bytes 131104 | tf_op jit(solution)/shard_map/ppermute | solution.py:710
  92.3 1.0 fusion.10
  93.3 2.0 %collective-permute-start.17 = (bf16[32,2048]{1,0:T(8,128)(2,1)S(1)}, bf16[32,2048]{1,0:T(8,128)(2,1)S(1)}, u32[]{:S(2)}, u32[]{:S(2)}) collective-permute-start(bf16[32,2048]{1,0:T(8,128)(2,1)S(1)} %get-tuple-element.127), channel_id=1, source_target_pairs={{0,1},{1,0},{2,3},{3,2},{4,5},{5,4},{6,7},{7,6},{8,9},{9,8},{10,11... | collective-permute-start | bytes 393224 | tf_op jit(solution)/shard_map/ppermute | solution.py:717
  95.3 1.1 collective-permute-start.18
  96.4 1.4 collective-permute-start.19
  97.8 1.9 %collective-permute-done.17 = bf16[32,2048]{1,0:T(8,128)(2,1)S(1)} collective-permute-done((bf16[32,2048]{1,0:T(8,128)(2,1)S(1)}, bf16[32,2048]{1,0:T(8,128)(2,1)S(1)}, u32[]{:S(2)}, u32[]{:S(2)}) %collective-permute-start.17) | collective-permute-done | bytes 131104 | tf_op jit(solution)/shard_map/ppermute | solution.py:717
  99.7 7.4 %collective-permute-done.18 = bf16[32,2048]{1,0:T(8,128)(2,1)S(1)} collective-permute-done((bf16[32,2048]{1,0:T(8,128)(2,1)S(1)}, bf16[32,2048]{1,0:T(8,128)(2,1)S(1)}, u32[]{:S(2)}, u32[]{:S(2)}) %collective-permute-start.18) | collective-permute-done | bytes 131104 | tf_op jit(solution)/shard_map/ppermute | solution.py:717
  107.1 0.8 pad_maximum_fusion.cot.refs_0_.refs_6_
  108.0 1.8 %collective-permute-start.20 = (bf16[128,2048]{1,0:T(8,128)(2,1)}, bf16[128,2048]{1,0:T(8,128)(2,1)}, u32[]{:S(2)}, u32[]{:S(2)}) collective-permute-start(bf16[128,2048]{1,0:T(8,128)(2,1)} %pad_maximum_fusion.cot.refs_0_.refs_6_), channel_id=1, source_target_pairs={{0,8},{4,12},{8,0},{12,4},{16,24},{20,28},{24,16},{28,20},{1,9},{5... | collective-permute-start | bytes 1572872 | tf_op jit(solution)/shard_map/ppermute | solution.py:49
  109.8 0.8 collective-permute-start.21
  110.6 8.0 %item_own.1 = (bf16[32,2048]{1,0:T(8,128)(2,1)}, bf16[32,2048]{1,0:T(8,128)(2,1)}, bf16[32,2048]{1,0:T(8,128)(2,1)}, bf16[32,2048]{1,0:T(8,128)(2,1)}) custom-call(bf16[128,2048]{1,0:T(8,128)(2,1)} %pad_maximum_fusion.cot.refs_0_.refs_6_, bf16[1024,768]{1,0:T(8,128)(2,1)} %get-tuple-element.91.slope_up.refs_9_.refs_5_, ...), custom_call_target="tpu_custom_call" | custom-call | flops 201326592 | bytes 1833333 | tf_op jit(solution)/shard_map/item_own/pallas_call | solution.py:422
  118.6 1.8 %collective-permute-done.20.refs_1_ = bf16[128,2048]{1,0:T(8,128)(2,1)} collective-permute-done((bf16[128,2048]{1,0:T(8,128)(2,1)}, bf16[128,2048]{1,0:T(8,128)(2,1)}, u32[]{:S(2)}, u32[]{:S(2)}) %collective-permute-start.20) | collective-permute-done | bytes 524320 | tf_op jit(solution)/shard_map/ppermute | solution.py:49
  120.4 1.1 collective-permute-done.21.refs_2_
  121.6 3.0 %add_convert_fusion.2 = (bf16[1,128,2304]{2,1,0:T(8,128)(2,1)}, bf16[128,2304]{1,0:T(8,128)(2,1)}, bf16[1,128,2304]{2,1,0:T(8,128)(2,1)}, bf16[128,2304]{1,0:T(8,128)(2,1)}) fusion(bf16[2,128,2304]{2,1,0:T(8,128)(2,1)S(1)} %collective-permute-done.12, bf16[2,128,2304]{2,1,0:T(8,128)(2,1)S(1)} %copy-done.2, bf16[2,128,2304]{2,1,0:T(8,128)(2,1)} %collective-permute-done.13, ...), kind=kLoop, calls=%fused_computation.2 | loop fusion | flops 4718592 | bytes 7077888 | tf_op jit(solution)/shard_map/convert_element_type | solution.py:608
  124.6 0.5 collective-permute-start.27
  125.1 1.8 %collective-permute-start.24 = (bf16[128,2048]{1,0:T(8,128)(2,1)}, bf16[128,2048]{1,0:T(8,128)(2,1)S(1)}, u32[]{:S(2)}, u32[]{:S(2)}) collective-permute-start(bf16[128,2048]{1,0:T(8,128)(2,1)} %pad_maximum_fusion.cot.refs_0_.refs_6_), channel_id=1, source_target_pairs={{0,24},{4,28},{8,16},{12,20},{16,8},{20,12},{24,0},{28,4},{1,25},{... | collective-permute-start | bytes 1572872 | tf_op jit(solution)/shard_map/ppermute | solution.py:49
  126.9 0.9 constant_dynamic-slice_fusion
  127.8 2.3 %collective-permute-start.29 = (bf16[32,2048]{1,0:T(8,128)(2,1)}, bf16[32,2048]{1,0:T(8,128)(2,1)S(1)}, u32[]{:S(2)}, u32[]{:S(2)}) collective-permute-start(bf16[32,2048]{1,0:T(8,128)(2,1)} %get-tuple-element.111), channel_id=1, source_target_pairs={{0,1},{1,0},{2,3},{3,2},{4,5},{5,4},{6,7},{7,6},{8,9},{9,8},{10,11... | collective-permute-start | bytes 393224 | tf_op jit(solution)/shard_map/ppermute | solution.py:710
  130.1 1.9 %collective-permute-start.30 = (bf16[32,2048]{1,0:T(8,128)(2,1)}, bf16[32,2048]{1,0:T(8,128)(2,1)S(1)}, u32[]{:S(2)}, u32[]{:S(2)}) collective-permute-start(bf16[32,2048]{1,0:T(8,128)(2,1)} %get-tuple-element.112), channel_id=1, source_target_pairs={{0,2},{1,3},{2,0},{3,1},{4,6},{5,7},{6,4},{7,5},{8,10},{9,11},{10,... | collective-permute-start | bytes 393224 | tf_op jit(solution)/shard_map/ppermute | solution.py:710
  132.1 1.5 collective-permute-start.31
  133.5 0.4 collective-permute-start.22
  133.9 0.4 copy-done.12
  134.3 11.0 %item_late.2 = (f32[256,768]{1,0:T(8,128)}, f32[256,768]{1,0:T(8,128)}, f32[768,256]{1,0:T(8,128)}) custom-call(s32[4]{0:T(128)} %pad_add_fusion.place_ref.table_ref, bf16[128,2048]{1,0:T(8,128)(2,1)} %pad_maximum_fusion.cot.refs_0_.refs_6_, bf16[128,2048]{1,0:T(8,128)(2,1)} %collective-permute-done.20.refs_1_, ...), custom_call_target="tpu_custom_call" | custom-call | flops 1107296256 | bytes 2666666 | tf_op jit(solution)/shard_map/item_late/pallas_call | solution.py:491
  145.4 0.1 fusion.9
  145.5 1.2 collective-permute-start.23
  146.8 0.2 fusion.4
  147.0 0.1 fusion.8.refs_0_
  147.2 0.6 collective-permute-start.32
  147.8 2.4 %collective-permute-start.33 = (bf16[32,2048]{1,0:T(8,128)(2,1)S(1)}, bf16[32,2048]{1,0:T(8,128)(2,1)S(1)}, u32[]{:S(2)}, u32[]{:S(2)}) collective-permute-start(bf16[32,2048]{1,0:T(8,128)(2,1)S(1)} %fusion.8.refs_0_), channel_id=1, source_target_pairs={{0,2},{1,3},{2,0},{3,1},{4,6},{5,7},{6,4},{7,5},{8,10},{9,11},{10,... | collective-permute-start | bytes 393224 | tf_op jit(solution)/shard_map/ppermute | solution.py:717
  150.2 1.5 collective-permute-start.34
  151.7 7.3 %item_late.3 = (f32[256,768]{1,0:T(8,128)}, f32[256,768]{1,0:T(8,128)}, f32[768,256]{1,0:T(8,128)}) custom-call(s32[4]{0:T(128)} %pad_add_fusion.place_ref.table_ref, bf16[128,2048]{1,0:T(8,128)(2,1)} %copy-done.1, bf16[128,2048]{1,0:T(8,128)(2,1)} %copy-done.15, bf16[128,2048]{1,0:T(8,128)(2,1)} %copy-done.1, ...), custom_call_target="tpu_custom_call" | custom-call | flops 369098752 | bytes 2666666 | tf_op jit(solution)/shard_map/item_late/pallas_call | solution.py:491
  159.0 1.0 collective-permute-done.23
  160.0 0.7 collective-permute-done.33.refs_2_
  160.9 0.5 copy-done.21
  161.4 3.6 %final_sums.1 = (bf16[128,2048]{1,0:T(8,128)(2,1)}, f32[256,768]{1,0:T(8,128)}, f32[256,768]{1,0:T(8,128)}, f32[768,256]{1,0:T(8,128)}) custom-call(s32[1]{0:T(128)} %bitcast.here_ref, bf16[128,2304]{1,0:T(8,128)(2,1)} %get-tuple-element.135.kept_a, bf16[128,2304]{1,0:T(8,128)(2,1)} %bitcast.14, bf16[128,2304]{1,0:T(8,128)(2,1)} %get-tuple-element.137.kept_b, ...), custom_call_target="tpu_custom_call" | custom-call | bytes 491520 | tf_op jit(solution)/shard_map/final_sums/pallas_call | solution.py:569
  (77 shorter events, 0.4 us)
Async XLA Ops:
  0.6 24.3 %collective-permute-start = (bf16[128,2048]{1,0:T(8,128)(2,1)}, bf16[128,2048]{1,0:T(8,128)(2,1)S(1)}, u32[]{:S(2)}, u32[]{:S(2)}) collective-permute-start(bf16[128,2048]{1,0:T(8,128)(2,1)} %refs_0_.1), channel_id=1, source_target_pairs={{0,8},{4,12},{8,0},{12,4},{16,24},{20,28},{24,16},{28,20},{1,9},{5... | collective-permute-start | bytes 1572872 | tf_op jit(solution)/shard_map/ppermute | solution.py:49
  3.6 24.8 %collective-permute-start.1 = (bf16[128,2048]{1,0:T(8,128)(2,1)}, bf16[128,2048]{1,0:T(8,128)(2,1)S(1)}, u32[]{:S(2)}, u32[]{:S(2)}) collective-permute-start(bf16[128,2048]{1,0:T(8,128)(2,1)} %refs_0_.1), channel_id=1, source_target_pairs={{0,16},{4,20},{8,24},{12,28},{16,0},{20,4},{24,8},{28,12},{1,17},{... | collective-permute-start | bytes 1572872 | tf_op jit(solution)/shard_map/ppermute | solution.py:49
  5.2 23.3 %collective-permute-start.2 = (bf16[128,2048]{1,0:T(8,128)(2,1)}, bf16[128,2048]{1,0:T(8,128)(2,1)}, u32[]{:S(2)}, u32[]{:S(2)}) collective-permute-start(bf16[128,2048]{1,0:T(8,128)(2,1)} %refs_0_.1), channel_id=1, source_target_pairs={{0,24},{4,28},{8,16},{12,20},{16,8},{20,12},{24,0},{28,4},{1,25},{... | collective-permute-start | bytes 1572872 | tf_op jit(solution)/shard_map/ppermute | solution.py:49
  25.0 11.8 %copy-start.8 = (bf16[128,2048]{1,0:T(8,128)(2,1)}, bf16[128,2048]{1,0:T(8,128)(2,1)S(1)}, u32[]{:S(2)}) copy-start(bf16[128,2048]{1,0:T(8,128)(2,1)S(1)} %collective-permute-done.refs_1_) | copy-start | bytes 1572868
  28.5 8.7 %copy-start.9 = (bf16[128,2048]{1,0:T(8,128)(2,1)}, bf16[128,2048]{1,0:T(8,128)(2,1)S(1)}, u32[]{:S(2)}) copy-start(bf16[128,2048]{1,0:T(8,128)(2,1)S(1)} %collective-permute-done.1.refs_2_) | copy-start | bytes 1572868
  28.5 7.8 %collective-permute-start.3 = (bf16[512,2048]{1,0:T(8,128)(2,1)}, bf16[512,2048]{1,0:T(8,128)(2,1)}, u32[]{:S(2)}, u32[]{:S(2)}) collective-permute-start(bf16[512,2048]{1,0:T(8,128)(2,1)} %get-tuple-element.72), channel_id=1, source_target_pairs={{0,4},{4,0},{8,12},{12,8},{16,20},{20,16},{24,28},{28,24},{1,5},{5... | collective-permute-start | bytes 6291464 | tf_op jit(solution)/shard_map/ppermute | solution.py:49
  28.5 8.1 %copy-start.4 = (bf16[128,2048]{1,0:T(8,128)(2,1)S(1)}, bf16[128,2048]{1,0:T(8,128)(2,1)}, u32[]{:S(2)}) copy-start(bf16[128,2048]{1,0:T(8,128)(2,1)} %refs_0_.1) | copy-start | bytes 1572868
  28.5 9.1 %copy-start = (bf16[512,2048]{1,0:T(8,128)(2,1)S(1)}, bf16[512,2048]{1,0:T(8,128)(2,1)}, u32[]{:S(2)}) copy-start(bf16[512,2048]{1,0:T(8,128)(2,1)} %get-tuple-element.77.kept_ref) | copy-start | bytes 6291460
  36.2 27.1 %collective-permute-start.4 = (bf16[4,256,2304]{2,1,0:T(8,128)(2,1)}, bf16[4,256,2304]{2,1,0:T(8,128)(2,1)}, u32[]{:S(2)}, u32[]{:S(2)}) collective-permute-start(bf16[4,256,2304]{2,1,0:T(8,128)(2,1)} %sent_grads.1), channel_id=1, source_target_pairs={{0,4},{4,0},{8,12},{12,8},{16,20},{20,16},{24,28},{28,24},{1,5},{5... | collective-permute-start | bytes 14155784 | tf_op jit(solution)/shard_map/ppermute | solution.py:49
  36.6 5.9 %collective-permute-start.5 = (bf16[128,2048]{1,0:T(8,128)(2,1)S(1)}, bf16[128,2048]{1,0:T(8,128)(2,1)S(1)}, u32[]{:S(2)}, u32[]{:S(2)}) collective-permute-start(bf16[128,2048]{1,0:T(8,128)(2,1)S(1)} %copy-done.4), channel_id=1, source_target_pairs={{0,4},{4,0},{8,12},{12,8},{16,20},{20,16},{24,28},{28,24},{1,5},{5... | collective-permute-start | bytes 1572872 | tf_op jit(solution)/shard_map/ppermute | solution.py:49
  36.8 8.4 %collective-permute-start.6 = (bf16[128,2048]{1,0:T(8,128)(2,1)S(1)}, bf16[128,2048]{1,0:T(8,128)(2,1)S(1)}, u32[]{:S(2)}, u32[]{:S(2)}) collective-permute-start(bf16[128,2048]{1,0:T(8,128)(2,1)S(1)} %collective-permute-done.refs_1_), channel_id=1, source_target_pairs={{0,4},{4,0},{8,12},{12,8},{16,20},{20,16},{24,28},{28,24},{1,5},{5... | collective-permute-start | bytes 1572872 | tf_op jit(solution)/shard_map/ppermute | solution.py:49
  37.1 8.4 %collective-permute-start.7 = (bf16[128,2048]{1,0:T(8,128)(2,1)S(1)}, bf16[128,2048]{1,0:T(8,128)(2,1)S(1)}, u32[]{:S(2)}, u32[]{:S(2)}) collective-permute-start(bf16[128,2048]{1,0:T(8,128)(2,1)S(1)} %collective-permute-done.1.refs_2_), channel_id=1, source_target_pairs={{0,4},{4,0},{8,12},{12,8},{16,20},{20,16},{24,28},{28,24},{1,5},{5... | collective-permute-start | bytes 1572872 | tf_op jit(solution)/shard_map/ppermute | solution.py:49
  37.3 11.0 %collective-permute-start.8 = (bf16[128,2048]{1,0:T(8,128)(2,1)}, bf16[128,2048]{1,0:T(8,128)(2,1)}, u32[]{:S(2)}, u32[]{:S(2)}) collective-permute-start(bf16[128,2048]{1,0:T(8,128)(2,1)} %collective-permute-done.2.refs_3_), channel_id=1, source_target_pairs={{0,4},{4,0},{8,12},{12,8},{16,20},{20,16},{24,28},{28,24},{1,5},{5... | collective-permute-start | bytes 1572872 | tf_op jit(solution)/shard_map/ppermute | solution.py:49
  42.5 3.0 %copy-start.14 = (bf16[128,2048]{1,0:T(8,128)(2,1)}, bf16[128,2048]{1,0:T(8,128)(2,1)S(1)}, u32[]{:S(2)}) copy-start(bf16[128,2048]{1,0:T(8,128)(2,1)S(1)} %collective-permute-done.5.refs_4_) | copy-start | bytes 1572868
  42.5 30.4 %collective-permute-start.9 = (bf16[128,2048]{1,0:T(8,128)(2,1)}, bf16[128,2048]{1,0:T(8,128)(2,1)S(1)}, u32[]{:S(2)}, u32[]{:S(2)}) collective-permute-start(bf16[128,2048]{1,0:T(8,128)(2,1)} %get-tuple-element.131), channel_id=1, source_target_pairs={{0,8},{4,12},{8,0},{12,4},{16,24},{20,28},{24,16},{28,20},{1,9},{5... | collective-permute-start | bytes 1572872 | tf_op jit(solution)/shard_map/ppermute | solution.py:49
  45.2 0.8 copy-start.16
  45.2 27.8 %collective-permute-start.10 = (bf16[128,2048]{1,0:T(8,128)(2,1)}, bf16[128,2048]{1,0:T(8,128)(2,1)S(1)}, u32[]{:S(2)}, u32[]{:S(2)}) collective-permute-start(bf16[128,2048]{1,0:T(8,128)(2,1)} %get-tuple-element.130), channel_id=1, source_target_pairs={{0,16},{4,20},{8,24},{12,28},{16,0},{20,4},{24,8},{28,12},{1,17},{... | collective-permute-start | bytes 1572872 | tf_op jit(solution)/shard_map/ppermute | solution.py:49
  45.6 2.7 %copy-start.17 = (bf16[128,2048]{1,0:T(8,128)(2,1)}, bf16[128,2048]{1,0:T(8,128)(2,1)S(1)}, u32[]{:S(2)}) copy-start(bf16[128,2048]{1,0:T(8,128)(2,1)S(1)} %collective-permute-done.7.refs_6_) | copy-start | bytes 1572868
  46.0 27.0 %collective-permute-start.11 = (bf16[128,2048]{1,0:T(8,128)(2,1)}, bf16[128,2048]{1,0:T(8,128)(2,1)S(1)}, u32[]{:S(2)}, u32[]{:S(2)}) collective-permute-start(bf16[128,2048]{1,0:T(8,128)(2,1)} %get-tuple-element.129), channel_id=1, source_target_pairs={{0,24},{4,28},{8,16},{12,20},{16,8},{20,12},{24,0},{28,4},{1,25},{... | collective-permute-start | bytes 1572872 | tf_op jit(solution)/shard_map/ppermute | solution.py:49
  72.9 0.8 copy-start.10
  73.0 0.9 copy-start.11
  73.9 0.8 copy-start.13
  77.8 6.7 %collective-permute-start.14 = (bf16[32,2048]{1,0:T(8,128)(2,1)}, bf16[32,2048]{1,0:T(8,128)(2,1)S(1)}, u32[]{:S(2)}, u32[]{:S(2)}) collective-permute-start(bf16[32,2048]{1,0:T(8,128)(2,1)} %get-tuple-element.88), channel_id=1, source_target_pairs={{0,1},{1,0},{2,3},{3,2},{4,5},{5,4},{6,7},{7,6},{8,9},{9,8},{10,11... | collective-permute-start | bytes 393224 | tf_op jit(solution)/shard_map/ppermute | solution.py:710
  79.4 12.9 %collective-permute-start.15 = (bf16[32,2048]{1,0:T(8,128)(2,1)}, bf16[32,2048]{1,0:T(8,128)(2,1)S(1)}, u32[]{:S(2)}, u32[]{:S(2)}) collective-permute-start(bf16[32,2048]{1,0:T(8,128)(2,1)} %get-tuple-element.89), channel_id=1, source_target_pairs={{0,2},{1,3},{2,0},{3,1},{4,6},{5,7},{6,4},{7,5},{8,10},{9,11},{10,... | collective-permute-start | bytes 393224 | tf_op jit(solution)/shard_map/ppermute | solution.py:710
  82.0 10.3 %collective-permute-start.16 = (bf16[32,2048]{1,0:T(8,128)(2,1)}, bf16[32,2048]{1,0:T(8,128)(2,1)S(1)}, u32[]{:S(2)}, u32[]{:S(2)}) collective-permute-start(bf16[32,2048]{1,0:T(8,128)(2,1)} %get-tuple-element.90), channel_id=1, source_target_pairs={{0,3},{1,2},{2,1},{3,0},{4,7},{5,6},{6,5},{7,4},{8,11},{9,10},{10,... | collective-permute-start | bytes 393224 | tf_op jit(solution)/shard_map/ppermute | solution.py:710
  82.2 39.3 %collective-permute-start.12 = (bf16[2,128,2304]{2,1,0:T(8,128)(2,1)}, bf16[2,128,2304]{2,1,0:T(8,128)(2,1)S(1)}, u32[]{:S(2)}, u32[]{:S(2)}) collective-permute-start(bf16[2,128,2304]{2,1,0:T(8,128)(2,1)} %get-tuple-element.85), channel_id=1, source_target_pairs={{0,8},{4,12},{8,0},{12,4},{16,24},{20,28},{24,16},{28,20},{1,9},{5... | collective-permute-start | bytes 3538952 | tf_op jit(solution)/shard_map/ppermute | solution.py:49
  82.9 38.6 %collective-permute-start.13 = (bf16[2,128,2304]{2,1,0:T(8,128)(2,1)}, bf16[2,128,2304]{2,1,0:T(8,128)(2,1)}, u32[]{:S(2)}, u32[]{:S(2)}) collective-permute-start(bf16[2,128,2304]{2,1,0:T(8,128)(2,1)} %get-tuple-element.86), channel_id=1, source_target_pairs={{0,16},{4,20},{8,24},{12,28},{16,0},{20,4},{24,8},{28,12},{1,17},{... | collective-permute-start | bytes 3538952 | tf_op jit(solution)/shard_map/ppermute | solution.py:49
  93.3 6.4 %collective-permute-start.17 = (bf16[32,2048]{1,0:T(8,128)(2,1)S(1)}, bf16[32,2048]{1,0:T(8,128)(2,1)S(1)}, u32[]{:S(2)}, u32[]{:S(2)}) collective-permute-start(bf16[32,2048]{1,0:T(8,128)(2,1)S(1)} %get-tuple-element.127), channel_id=1, source_target_pairs={{0,1},{1,0},{2,3},{3,2},{4,5},{5,4},{6,7},{7,6},{8,9},{9,8},{10,11... | collective-permute-start | bytes 393224 | tf_op jit(solution)/shard_map/ppermute | solution.py:717
  95.3 11.9 %collective-permute-start.18 = (bf16[32,2048]{1,0:T(8,128)(2,1)S(1)}, bf16[32,2048]{1,0:T(8,128)(2,1)S(1)}, u32[]{:S(2)}, u32[]{:S(2)}) collective-permute-start(bf16[32,2048]{1,0:T(8,128)(2,1)S(1)} %get-tuple-element.127), channel_id=1, source_target_pairs={{0,2},{1,3},{2,0},{3,1},{4,6},{5,7},{6,4},{7,5},{8,10},{9,11},{10,... | collective-permute-start | bytes 393224 | tf_op jit(solution)/shard_map/ppermute | solution.py:717
  96.4 10.8 %collective-permute-start.19 = (bf16[32,2048]{1,0:T(8,128)(2,1)S(1)}, bf16[32,2048]{1,0:T(8,128)(2,1)S(1)}, u32[]{:S(2)}, u32[]{:S(2)}) collective-permute-start(bf16[32,2048]{1,0:T(8,128)(2,1)S(1)} %get-tuple-element.127), channel_id=1, source_target_pairs={{0,3},{1,2},{2,1},{3,0},{4,7},{5,6},{6,5},{7,4},{8,11},{9,10},{10,... | collective-permute-start | bytes 393224 | tf_op jit(solution)/shard_map/ppermute | solution.py:717
  108.0 12.4 %collective-permute-start.20 = (bf16[128,2048]{1,0:T(8,128)(2,1)}, bf16[128,2048]{1,0:T(8,128)(2,1)}, u32[]{:S(2)}, u32[]{:S(2)}) collective-permute-start(bf16[128,2048]{1,0:T(8,128)(2,1)} %pad_maximum_fusion.cot.refs_0_.refs_6_), channel_id=1, source_target_pairs={{0,8},{4,12},{8,0},{12,4},{16,24},{20,28},{24,16},{28,20},{1,9},{5... | collective-permute-start | bytes 1572872 | tf_op jit(solution)/shard_map/ppermute | solution.py:49
  109.8 11.7 %collective-permute-start.21 = (bf16[128,2048]{1,0:T(8,128)(2,1)}, bf16[128,2048]{1,0:T(8,128)(2,1)}, u32[]{:S(2)}, u32[]{:S(2)}) collective-permute-start(bf16[128,2048]{1,0:T(8,128)(2,1)} %pad_maximum_fusion.cot.refs_0_.refs_6_), channel_id=1, source_target_pairs={{0,16},{4,20},{8,24},{12,28},{16,0},{20,4},{24,8},{28,12},{1,17},{... | collective-permute-start | bytes 1572872 | tf_op jit(solution)/shard_map/ppermute | solution.py:49
  110.6 19.5 %collective-permute-start.26 = (bf16[128,2048]{1,0:T(8,128)(2,1)}, bf16[128,2048]{1,0:T(8,128)(2,1)}, u32[]{:S(2)}, u32[]{:S(2)}) collective-permute-start(bf16[128,2048]{1,0:T(8,128)(2,1)} %pad_maximum_fusion.cot.refs_0_.refs_6_), channel_id=1, source_target_pairs={{0,4},{4,0},{8,12},{12,8},{16,20},{20,16},{24,28},{28,24},{1,5},{5... | collective-permute-start | bytes 1572872 | tf_op jit(solution)/shard_map/ppermute | solution.py:49
  110.6 10.9 %copy-start.2 = (bf16[2,128,2304]{2,1,0:T(8,128)(2,1)S(1)}, bf16[2,128,2304]{2,1,0:T(8,128)(2,1)}, u32[]{:S(2)}) copy-start(bf16[2,128,2304]{2,1,0:T(8,128)(2,1)} %get-tuple-element.76) | copy-start | bytes 3538948
  110.6 10.9 %copy-start.3 = (bf16[2,128,2304]{2,1,0:T(8,128)(2,1)S(1)}, bf16[2,128,2304]{2,1,0:T(8,128)(2,1)}, u32[]{:S(2)}) copy-start(bf16[2,128,2304]{2,1,0:T(8,128)(2,1)} %get-tuple-element.95) | copy-start | bytes 3538948
  121.5 10.6 %collective-permute-start.28 = (bf16[128,2048]{1,0:T(8,128)(2,1)}, bf16[128,2048]{1,0:T(8,128)(2,1)}, u32[]{:S(2)}, u32[]{:S(2)}) collective-permute-start(bf16[128,2048]{1,0:T(8,128)(2,1)} %collective-permute-done.21.refs_2_), channel_id=1, source_target_pairs={{0,4},{4,0},{8,12},{12,8},{16,20},{20,16},{24,28},{28,24},{1,5},{5... | collective-permute-start | bytes 1572872 | tf_op jit(solution)/shard_map/ppermute | solution.py:49
  121.5 6.3 %copy-start.23 = (bf16[2048]{0:T(1024)(128)(2,1)S(1)}, bf16[2048]{0:T(1024)(128)(2,1)}, u32[]{:S(2)}) copy-start(bf16[2048]{0:T(1024)(128)(2,1)} %gain_ref.3) | copy-start | bytes 12292
  121.5 10.5 %copy-start.24 = (bf16[32,2048]{1,0:T(8,128)(2,1)S(1)}, bf16[32,2048]{1,0:T(8,128)(2,1)}, u32[]{:S(2)}) copy-start(bf16[32,2048]{1,0:T(8,128)(2,1)} %get-tuple-element.113) | copy-start | bytes 393220
  124.6 8.9 %collective-permute-start.27 = (bf16[128,2048]{1,0:T(8,128)(2,1)}, bf16[128,2048]{1,0:T(8,128)(2,1)S(1)}, u32[]{:S(2)}, u32[]{:S(2)}) collective-permute-start(bf16[128,2048]{1,0:T(8,128)(2,1)} %collective-permute-done.20.refs_1_), channel_id=1, source_target_pairs={{0,4},{4,0},{8,12},{12,8},{16,20},{20,16},{24,28},{28,24},{1,5},{5... | collective-permute-start | bytes 1572872 | tf_op jit(solution)/shard_map/ppermute | solution.py:49
  125.1 21.7 %collective-permute-start.24 = (bf16[128,2048]{1,0:T(8,128)(2,1)}, bf16[128,2048]{1,0:T(8,128)(2,1)S(1)}, u32[]{:S(2)}, u32[]{:S(2)}) collective-permute-start(bf16[128,2048]{1,0:T(8,128)(2,1)} %pad_maximum_fusion.cot.refs_0_.refs_6_), channel_id=1, source_target_pairs={{0,24},{4,28},{8,16},{12,20},{16,8},{20,12},{24,0},{28,4},{1,25},{... | collective-permute-start | bytes 1572872 | tf_op jit(solution)/shard_map/ppermute | solution.py:49
  127.8 17.7 %collective-permute-start.29 = (bf16[32,2048]{1,0:T(8,128)(2,1)}, bf16[32,2048]{1,0:T(8,128)(2,1)S(1)}, u32[]{:S(2)}, u32[]{:S(2)}) collective-permute-start(bf16[32,2048]{1,0:T(8,128)(2,1)} %get-tuple-element.111), channel_id=1, source_target_pairs={{0,1},{1,0},{2,3},{3,2},{4,5},{5,4},{6,7},{7,6},{8,9},{9,8},{10,11... | collective-permute-start | bytes 393224 | tf_op jit(solution)/shard_map/ppermute | solution.py:710
  130.1 16.6 %collective-permute-start.30 = (bf16[32,2048]{1,0:T(8,128)(2,1)}, bf16[32,2048]{1,0:T(8,128)(2,1)S(1)}, u32[]{:S(2)}, u32[]{:S(2)}) collective-permute-start(bf16[32,2048]{1,0:T(8,128)(2,1)} %get-tuple-element.112), channel_id=1, source_target_pairs={{0,2},{1,3},{2,0},{3,1},{4,6},{5,7},{6,4},{7,5},{8,10},{9,11},{10,... | collective-permute-start | bytes 393224 | tf_op jit(solution)/shard_map/ppermute | solution.py:710
  132.1 14.7 %collective-permute-start.31 = (bf16[32,2048]{1,0:T(8,128)(2,1)S(1)}, bf16[32,2048]{1,0:T(8,128)(2,1)S(1)}, u32[]{:S(2)}, u32[]{:S(2)}) collective-permute-start(bf16[32,2048]{1,0:T(8,128)(2,1)S(1)} %copy-done.24), channel_id=1, source_target_pairs={{0,3},{1,2},{2,1},{3,0},{4,7},{5,6},{6,5},{7,4},{8,11},{9,10},{10,... | collective-permute-start | bytes 393224 | tf_op jit(solution)/shard_map/ppermute | solution.py:710
  133.5 0.8 copy-start.12
  133.5 25.5 %collective-permute-start.22 = (bf16[1,128,2304]{2,1,0:T(8,128)(2,1)}, bf16[1,128,2304]{2,1,0:T(8,128)(2,1)S(1)}, u32[]{:S(2)}, u32[]{:S(2)}) collective-permute-start(bf16[1,128,2304]{2,1,0:T(8,128)(2,1)} %get-tuple-element.98), channel_id=1, source_target_pairs={{0,16},{4,20},{8,24},{12,28},{16,0},{20,4},{24,8},{28,12},{1,17},{... | collective-permute-start | bytes 1769480 | tf_op jit(solution)/shard_map/ppermute | solution.py:49
  134.3 11.2 %copy-start.5 = (bf16[1,128,2304]{2,1,0:T(8,128)(2,1)S(1)}, bf16[1,128,2304]{2,1,0:T(8,128)(2,1)}, u32[]{:S(2)}) copy-start(bf16[1,128,2304]{2,1,0:T(8,128)(2,1)} %get-tuple-element.99) | copy-start | bytes 1769476
  134.3 12.5 %copy-start.19 = (bf16[32,2048]{1,0:T(8,128)(2,1)S(1)}, bf16[32,2048]{1,0:T(8,128)(2,1)}, u32[]{:S(2)}) copy-start(bf16[32,2048]{1,0:T(8,128)(2,1)} %get-tuple-element.93) | copy-start | bytes 393220
  145.5 14.5 %collective-permute-start.23 = (bf16[1,128,2304]{2,1,0:T(8,128)(2,1)S(1)}, bf16[1,128,2304]{2,1,0:T(8,128)(2,1)S(1)}, u32[]{:S(2)}, u32[]{:S(2)}) collective-permute-start(bf16[1,128,2304]{2,1,0:T(8,128)(2,1)S(1)} %copy-done.5), channel_id=1, source_target_pairs={{0,8},{4,12},{8,0},{12,4},{16,24},{20,28},{24,16},{28,20},{1,9},{5... | collective-permute-start | bytes 1769480 | tf_op jit(solution)/shard_map/ppermute | solution.py:49
  146.8 4.9 %copy-start.1 = (bf16[128,2048]{1,0:T(8,128)(2,1)}, bf16[128,2048]{1,0:T(8,128)(2,1)S(1)}, u32[]{:S(2)}) copy-start(bf16[128,2048]{1,0:T(8,128)(2,1)S(1)} %collective-permute-done.24.refs_0_.refs_2_) | copy-start | bytes 1572868
  146.8 3.4 %collective-permute-start.25 = (bf16[128,2048]{1,0:T(8,128)(2,1)S(1)}, bf16[128,2048]{1,0:T(8,128)(2,1)S(1)}, u32[]{:S(2)}, u32[]{:S(2)}) collective-permute-start(bf16[128,2048]{1,0:T(8,128)(2,1)S(1)} %collective-permute-done.24.refs_0_.refs_2_), channel_id=1, source_target_pairs={{0,4},{4,0},{8,12},{12,8},{16,20},{20,16},{24,28},{28,24},{1,5},{5... | collective-permute-start | bytes 1572872 | tf_op jit(solution)/shard_map/ppermute | solution.py:49
  147.2 11.8 %copy-start.18 = (bf16[32,2048]{1,0:T(8,128)(2,1)}, bf16[32,2048]{1,0:T(8,128)(2,1)S(1)}, u32[]{:S(2)}) copy-start(bf16[32,2048]{1,0:T(8,128)(2,1)S(1)} %fusion.8.refs_0_) | copy-start | bytes 393220
  147.2 12.8 %collective-permute-start.32 = (bf16[32,2048]{1,0:T(8,128)(2,1)S(1)}, bf16[32,2048]{1,0:T(8,128)(2,1)S(1)}, u32[]{:S(2)}, u32[]{:S(2)}) collective-permute-start(bf16[32,2048]{1,0:T(8,128)(2,1)S(1)} %fusion.8.refs_0_), channel_id=1, source_target_pairs={{0,1},{1,0},{2,3},{3,2},{4,5},{5,4},{6,7},{7,6},{8,9},{9,8},{10,11... | collective-permute-start | bytes 393224 | tf_op jit(solution)/shard_map/ppermute | solution.py:717
  147.8 12.9 %collective-permute-start.33 = (bf16[32,2048]{1,0:T(8,128)(2,1)S(1)}, bf16[32,2048]{1,0:T(8,128)(2,1)S(1)}, u32[]{:S(2)}, u32[]{:S(2)}) collective-permute-start(bf16[32,2048]{1,0:T(8,128)(2,1)S(1)} %fusion.8.refs_0_), channel_id=1, source_target_pairs={{0,2},{1,3},{2,0},{3,1},{4,6},{5,7},{6,4},{7,5},{8,10},{9,11},{10,... | collective-permute-start | bytes 393224 | tf_op jit(solution)/shard_map/ppermute | solution.py:717
  150.2 1.5 copy-start.15
  150.2 10.5 %collective-permute-start.34 = (bf16[32,2048]{1,0:T(8,128)(2,1)S(1)}, bf16[32,2048]{1,0:T(8,128)(2,1)S(1)}, u32[]{:S(2)}, u32[]{:S(2)}) collective-permute-start(bf16[32,2048]{1,0:T(8,128)(2,1)S(1)} %fusion.8.refs_0_), channel_id=1, source_target_pairs={{0,3},{1,2},{2,1},{3,0},{4,7},{5,6},{6,5},{7,4},{8,11},{9,10},{10,... | collective-permute-start | bytes 393224 | tf_op jit(solution)/shard_map/ppermute | solution.py:717
  159.0 1.7 %copy-start.6 = (bf16[1,128,2304]{2,1,0:T(8,128)(2,1)}, bf16[1,128,2304]{2,1,0:T(8,128)(2,1)S(1)}, u32[]{:S(2)}) copy-start(bf16[1,128,2304]{2,1,0:T(8,128)(2,1)S(1)} %collective-permute-done.22) | copy-start | bytes 1769476
  160.0 0.8 copy-start.7
  160.0 0.9 copy-start.20
  160.7 0.6 copy-start.21
  160.7 0.7 copy-start.22

commit v5 on v4

--- a/solution.py
+++ b/solution.py
@@ -462,17 +462,12 @@
     loads = [pltpu.make_async_copy(src, dst, sems.at[k]) for k, (src, dst) in enumerate(copies)]
     for load in loads:
         load.start()
-    for load in loads[:count]:
+    for load in loads:
         load.wait()
     if not narrow:
         column[...] = cot[:, pl.ds(pl.multiple_of(place_ref[2] * block, 128), block)]
-    downs, rest = loads[count : count + len(tiles(hid, TILE))], loads[count + len(tiles(hid, TILE)) :]
-    for k, to in enumerate(tiles(hid, TILE)):
-        downs[k].wait()
+    for to in tiles(hid, TILE):
         d_hidden = mm(cot[...], down[to, :], LAST)
-        if k == 0:
-            for load in rest:
-                load.wait()
         d_both[:, to] = (d_hidden * slope_gate[:, to].astype(F32)).astype(BF16)
         at = slice(hid + to.start, hid + to.stop)
         d_both[:, at] = (d_hidden * slope_up[:, to].astype(F32)).astype(BF16)
@@ -480,10 +475,12 @@
     down_part = mm(column[...], hidden[...], FIRST).T * scale
     parts = (both_part[:, :hid], both_part[:, hid:], down_part)
     for k, part in enumerate(parts):
-        outs[k][...] = part + earlier[k][...] if before else part
-
-
-def item_late(place, slots, pieces, column, normed, hidden, slope_up, slope_gate, w_down, before, scale):
+        outs[k][...] = (part + earlier[k][...].astype(F32) if before else part).astype(outs[k].dtype)
+
+
+def item_late(
+    place, slots, pieces, column, normed, hidden, slope_up, slope_gate, w_down, before, scale, kind
+):
     count = len(pieces)
     rows, width = count * pieces[0].shape[0], pieces[0].shape[1]
     hid, block = w_down.shape[0], normed.shape[1]
@@ -493,9 +490,9 @@
         in_specs=[smem()] + [hbm()] * (count + 6) + [vmem()] * len(before),
         out_specs=[vmem()] * 3,
         out_shape=[
-            jax.ShapeDtypeStruct((block, hid), F32),
-            jax.ShapeDtypeStruct((block, hid), F32),
-            jax.ShapeDtypeStruct((hid, block), F32),
+            jax.ShapeDtypeStruct((block, hid), kind),
+            jax.ShapeDtypeStruct((block, hid), kind),
+            jax.ShapeDtypeStruct((hid, block), kind),
         ],
         scratch_shapes=[
             pltpu.VMEM((rows, width), BF16),
@@ -760,6 +757,7 @@
             item_late(
                 place, [k % group for k in lot], parts, column, normed_k, hidden_k, slope_up_k,
                 slope_gate_k, item_down, before, 1.0 / n_wide,
+                F32 if lot is lots[-1] or len(lots) > 2 else BF16,
             )
         )
 

time: 166 us -> 165 us (level)
  no operation moved by 1% of the time
where the time goes in v5:
time: 165 us; the launch traced here: 164 us
  Pallas kernels  83.4 us (51%)
  starting transfers between devices  38.3 us (23%)
  waiting for transfers between devices  28.8 us (17%)
  other arithmetic  8.85 us (5%)
  local copies, waits for them, and re-layouts  4.21 us (3%)
    ppermute x23, starting transfers between devices, swap(): return lax.ppermute(value, 'wide', [(i, i ^ bit) for i in range(count)])  19.2 us
    pallas_call x1, Pallas kernels, user_layer(): pl.pallas_call(functools.partial(user_kernel, share, item_dev), in_specs=...  19.1 us
    pallas_call x2, Pallas kernels, item_late(): pl.pallas_call(functools.partial(late_kernel, tuple(slots), bool(before),...  17.1 us
    pallas_call x1, Pallas kernels, item_forward(): pl.pallas_call(functools.partial(forward_kernel, count, n_narrow), in_spe...  15 us
    ppermute x6, waiting for transfers between devices, narrow_slots(): lax.ppermute(piece, 'narrow', [(i, i ^ k) for i in range(n_narrow)])  10.1 us
    ppermute x6, starting transfers between devices, narrow_scatter(): lax.ppermute(part, 'narrow', [(i, i ^ k) for i in range(n_narrow)])  10.1 us
    ppermute x23, waiting for transfers between devices, swap(): return lax.ppermute(value, 'wide', [(i, i ^ bit) for i in range(count)])  10.1 us
    pallas_call x1, Pallas kernels, kept_grads(): pl.pallas_call(kept_kernel, grid_spec=pltpu.PrefetchScalarGridSpec(num_sc...  9.64 us
  transfers between devices with their start and end apart: 35, of which 10 were waited for; matrix products, arithmetic and copies ran while one was open for 6% of the time, Pallas kernels for 47%

profile of v5, /device:TPU:0, one launch (start us, length us, event | category | flops | bytes accessed | tf_op | source)
XLA Modules:
  0.0 164.4 jit_solution(7344680039790860390)
XLA Ops:
  0.6 3.0 %collective-permute-start = (bf16[128,2048]{1,0:T(8,128)(2,1)}, bf16[128,2048]{1,0:T(8,128)(2,1)S(1)}, u32[]{:S(2)}, u32[]{:S(2)}) collective-permute-start(bf16[128,2048]{1,0:T(8,128)(2,1)} %refs_0_.1), channel_id=1, source_target_pairs={{0,8},{4,12},{8,0},{12,4},{16,24},{20,28},{24,16},{28,20},{1,9},{5... | collective-permute-start | bytes 1572872 | tf_op jit(solution)/shard_map/ppermute | solution.py:49
  3.6 1.5 collective-permute-start.1
  5.2 0.7 pad_add_fusion.place_ref.table_ref
  5.8 19.1 %user_layer.1 = (bf16[512,2048]{1,0:T(8,128)(2,1)}, bf16[512,2048]{1,0:T(8,128)(2,1)}, bf16[512,768]{1,0:T(8,128)(2,1)}, bf16[512,1536]{1,0:T(8,128)(2,1)}, bf16...) custom-call(s32[4]{0:T(128)} %pad_add_fusion.place_ref.table_ref, s32[8]{0:T(128)} %hist_len_ref.1, ...), custom_call_target="tpu_custom_call" | custom-call | flops 1342177280 | bytes 4000000 | tf_op jit(solution)/shard_map/user_layer/pallas_call | solution.py:172
  25.0 3.5 %collective-permute-done.1.refs_2_ = bf16[128,2048]{1,0:T(8,128)(2,1)S(1)} collective-permute-done((bf16[128,2048]{1,0:T(8,128)(2,1)}, bf16[128,2048]{1,0:T(8,128)(2,1)S(1)}, u32[]{:S(2)}, u32[]{:S(2)}) %collective-permute-start.1) | collective-permute-done | bytes 524320 | tf_op jit(solution)/shard_map/ppermute | solution.py:49
  28.5 7.7 %sent_grads.1 = bf16[4,256,2304]{2,1,0:T(8,128)(2,1)} custom-call(s32[4]{0:T(128)} %pad_add_fusion.place_ref.table_ref, bf16[512,2048]{1,0:T(8,128)(2,1)} %get-tuple-element.67.normed_ref, bf16[512,2048]{1,0:T(8,128)(2,1)} %get-tuple-element.68.masked_ref, bf16[512,1536]{1,0:T(8,128)(2,1)} %get-tuple-element.69.d_both_ref, ...), custom_call_target="tpu_custom_call" | custom-call | flops 402653184 | bytes 1666666 | tf_op jit(solution)/shard_map/sent_grads/pallas_call | solution.py:256
  36.2 0.4 collective-permute-start.4
  36.6 0.1 collective-permute-start.5
  36.8 0.4 collective-permute-start.6
  37.1 0.1 collective-permute-start.7
  37.3 0.4 collective-permute-start.8
  37.6 2.8 %add_convert_fusion.4 = (bf16[128,2048]{1,0:T(8,128)(2,1)}, bf16[128,2048]{1,0:T(8,128)(2,1)}, bf16[128,2048]{1,0:T(8,128)(2,1)}) fusion(bf16[512,2048]{1,0:T(8,128)(2,1)} %collective-permute-done.3.got_ref, bf16[512,2048]{1,0:T(8,128)(2,1)S(1)} %copy-done), kind=kLoop, calls=%fused_computation.4 | loop fusion | flops 3145728 | bytes 4718592 | tf_op jit(solution)/shard_map/convert_element_type | solution.py:683
  40.5 2.1 %collective-permute-done.5.refs_4_ = bf16[128,2048]{1,0:T(8,128)(2,1)S(1)} collective-permute-done((bf16[128,2048]{1,0:T(8,128)(2,1)S(1)}, bf16[128,2048]{1,0:T(8,128)(2,1)S(1)}, u32[]{:S(2)}, u32[]{:S(2)}) %collective-permute-start.5) | collective-permute-done | bytes 524320 | tf_op jit(solution)/shard_map/ppermute | solution.py:49
  42.5 2.6 %collective-permute-start.9 = (bf16[128,2048]{1,0:T(8,128)(2,1)}, bf16[128,2048]{1,0:T(8,128)(2,1)S(1)}, u32[]{:S(2)}, u32[]{:S(2)}) collective-permute-start(bf16[128,2048]{1,0:T(8,128)(2,1)} %get-tuple-element.131), channel_id=1, source_target_pairs={{0,8},{4,12},{8,0},{12,4},{16,24},{20,28},{24,16},{28,20},{1,9},{5... | collective-permute-start | bytes 1572872 | tf_op jit(solution)/shard_map/ppermute | solution.py:49
  45.2 0.4 collective-permute-start.10
  45.6 0.4 copy-done.16
  46.0 2.2 %collective-permute-start.11 = (bf16[128,2048]{1,0:T(8,128)(2,1)}, bf16[128,2048]{1,0:T(8,128)(2,1)S(1)}, u32[]{:S(2)}, u32[]{:S(2)}) collective-permute-start(bf16[128,2048]{1,0:T(8,128)(2,1)} %get-tuple-element.129), channel_id=1, source_target_pairs={{0,24},{4,28},{8,16},{12,20},{16,8},{20,12},{24,0},{28,4},{1,25},{... | collective-permute-start | bytes 1572872 | tf_op jit(solution)/shard_map/ppermute | solution.py:49
  48.2 15.0 %item_forward.1 = (bf16[1024,256]{1,0:T(8,128)(2,1)}, bf16[1024,768]{1,0:T(8,128)(2,1)}, bf16[1024,768]{1,0:T(8,128)(2,1)}, bf16[1024,768]{1,0:T(8,128)(2,1)}) custom-call(s32[4]{0:T(128)} %pad_add_fusion.place_ref.table_ref, bf16[2048]{0:T(1024)(128)(2,1)} %gain_ref.3, bf16[128,2048]{1,0:T(8,128)(2,1)} %refs_0_.1, bf16[128,2048]{1,0:T(8,128)(2,1)} %copy-done.8, ...), custom_call_target="tpu_custom_call" | custom-call | flops 1073741824 | bytes 2666666 | tf_op jit(solution)/shard_map/item_forward/pallas_call | solution.py:375
  63.3 9.6 %kept_grads.1 = (bf16[2,128,2304]{2,1,0:T(8,128)(2,1)}, bf16[2,128,2304]{2,1,0:T(8,128)(2,1)}, bf16[2,128,2304]{2,1,0:T(8,128)(2,1)}, bf16[2,128,2304]{2,1,0:T(8,128)(2,1)}) custom-call(s32[4]{0:T(128)} %pad_add_fusion.place_ref.table_ref, s32[7,4]{1,0:T(8,128)} %constant.48.clone.table_ref, bf16[512,2048]{1,0:T(8,128)(2,1)} %get-tuple-element.67.normed_ref, ...), custom_call_target="tpu_custom_call" | custom-call | flops 402653184 | bytes 2500000 | tf_op jit(solution)/shard_map/kept_grads/pallas_call | solution.py:279
  73.0 0.8 copy-done.10
  73.7 0.2 copy-done.11
  73.9 0.8 copy-done.13
  74.7 3.1 %merge_chips.1 = (bf16[32,2048]{1,0:T(8,128)(2,1)}, bf16[32,2048]{1,0:T(8,128)(2,1)}, bf16[32,2048]{1,0:T(8,128)(2,1)}, bf16[32,2048]{1,0:T(8,128)(2,1)}) custom-call(s32[1]{0:T(128)} %bitcast.here_ref, bf16[512,2048]{1,0:T(8,128)(2,1)} %get-tuple-element.77.kept_ref, bf16[512,2048]{1,0:T(8,128)(2,1)} %collective-permute-done.3.got_ref, ...), custom_call_target="tpu_custom_call" | custom-call | bytes 611669 | tf_op jit(solution)/shard_map/merge_chips/pallas_call | solution.py:536
  77.8 1.6 collective-permute-start.14
  79.4 2.6 %collective-permute-start.15 = (bf16[32,2048]{1,0:T(8,128)(2,1)}, bf16[32,2048]{1,0:T(8,128)(2,1)S(1)}, u32[]{:S(2)}, u32[]{:S(2)}) collective-permute-start(bf16[32,2048]{1,0:T(8,128)(2,1)} %get-tuple-element.89), channel_id=1, source_target_pairs={{0,2},{1,3},{2,0},{3,1},{4,6},{5,7},{6,4},{7,5},{8,10},{9,11},{10,... | collective-permute-start | bytes 393224 | tf_op jit(solution)/shard_map/ppermute | solution.py:707
  82.0 0.2 collective-permute-start.16
  82.2 0.7 collective-permute-start.12
  82.9 0.7 collective-permute-start.13
  83.7 0.8 collective-permute-done.14
  84.5 7.8 %collective-permute-done.15 = bf16[32,2048]{1,0:T(8,128)(2,1)S(1)} collective-permute-done((bf16[32,2048]{1,0:T(8,128)(2,1)}, bf16[32,2048]{1,0:T(8,128)(2,1)S(1)}, u32[]{:S(2)}, u32[]{:S(2)}) %collective-permute-start.15) | collective-permute-done | bytes 131104 | tf_op jit(solution)/shard_map/ppermute | solution.py:707
  92.3 1.0 fusion.10
  93.3 2.0 %collective-permute-start.17 = (bf16[32,2048]{1,0:T(8,128)(2,1)S(1)}, bf16[32,2048]{1,0:T(8,128)(2,1)S(1)}, u32[]{:S(2)}, u32[]{:S(2)}) collective-permute-start(bf16[32,2048]{1,0:T(8,128)(2,1)S(1)} %get-tuple-element.127), channel_id=1, source_target_pairs={{0,1},{1,0},{2,3},{3,2},{4,5},{5,4},{6,7},{7,6},{8,9},{9,8},{10,11... | collective-permute-start | bytes 393224 | tf_op jit(solution)/shard_map/ppermute | solution.py:714
  95.3 1.1 collective-permute-start.18
  96.4 1.4 collective-permute-start.19
  97.8 1.9 %collective-permute-done.17 = bf16[32,2048]{1,0:T(8,128)(2,1)S(1)} collective-permute-done((bf16[32,2048]{1,0:T(8,128)(2,1)S(1)}, bf16[32,2048]{1,0:T(8,128)(2,1)S(1)}, u32[]{:S(2)}, u32[]{:S(2)}) %collective-permute-start.17) | collective-permute-done | bytes 131104 | tf_op jit(solution)/shard_map/ppermute | solution.py:714
  99.7 7.4 %collective-permute-done.18 = bf16[32,2048]{1,0:T(8,128)(2,1)S(1)} collective-permute-done((bf16[32,2048]{1,0:T(8,128)(2,1)S(1)}, bf16[32,2048]{1,0:T(8,128)(2,1)S(1)}, u32[]{:S(2)}, u32[]{:S(2)}) %collective-permute-start.18) | collective-permute-done | bytes 131104 | tf_op jit(solution)/shard_map/ppermute | solution.py:714
  107.1 0.8 pad_maximum_fusion.cot.refs_0_.refs_6_
  108.0 1.8 %collective-permute-start.20 = (bf16[128,2048]{1,0:T(8,128)(2,1)}, bf16[128,2048]{1,0:T(8,128)(2,1)}, u32[]{:S(2)}, u32[]{:S(2)}) collective-permute-start(bf16[128,2048]{1,0:T(8,128)(2,1)} %pad_maximum_fusion.cot.refs_0_.refs_6_), channel_id=1, source_target_pairs={{0,8},{4,12},{8,0},{12,4},{16,24},{20,28},{24,16},{28,20},{1,9},{5... | collective-permute-start | bytes 1572872 | tf_op jit(solution)/shard_map/ppermute | solution.py:49
  109.8 0.8 collective-permute-start.21
  110.6 8.0 %item_own.1 = (bf16[32,2048]{1,0:T(8,128)(2,1)}, bf16[32,2048]{1,0:T(8,128)(2,1)}, bf16[32,2048]{1,0:T(8,128)(2,1)}, bf16[32,2048]{1,0:T(8,128)(2,1)}) custom-call(bf16[128,2048]{1,0:T(8,128)(2,1)} %pad_maximum_fusion.cot.refs_0_.refs_6_, bf16[1024,768]{1,0:T(8,128)(2,1)} %get-tuple-element.91.slope_up.refs_9_.refs_5_, ...), custom_call_target="tpu_custom_call" | custom-call | flops 201326592 | bytes 1833333 | tf_op jit(solution)/shard_map/item_own/pallas_call | solution.py:422
  118.6 1.8 %collective-permute-done.20.refs_1_ = bf16[128,2048]{1,0:T(8,128)(2,1)} collective-permute-done((bf16[128,2048]{1,0:T(8,128)(2,1)}, bf16[128,2048]{1,0:T(8,128)(2,1)}, u32[]{:S(2)}, u32[]{:S(2)}) %collective-permute-start.20) | collective-permute-done | bytes 524320 | tf_op jit(solution)/shard_map/ppermute | solution.py:49
  120.4 1.1 collective-permute-done.21.refs_2_
  121.6 3.0 %add_convert_fusion.2 = (bf16[1,128,2304]{2,1,0:T(8,128)(2,1)}, bf16[128,2304]{1,0:T(8,128)(2,1)}, bf16[1,128,2304]{2,1,0:T(8,128)(2,1)}, bf16[128,2304]{1,0:T(8,128)(2,1)}) fusion(bf16[2,128,2304]{2,1,0:T(8,128)(2,1)S(1)} %collective-permute-done.12, bf16[2,128,2304]{2,1,0:T(8,128)(2,1)S(1)} %copy-done.2, bf16[2,128,2304]{2,1,0:T(8,128)(2,1)} %collective-permute-done.13, ...), kind=kLoop, calls=%fused_computation.2 | loop fusion | flops 4718592 | bytes 7077888 | tf_op jit(solution)/shard_map/convert_element_type | solution.py:605
  124.6 0.5 collective-permute-start.27
  125.1 1.8 %collective-permute-start.24 = (bf16[128,2048]{1,0:T(8,128)(2,1)}, bf16[128,2048]{1,0:T(8,128)(2,1)S(1)}, u32[]{:S(2)}, u32[]{:S(2)}) collective-permute-start(bf16[128,2048]{1,0:T(8,128)(2,1)} %pad_maximum_fusion.cot.refs_0_.refs_6_), channel_id=1, source_target_pairs={{0,24},{4,28},{8,16},{12,20},{16,8},{20,12},{24,0},{28,4},{1,25},{... | collective-permute-start | bytes 1572872 | tf_op jit(solution)/shard_map/ppermute | solution.py:49
  126.9 0.9 constant_dynamic-slice_fusion
  127.8 2.3 %collective-permute-start.29 = (bf16[32,2048]{1,0:T(8,128)(2,1)}, bf16[32,2048]{1,0:T(8,128)(2,1)S(1)}, u32[]{:S(2)}, u32[]{:S(2)}) collective-permute-start(bf16[32,2048]{1,0:T(8,128)(2,1)} %get-tuple-element.111), channel_id=1, source_target_pairs={{0,1},{1,0},{2,3},{3,2},{4,5},{5,4},{6,7},{7,6},{8,9},{9,8},{10,11... | collective-permute-start | bytes 393224 | tf_op jit(solution)/shard_map/ppermute | solution.py:707
  130.1 1.9 %collective-permute-start.30 = (bf16[32,2048]{1,0:T(8,128)(2,1)}, bf16[32,2048]{1,0:T(8,128)(2,1)S(1)}, u32[]{:S(2)}, u32[]{:S(2)}) collective-permute-start(bf16[32,2048]{1,0:T(8,128)(2,1)} %get-tuple-element.112), channel_id=1, source_target_pairs={{0,2},{1,3},{2,0},{3,1},{4,6},{5,7},{6,4},{7,5},{8,10},{9,11},{10,... | collective-permute-start | bytes 393224 | tf_op jit(solution)/shard_map/ppermute | solution.py:707
  132.1 1.5 collective-permute-start.31
  133.5 0.4 collective-permute-start.22
  133.9 0.4 copy-done.12
  134.3 10.4 %item_late.2 = (bf16[256,768]{1,0:T(8,128)(2,1)}, bf16[256,768]{1,0:T(8,128)(2,1)}, bf16[768,256]{1,0:T(8,128)(2,1)}) custom-call(s32[4]{0:T(128)} %pad_add_fusion.place_ref.table_ref, bf16[128,2048]{1,0:T(8,128)(2,1)} %pad_maximum_fusion.cot.refs_0_.refs_6_, bf16[128,2048]{1,0:T(8,128)(2,1)} %collective-permute-done.20.refs_1_, ...), custom_call_target="tpu_custom_call" | custom-call | flops 1107296256 | bytes 2666666 | tf_op jit(solution)/shard_map/item_late/pallas_call | solution.py:488
  144.7 0.1 fusion.9
  144.9 1.3 collective-permute-start.23
  146.2 0.2 fusion.4
  146.4 0.1 fusion.8.refs_0_
  146.5 0.6 collective-permute-start.32
  147.2 2.4 %collective-permute-start.33 = (bf16[32,2048]{1,0:T(8,128)(2,1)S(1)}, bf16[32,2048]{1,0:T(8,128)(2,1)S(1)}, u32[]{:S(2)}, u32[]{:S(2)}) collective-permute-start(bf16[32,2048]{1,0:T(8,128)(2,1)S(1)} %fusion.8.refs_0_), channel_id=1, source_target_pairs={{0,2},{1,3},{2,0},{3,1},{4,6},{5,7},{6,4},{7,5},{8,10},{9,11},{10,... | collective-permute-start | bytes 393224 | tf_op jit(solution)/shard_map/ppermute | solution.py:714
  149.6 1.5 collective-permute-start.34
  151.0 6.8 %item_late.3 = (f32[256,768]{1,0:T(8,128)}, f32[256,768]{1,0:T(8,128)}, f32[768,256]{1,0:T(8,128)}) custom-call(s32[4]{0:T(128)} %pad_add_fusion.place_ref.table_ref, bf16[128,2048]{1,0:T(8,128)(2,1)} %copy-done.1, bf16[128,2048]{1,0:T(8,128)(2,1)} %copy-done.15, bf16[128,2048]{1,0:T(8,128)(2,1)} %copy-done.1, ...), custom_call_target="tpu_custom_call" | custom-call | flops 369098752 | bytes 2666666 | tf_op jit(solution)/shard_map/item_late/pallas_call | solution.py:488
  157.8 1.6 collective-permute-done.23
  159.4 0.7 collective-permute-done.33.refs_2_
  160.2 0.5 copy-done.21
  160.8 3.6 %final_sums.1 = (bf16[128,2048]{1,0:T(8,128)(2,1)}, f32[256,768]{1,0:T(8,128)}, f32[256,768]{1,0:T(8,128)}, f32[768,256]{1,0:T(8,128)}) custom-call(s32[1]{0:T(128)} %bitcast.here_ref, bf16[128,2304]{1,0:T(8,128)(2,1)} %get-tuple-element.135.kept_a, bf16[128,2304]{1,0:T(8,128)(2,1)} %bitcast.14, bf16[128,2304]{1,0:T(8,128)(2,1)} %get-tuple-element.137.kept_b, ...), custom_call_target="tpu_custom_call" | custom-call | bytes 491520 | tf_op jit(solution)/shard_map/final_sums/pallas_call | solution.py:566
  (77 shorter events, 0.4 us)
Async XLA Ops:
  0.6 24.3 %collective-permute-start = (bf16[128,2048]{1,0:T(8,128)(2,1)}, bf16[128,2048]{1,0:T(8,128)(2,1)S(1)}, u32[]{:S(2)}, u32[]{:S(2)}) collective-permute-start(bf16[128,2048]{1,0:T(8,128)(2,1)} %refs_0_.1), channel_id=1, source_target_pairs={{0,8},{4,12},{8,0},{12,4},{16,24},{20,28},{24,16},{28,20},{1,9},{5... | collective-permute-start | bytes 1572872 | tf_op jit(solution)/shard_map/ppermute | solution.py:49
  3.6 24.8 %collective-permute-start.1 = (bf16[128,2048]{1,0:T(8,128)(2,1)}, bf16[128,2048]{1,0:T(8,128)(2,1)S(1)}, u32[]{:S(2)}, u32[]{:S(2)}) collective-permute-start(bf16[128,2048]{1,0:T(8,128)(2,1)} %refs_0_.1), channel_id=1, source_target_pairs={{0,16},{4,20},{8,24},{12,28},{16,0},{20,4},{24,8},{28,12},{1,17},{... | collective-permute-start | bytes 1572872 | tf_op jit(solution)/shard_map/ppermute | solution.py:49
  5.2 23.3 %collective-permute-start.2 = (bf16[128,2048]{1,0:T(8,128)(2,1)}, bf16[128,2048]{1,0:T(8,128)(2,1)}, u32[]{:S(2)}, u32[]{:S(2)}) collective-permute-start(bf16[128,2048]{1,0:T(8,128)(2,1)} %refs_0_.1), channel_id=1, source_target_pairs={{0,24},{4,28},{8,16},{12,20},{16,8},{20,12},{24,0},{28,4},{1,25},{... | collective-permute-start | bytes 1572872 | tf_op jit(solution)/shard_map/ppermute | solution.py:49
  25.0 11.8 %copy-start.8 = (bf16[128,2048]{1,0:T(8,128)(2,1)}, bf16[128,2048]{1,0:T(8,128)(2,1)S(1)}, u32[]{:S(2)}) copy-start(bf16[128,2048]{1,0:T(8,128)(2,1)S(1)} %collective-permute-done.refs_1_) | copy-start | bytes 1572868
  28.5 8.7 %copy-start.9 = (bf16[128,2048]{1,0:T(8,128)(2,1)}, bf16[128,2048]{1,0:T(8,128)(2,1)S(1)}, u32[]{:S(2)}) copy-start(bf16[128,2048]{1,0:T(8,128)(2,1)S(1)} %collective-permute-done.1.refs_2_) | copy-start | bytes 1572868
  28.5 7.8 %collective-permute-start.3 = (bf16[512,2048]{1,0:T(8,128)(2,1)}, bf16[512,2048]{1,0:T(8,128)(2,1)}, u32[]{:S(2)}, u32[]{:S(2)}) collective-permute-start(bf16[512,2048]{1,0:T(8,128)(2,1)} %get-tuple-element.72), channel_id=1, source_target_pairs={{0,4},{4,0},{8,12},{12,8},{16,20},{20,16},{24,28},{28,24},{1,5},{5... | collective-permute-start | bytes 6291464 | tf_op jit(solution)/shard_map/ppermute | solution.py:49
  28.5 8.1 %copy-start.4 = (bf16[128,2048]{1,0:T(8,128)(2,1)S(1)}, bf16[128,2048]{1,0:T(8,128)(2,1)}, u32[]{:S(2)}) copy-start(bf16[128,2048]{1,0:T(8,128)(2,1)} %refs_0_.1) | copy-start | bytes 1572868
  28.5 9.1 %copy-start = (bf16[512,2048]{1,0:T(8,128)(2,1)S(1)}, bf16[512,2048]{1,0:T(8,128)(2,1)}, u32[]{:S(2)}) copy-start(bf16[512,2048]{1,0:T(8,128)(2,1)} %get-tuple-element.77.kept_ref) | copy-start | bytes 6291460
  36.2 27.1 %collective-permute-start.4 = (bf16[4,256,2304]{2,1,0:T(8,128)(2,1)}, bf16[4,256,2304]{2,1,0:T(8,128)(2,1)}, u32[]{:S(2)}, u32[]{:S(2)}) collective-permute-start(bf16[4,256,2304]{2,1,0:T(8,128)(2,1)} %sent_grads.1), channel_id=1, source_target_pairs={{0,4},{4,0},{8,12},{12,8},{16,20},{20,16},{24,28},{28,24},{1,5},{5... | collective-permute-start | bytes 14155784 | tf_op jit(solution)/shard_map/ppermute | solution.py:49
  36.6 5.9 %collective-permute-start.5 = (bf16[128,2048]{1,0:T(8,128)(2,1)S(1)}, bf16[128,2048]{1,0:T(8,128)(2,1)S(1)}, u32[]{:S(2)}, u32[]{:S(2)}) collective-permute-start(bf16[128,2048]{1,0:T(8,128)(2,1)S(1)} %copy-done.4), channel_id=1, source_target_pairs={{0,4},{4,0},{8,12},{12,8},{16,20},{20,16},{24,28},{28,24},{1,5},{5... | collective-permute-start | bytes 1572872 | tf_op jit(solution)/shard_map/ppermute | solution.py:49
  36.8 8.4 %collective-permute-start.6 = (bf16[128,2048]{1,0:T(8,128)(2,1)S(1)}, bf16[128,2048]{1,0:T(8,128)(2,1)S(1)}, u32[]{:S(2)}, u32[]{:S(2)}) collective-permute-start(bf16[128,2048]{1,0:T(8,128)(2,1)S(1)} %collective-permute-done.refs_1_), channel_id=1, source_target_pairs={{0,4},{4,0},{8,12},{12,8},{16,20},{20,16},{24,28},{28,24},{1,5},{5... | collective-permute-start | bytes 1572872 | tf_op jit(solution)/shard_map/ppermute | solution.py:49
  37.1 8.4 %collective-permute-start.7 = (bf16[128,2048]{1,0:T(8,128)(2,1)S(1)}, bf16[128,2048]{1,0:T(8,128)(2,1)S(1)}, u32[]{:S(2)}, u32[]{:S(2)}) collective-permute-start(bf16[128,2048]{1,0:T(8,128)(2,1)S(1)} %collective-permute-done.1.refs_2_), channel_id=1, source_target_pairs={{0,4},{4,0},{8,12},{12,8},{16,20},{20,16},{24,28},{28,24},{1,5},{5... | collective-permute-start | bytes 1572872 | tf_op jit(solution)/shard_map/ppermute | solution.py:49
  37.3 11.0 %collective-permute-start.8 = (bf16[128,2048]{1,0:T(8,128)(2,1)}, bf16[128,2048]{1,0:T(8,128)(2,1)}, u32[]{:S(2)}, u32[]{:S(2)}) collective-permute-start(bf16[128,2048]{1,0:T(8,128)(2,1)} %collective-permute-done.2.refs_3_), channel_id=1, source_target_pairs={{0,4},{4,0},{8,12},{12,8},{16,20},{20,16},{24,28},{28,24},{1,5},{5... | collective-permute-start | bytes 1572872 | tf_op jit(solution)/shard_map/ppermute | solution.py:49
  42.5 3.0 %copy-start.14 = (bf16[128,2048]{1,0:T(8,128)(2,1)}, bf16[128,2048]{1,0:T(8,128)(2,1)S(1)}, u32[]{:S(2)}) copy-start(bf16[128,2048]{1,0:T(8,128)(2,1)S(1)} %collective-permute-done.5.refs_4_) | copy-start | bytes 1572868
  42.5 30.4 %collective-permute-start.9 = (bf16[128,2048]{1,0:T(8,128)(2,1)}, bf16[128,2048]{1,0:T(8,128)(2,1)S(1)}, u32[]{:S(2)}, u32[]{:S(2)}) collective-permute-start(bf16[128,2048]{1,0:T(8,128)(2,1)} %get-tuple-element.131), channel_id=1, source_target_pairs={{0,8},{4,12},{8,0},{12,4},{16,24},{20,28},{24,16},{28,20},{1,9},{5... | collective-permute-start | bytes 1572872 | tf_op jit(solution)/shard_map/ppermute | solution.py:49
  45.2 0.8 copy-start.16
  45.2 27.8 %collective-permute-start.10 = (bf16[128,2048]{1,0:T(8,128)(2,1)}, bf16[128,2048]{1,0:T(8,128)(2,1)S(1)}, u32[]{:S(2)}, u32[]{:S(2)}) collective-permute-start(bf16[128,2048]{1,0:T(8,128)(2,1)} %get-tuple-element.130), channel_id=1, source_target_pairs={{0,16},{4,20},{8,24},{12,28},{16,0},{20,4},{24,8},{28,12},{1,17},{... | collective-permute-start | bytes 1572872 | tf_op jit(solution)/shard_map/ppermute | solution.py:49
  45.6 2.7 %copy-start.17 = (bf16[128,2048]{1,0:T(8,128)(2,1)}, bf16[128,2048]{1,0:T(8,128)(2,1)S(1)}, u32[]{:S(2)}) copy-start(bf16[128,2048]{1,0:T(8,128)(2,1)S(1)} %collective-permute-done.7.refs_6_) | copy-start | bytes 1572868
  46.0 27.0 %collective-permute-start.11 = (bf16[128,2048]{1,0:T(8,128)(2,1)}, bf16[128,2048]{1,0:T(8,128)(2,1)S(1)}, u32[]{:S(2)}, u32[]{:S(2)}) collective-permute-start(bf16[128,2048]{1,0:T(8,128)(2,1)} %get-tuple-element.129), channel_id=1, source_target_pairs={{0,24},{4,28},{8,16},{12,20},{16,8},{20,12},{24,0},{28,4},{1,25},{... | collective-permute-start | bytes 1572872 | tf_op jit(solution)/shard_map/ppermute | solution.py:49
  72.9 0.8 copy-start.10
  73.0 0.9 copy-start.11
  73.9 0.8 copy-start.13
  77.8 6.7 %collective-permute-start.14 = (bf16[32,2048]{1,0:T(8,128)(2,1)}, bf16[32,2048]{1,0:T(8,128)(2,1)S(1)}, u32[]{:S(2)}, u32[]{:S(2)}) collective-permute-start(bf16[32,2048]{1,0:T(8,128)(2,1)} %get-tuple-element.88), channel_id=1, source_target_pairs={{0,1},{1,0},{2,3},{3,2},{4,5},{5,4},{6,7},{7,6},{8,9},{9,8},{10,11... | collective-permute-start | bytes 393224 | tf_op jit(solution)/shard_map/ppermute | solution.py:707
  79.4 12.9 %collective-permute-start.15 = (bf16[32,2048]{1,0:T(8,128)(2,1)}, bf16[32,2048]{1,0:T(8,128)(2,1)S(1)}, u32[]{:S(2)}, u32[]{:S(2)}) collective-permute-start(bf16[32,2048]{1,0:T(8,128)(2,1)} %get-tuple-element.89), channel_id=1, source_target_pairs={{0,2},{1,3},{2,0},{3,1},{4,6},{5,7},{6,4},{7,5},{8,10},{9,11},{10,... | collective-permute-start | bytes 393224 | tf_op jit(solution)/shard_map/ppermute | solution.py:707
  82.0 10.3 %collective-permute-start.16 = (bf16[32,2048]{1,0:T(8,128)(2,1)}, bf16[32,2048]{1,0:T(8,128)(2,1)S(1)}, u32[]{:S(2)}, u32[]{:S(2)}) collective-permute-start(bf16[32,2048]{1,0:T(8,128)(2,1)} %get-tuple-element.90), channel_id=1, source_target_pairs={{0,3},{1,2},{2,1},{3,0},{4,7},{5,6},{6,5},{7,4},{8,11},{9,10},{10,... | collective-permute-start | bytes 393224 | tf_op jit(solution)/shard_map/ppermute | solution.py:707
  82.2 39.3 %collective-permute-start.12 = (bf16[2,128,2304]{2,1,0:T(8,128)(2,1)}, bf16[2,128,2304]{2,1,0:T(8,128)(2,1)S(1)}, u32[]{:S(2)}, u32[]{:S(2)}) collective-permute-start(bf16[2,128,2304]{2,1,0:T(8,128)(2,1)} %get-tuple-element.85), channel_id=1, source_target_pairs={{0,8},{4,12},{8,0},{12,4},{16,24},{20,28},{24,16},{28,20},{1,9},{5... | collective-permute-start | bytes 3538952 | tf_op jit(solution)/shard_map/ppermute | solution.py:49
  82.9 38.6 %collective-permute-start.13 = (bf16[2,128,2304]{2,1,0:T(8,128)(2,1)}, bf16[2,128,2304]{2,1,0:T(8,128)(2,1)}, u32[]{:S(2)}, u32[]{:S(2)}) collective-permute-start(bf16[2,128,2304]{2,1,0:T(8,128)(2,1)} %get-tuple-element.86), channel_id=1, source_target_pairs={{0,16},{4,20},{8,24},{12,28},{16,0},{20,4},{24,8},{28,12},{1,17},{... | collective-permute-start | bytes 3538952 | tf_op jit(solution)/shard_map/ppermute | solution.py:49
  93.3 6.4 %collective-permute-start.17 = (bf16[32,2048]{1,0:T(8,128)(2,1)S(1)}, bf16[32,2048]{1,0:T(8,128)(2,1)S(1)}, u32[]{:S(2)}, u32[]{:S(2)}) collective-permute-start(bf16[32,2048]{1,0:T(8,128)(2,1)S(1)} %get-tuple-element.127), channel_id=1, source_target_pairs={{0,1},{1,0},{2,3},{3,2},{4,5},{5,4},{6,7},{7,6},{8,9},{9,8},{10,11... | collective-permute-start | bytes 393224 | tf_op jit(solution)/shard_map/ppermute | solution.py:714
  95.3 11.9 %collective-permute-start.18 = (bf16[32,2048]{1,0:T(8,128)(2,1)S(1)}, bf16[32,2048]{1,0:T(8,128)(2,1)S(1)}, u32[]{:S(2)}, u32[]{:S(2)}) collective-permute-start(bf16[32,2048]{1,0:T(8,128)(2,1)S(1)} %get-tuple-element.127), channel_id=1, source_target_pairs={{0,2},{1,3},{2,0},{3,1},{4,6},{5,7},{6,4},{7,5},{8,10},{9,11},{10,... | collective-permute-start | bytes 393224 | tf_op jit(solution)/shard_map/ppermute | solution.py:714
  96.4 10.8 %collective-permute-start.19 = (bf16[32,2048]{1,0:T(8,128)(2,1)S(1)}, bf16[32,2048]{1,0:T(8,128)(2,1)S(1)}, u32[]{:S(2)}, u32[]{:S(2)}) collective-permute-start(bf16[32,2048]{1,0:T(8,128)(2,1)S(1)} %get-tuple-element.127), channel_id=1, source_target_pairs={{0,3},{1,2},{2,1},{3,0},{4,7},{5,6},{6,5},{7,4},{8,11},{9,10},{10,... | collective-permute-start | bytes 393224 | tf_op jit(solution)/shard_map/ppermute | solution.py:714
  108.0 12.4 %collective-permute-start.20 = (bf16[128,2048]{1,0:T(8,128)(2,1)}, bf16[128,2048]{1,0:T(8,128)(2,1)}, u32[]{:S(2)}, u32[]{:S(2)}) collective-permute-start(bf16[128,2048]{1,0:T(8,128)(2,1)} %pad_maximum_fusion.cot.refs_0_.refs_6_), channel_id=1, source_target_pairs={{0,8},{4,12},{8,0},{12,4},{16,24},{20,28},{24,16},{28,20},{1,9},{5... | collective-permute-start | bytes 1572872 | tf_op jit(solution)/shard_map/ppermute | solution.py:49
  109.8 11.7 %collective-permute-start.21 = (bf16[128,2048]{1,0:T(8,128)(2,1)}, bf16[128,2048]{1,0:T(8,128)(2,1)}, u32[]{:S(2)}, u32[]{:S(2)}) collective-permute-start(bf16[128,2048]{1,0:T(8,128)(2,1)} %pad_maximum_fusion.cot.refs_0_.refs_6_), channel_id=1, source_target_pairs={{0,16},{4,20},{8,24},{12,28},{16,0},{20,4},{24,8},{28,12},{1,17},{... | collective-permute-start | bytes 1572872 | tf_op jit(solution)/shard_map/ppermute | solution.py:49
  110.6 19.5 %collective-permute-start.26 = (bf16[128,2048]{1,0:T(8,128)(2,1)}, bf16[128,2048]{1,0:T(8,128)(2,1)}, u32[]{:S(2)}, u32[]{:S(2)}) collective-permute-start(bf16[128,2048]{1,0:T(8,128)(2,1)} %pad_maximum_fusion.cot.refs_0_.refs_6_), channel_id=1, source_target_pairs={{0,4},{4,0},{8,12},{12,8},{16,20},{20,16},{24,28},{28,24},{1,5},{5... | collective-permute-start | bytes 1572872 | tf_op jit(solution)/shard_map/ppermute | solution.py:49
  110.6 10.9 %copy-start.2 = (bf16[2,128,2304]{2,1,0:T(8,128)(2,1)S(1)}, bf16[2,128,2304]{2,1,0:T(8,128)(2,1)}, u32[]{:S(2)}) copy-start(bf16[2,128,2304]{2,1,0:T(8,128)(2,1)} %get-tuple-element.76) | copy-start | bytes 3538948
  110.6 10.9 %copy-start.3 = (bf16[2,128,2304]{2,1,0:T(8,128)(2,1)S(1)}, bf16[2,128,2304]{2,1,0:T(8,128)(2,1)}, u32[]{:S(2)}) copy-start(bf16[2,128,2304]{2,1,0:T(8,128)(2,1)} %get-tuple-element.95) | copy-start | bytes 3538948
  121.5 10.6 %collective-permute-start.28 = (bf16[128,2048]{1,0:T(8,128)(2,1)}, bf16[128,2048]{1,0:T(8,128)(2,1)}, u32[]{:S(2)}, u32[]{:S(2)}) collective-permute-start(bf16[128,2048]{1,0:T(8,128)(2,1)} %collective-permute-done.21.refs_2_), channel_id=1, source_target_pairs={{0,4},{4,0},{8,12},{12,8},{16,20},{20,16},{24,28},{28,24},{1,5},{5... | collective-permute-start | bytes 1572872 | tf_op jit(solution)/shard_map/ppermute | solution.py:49
  121.5 6.3 %copy-start.23 = (bf16[2048]{0:T(1024)(128)(2,1)S(1)}, bf16[2048]{0:T(1024)(128)(2,1)}, u32[]{:S(2)}) copy-start(bf16[2048]{0:T(1024)(128)(2,1)} %gain_ref.3) | copy-start | bytes 12292
  121.5 10.5 %copy-start.24 = (bf16[32,2048]{1,0:T(8,128)(2,1)S(1)}, bf16[32,2048]{1,0:T(8,128)(2,1)}, u32[]{:S(2)}) copy-start(bf16[32,2048]{1,0:T(8,128)(2,1)} %get-tuple-element.113) | copy-start | bytes 393220
  124.6 8.9 %collective-permute-start.27 = (bf16[128,2048]{1,0:T(8,128)(2,1)}, bf16[128,2048]{1,0:T(8,128)(2,1)S(1)}, u32[]{:S(2)}, u32[]{:S(2)}) collective-permute-start(bf16[128,2048]{1,0:T(8,128)(2,1)} %collective-permute-done.20.refs_1_), channel_id=1, source_target_pairs={{0,4},{4,0},{8,12},{12,8},{16,20},{20,16},{24,28},{28,24},{1,5},{5... | collective-permute-start | bytes 1572872 | tf_op jit(solution)/shard_map/ppermute | solution.py:49
  125.1 21.0 %collective-permute-start.24 = (bf16[128,2048]{1,0:T(8,128)(2,1)}, bf16[128,2048]{1,0:T(8,128)(2,1)S(1)}, u32[]{:S(2)}, u32[]{:S(2)}) collective-permute-start(bf16[128,2048]{1,0:T(8,128)(2,1)} %pad_maximum_fusion.cot.refs_0_.refs_6_), channel_id=1, source_target_pairs={{0,24},{4,28},{8,16},{12,20},{16,8},{20,12},{24,0},{28,4},{1,25},{... | collective-permute-start | bytes 1572872 | tf_op jit(solution)/shard_map/ppermute | solution.py:49
  127.8 17.0 %collective-permute-start.29 = (bf16[32,2048]{1,0:T(8,128)(2,1)}, bf16[32,2048]{1,0:T(8,128)(2,1)S(1)}, u32[]{:S(2)}, u32[]{:S(2)}) collective-permute-start(bf16[32,2048]{1,0:T(8,128)(2,1)} %get-tuple-element.111), channel_id=1, source_target_pairs={{0,1},{1,0},{2,3},{3,2},{4,5},{5,4},{6,7},{7,6},{8,9},{9,8},{10,11... | collective-permute-start | bytes 393224 | tf_op jit(solution)/shard_map/ppermute | solution.py:707
  130.1 16.0 %collective-permute-start.30 = (bf16[32,2048]{1,0:T(8,128)(2,1)}, bf16[32,2048]{1,0:T(8,128)(2,1)S(1)}, u32[]{:S(2)}, u32[]{:S(2)}) collective-permute-start(bf16[32,2048]{1,0:T(8,128)(2,1)} %get-tuple-element.112), channel_id=1, source_target_pairs={{0,2},{1,3},{2,0},{3,1},{4,6},{5,7},{6,4},{7,5},{8,10},{9,11},{10,... | collective-permute-start | bytes 393224 | tf_op jit(solution)/shard_map/ppermute | solution.py:707
  132.1 14.1 %collective-permute-start.31 = (bf16[32,2048]{1,0:T(8,128)(2,1)S(1)}, bf16[32,2048]{1,0:T(8,128)(2,1)S(1)}, u32[]{:S(2)}, u32[]{:S(2)}) collective-permute-start(bf16[32,2048]{1,0:T(8,128)(2,1)S(1)} %copy-done.24), channel_id=1, source_target_pairs={{0,3},{1,2},{2,1},{3,0},{4,7},{5,6},{6,5},{7,4},{8,11},{9,10},{10,... | collective-permute-start | bytes 393224 | tf_op jit(solution)/shard_map/ppermute | solution.py:707
  133.5 0.8 copy-start.12
  133.5 24.3 %collective-permute-start.22 = (bf16[1,128,2304]{2,1,0:T(8,128)(2,1)}, bf16[1,128,2304]{2,1,0:T(8,128)(2,1)S(1)}, u32[]{:S(2)}, u32[]{:S(2)}) collective-permute-start(bf16[1,128,2304]{2,1,0:T(8,128)(2,1)} %get-tuple-element.98), channel_id=1, source_target_pairs={{0,16},{4,20},{8,24},{12,28},{16,0},{20,4},{24,8},{28,12},{1,17},{... | collective-permute-start | bytes 1769480 | tf_op jit(solution)/shard_map/ppermute | solution.py:49
  134.3 10.5 %copy-start.5 = (bf16[1,128,2304]{2,1,0:T(8,128)(2,1)S(1)}, bf16[1,128,2304]{2,1,0:T(8,128)(2,1)}, u32[]{:S(2)}) copy-start(bf16[1,128,2304]{2,1,0:T(8,128)(2,1)} %get-tuple-element.99) | copy-start | bytes 1769476
  134.3 11.8 %copy-start.19 = (bf16[32,2048]{1,0:T(8,128)(2,1)S(1)}, bf16[32,2048]{1,0:T(8,128)(2,1)}, u32[]{:S(2)}) copy-start(bf16[32,2048]{1,0:T(8,128)(2,1)} %get-tuple-element.93) | copy-start | bytes 393220
  144.9 14.5 %collective-permute-start.23 = (bf16[1,128,2304]{2,1,0:T(8,128)(2,1)S(1)}, bf16[1,128,2304]{2,1,0:T(8,128)(2,1)S(1)}, u32[]{:S(2)}, u32[]{:S(2)}) collective-permute-start(bf16[1,128,2304]{2,1,0:T(8,128)(2,1)S(1)} %copy-done.5), channel_id=1, source_target_pairs={{0,8},{4,12},{8,0},{12,4},{16,24},{20,28},{24,16},{28,20},{1,9},{5... | collective-permute-start | bytes 1769480 | tf_op jit(solution)/shard_map/ppermute | solution.py:49
  146.1 4.9 %copy-start.1 = (bf16[128,2048]{1,0:T(8,128)(2,1)}, bf16[128,2048]{1,0:T(8,128)(2,1)S(1)}, u32[]{:S(2)}) copy-start(bf16[128,2048]{1,0:T(8,128)(2,1)S(1)} %collective-permute-done.24.refs_0_.refs_2_) | copy-start | bytes 1572868
  146.1 3.4 %collective-permute-start.25 = (bf16[128,2048]{1,0:T(8,128)(2,1)S(1)}, bf16[128,2048]{1,0:T(8,128)(2,1)S(1)}, u32[]{:S(2)}, u32[]{:S(2)}) collective-permute-start(bf16[128,2048]{1,0:T(8,128)(2,1)S(1)} %collective-permute-done.24.refs_0_.refs_2_), channel_id=1, source_target_pairs={{0,4},{4,0},{8,12},{12,8},{16,20},{20,16},{24,28},{28,24},{1,5},{5... | collective-permute-start | bytes 1572872 | tf_op jit(solution)/shard_map/ppermute | solution.py:49
  146.5 11.2 %copy-start.18 = (bf16[32,2048]{1,0:T(8,128)(2,1)}, bf16[32,2048]{1,0:T(8,128)(2,1)S(1)}, u32[]{:S(2)}) copy-start(bf16[32,2048]{1,0:T(8,128)(2,1)S(1)} %fusion.8.refs_0_) | copy-start | bytes 393220
  146.5 12.8 %collective-permute-start.32 = (bf16[32,2048]{1,0:T(8,128)(2,1)S(1)}, bf16[32,2048]{1,0:T(8,128)(2,1)S(1)}, u32[]{:S(2)}, u32[]{:S(2)}) collective-permute-start(bf16[32,2048]{1,0:T(8,128)(2,1)S(1)} %fusion.8.refs_0_), channel_id=1, source_target_pairs={{0,1},{1,0},{2,3},{3,2},{4,5},{5,4},{6,7},{7,6},{8,9},{9,8},{10,11... | collective-permute-start | bytes 393224 | tf_op jit(solution)/shard_map/ppermute | solution.py:714
  147.2 12.9 %collective-permute-start.33 = (bf16[32,2048]{1,0:T(8,128)(2,1)S(1)}, bf16[32,2048]{1,0:T(8,128)(2,1)S(1)}, u32[]{:S(2)}, u32[]{:S(2)}) collective-permute-start(bf16[32,2048]{1,0:T(8,128)(2,1)S(1)} %fusion.8.refs_0_), channel_id=1, source_target_pairs={{0,2},{1,3},{2,0},{3,1},{4,6},{5,7},{6,4},{7,5},{8,10},{9,11},{10,... | collective-permute-start | bytes 393224 | tf_op jit(solution)/shard_map/ppermute | solution.py:714
  149.6 1.5 copy-start.15
  149.6 10.5 %collective-permute-start.34 = (bf16[32,2048]{1,0:T(8,128)(2,1)S(1)}, bf16[32,2048]{1,0:T(8,128)(2,1)S(1)}, u32[]{:S(2)}, u32[]{:S(2)}) collective-permute-start(bf16[32,2048]{1,0:T(8,128)(2,1)S(1)} %fusion.8.refs_0_), channel_id=1, source_target_pairs={{0,3},{1,2},{2,1},{3,0},{4,7},{5,6},{6,5},{7,4},{8,11},{9,10},{10,... | collective-permute-start | bytes 393224 | tf_op jit(solution)/shard_map/ppermute | solution.py:714
  157.8 2.3 %copy-start.6 = (bf16[1,128,2304]{2,1,0:T(8,128)(2,1)}, bf16[1,128,2304]{2,1,0:T(8,128)(2,1)S(1)}, u32[]{:S(2)}) copy-start(bf16[1,128,2304]{2,1,0:T(8,128)(2,1)S(1)} %collective-permute-done.22) | copy-start | bytes 1769476
  159.4 0.8 copy-start.7
  159.4 0.9 copy-start.20
  160.1 0.6 copy-start.21
  160.1 0.7 copy-start.22
